TPU v7x, 32 devices: a whole 2x2x4 slice. The times are simulated.
32 devices in a mesh: batch: 16 (over z, y, core), rows: 2 (over x).
Axes of the slice: x: 2, y: 2, z: 4, core: 2. Of those that a mesh axis runs over, the one named last changes fastest.
Arguments:
- images: bfloat16 [16, 4, 80, 2048], P('batch', 'rows'), may hold values from -6 to 6
- crop_height: int32 [16], replicated, may hold values from 3 to 4, as said below
- crop_width: int32 [16], replicated, may hold values from 21 to 80, as said below
- w_first: bfloat16 [2048, 512], P('batch'), may hold values from -0.125 to 0.125
- gain_first: bfloat16 [512], P('batch'), may hold values from 0.5 to 1.5
- shift_first: bfloat16 [512], P('batch'), may hold values from -3 to 3
- w_middle: bfloat16 [9, 512, 512], P(None, 'batch'), may hold values from -0.09375 to 0.09375
- gain_middle: bfloat16 [512], P('batch'), may hold values from 0.5 to 1.5
- shift_middle: bfloat16 [512], P('batch'), may hold values from -3 to 3
- w_last: bfloat16 [512, 2048], P('batch'), may hold values from -0.25 to 0.25
- gain_last: bfloat16 [2048], P('batch'), may hold values from 0.5 to 1.5
- shift_last: bfloat16 [2048], P('batch'), may hold values from -3 to 3
- w_reduce: bfloat16 [2048, 512], P('batch'), may hold values from -0.125 to 0.125
- w_heads: bfloat16 [4, 9, 512, 512], P('rows', None, 'batch'), may hold values from -0.09375 to 0.09375
- w_message: bfloat16 [4, 9, 512, 512], P('rows', None, 'batch'), may hold values from -0.09375 to 0.09375
- w_gates: bfloat16 [2, 512, 512], P(None, 'batch'), may hold values from -0.25 to 0.25
- w_classes: bfloat16 [512, 40], P('batch'), may hold values from -0.25 to 0.25
- depth_cot: bfloat16 [16, 4, 80, 512], P('batch', 'rows'), may hold values from -6 to 6
- class_cot: bfloat16 [16, 4, 80, 40], P('batch', 'rows'), may hold values from -6 to 6
Outputs:
- depth_stream: bfloat16 [16, 4, 80, 512], P('batch', 'rows')
- class_logits: bfloat16 [16, 4, 80, 40], P('batch', 'rows')
- image_grad: float32 [16, 4, 80, 2048], P('batch', 'rows')
- grad_first: float32 [2048, 512], P('batch')
- grad_gain_first: float32 [512], P('batch')
- grad_shift_first: float32 [512], P('batch')
- grad_middle: float32 [9, 512, 512], P(None, 'batch')
- grad_gain_middle: float32 [512], P('batch')
- grad_shift_middle: float32 [512], P('batch')
- grad_last: float32 [512, 2048], P('batch')
- grad_gain_last: float32 [2048], P('batch')
- grad_shift_last: float32 [2048], P('batch')
- grad_reduce: float32 [2048, 512], P('batch')
- grad_heads: float32 [4, 9, 512, 512], P('rows', None, 'batch')
- grad_message: float32 [4, 9, 512, 512], P('rows', None, 'batch')
- grad_gates: float32 [2, 512, 512], P(None, 'batch')
- grad_classes: float32 [512, 40], P('batch')
Inputs may be any that keep to these rules, and one draw needn't show every extreme that they name: `crop_height`: every image's crop reaches into the last row block: crop heights exceed 4 - 2; some image has the full height. `crop_width`: crops of the coarse maps use at most half of the columns; some image has the full width.
All inputs are finite; a program needn't handle non-finite values.
Results may differ from a plain program's by a relative error of at most 0.02.
Values may be sent and summed in bfloat16 or wider, within the bound.
A program may use at most 384 MiB of HBM per device.

v0:
```python
import jax
import jax.numpy as jnp
from jax import lax
from jax.sharding import PartitionSpec as P

EPS = 1e-05


def padded_2(cells, sides, width):
    for axis, dim in sides:
        count = lax.axis_size(axis)
        ends = count - 1
        head = lax.slice_in_dim(cells, 0, width, axis=dim)
        tail = lax.slice_in_dim(cells, cells.shape[dim] - width, cells.shape[dim], axis=dim)
        cells = jnp.concatenate(
            [
                lax.ppermute(tail, axis, [(i, (i + 1) % count) for i in range(ends)]),
                cells,
                lax.ppermute(head, axis, [((i + 1) % count, i) for i in range(ends)]),
            ],
            axis=dim,
        )
    return cells


def gelu_tanh(values):
    return jax.nn.gelu(values, approximate=True)


def gelu_slope(values, upstream):
    return jax.vjp(gelu_tanh, values)[1](upstream)[0]


def project(values, weight):
    return jnp.einsum("nrcj,jk->nrck", values, weight, preferred_element_type=jnp.float32)


def project_back(upstream, weight):
    return jnp.einsum("nrck,jk->nrcj", upstream, weight, preferred_element_type=jnp.float32)


def outer_sum(values, upstream):
    return jnp.einsum("nrcj,nrck->jk", values, upstream, preferred_element_type=jnp.float32)


def widen(padded):
    return jnp.pad(padded, ((0, 0), (0, 0), (1, 1), (0, 0)))


def halo_value(values):
    return padded_2(values, (("rows", 1),), 1)


def halo_grad(values):
    return padded_2(values, (("rows", 1),), 1)


def conv_apply(padded, kernel):
    row_count = padded.shape[1] - 2
    col_count = padded.shape[2]
    widened = widen(padded)
    running = jnp.zeros((padded.shape[0], row_count, col_count, kernel.shape[2]), jnp.float32)
    for tap_index in range(9):
        shift_down = tap_index // 3
        shift_right = tap_index % 3
        running = running + project(
            widened[
                :, shift_down : shift_down + row_count, shift_right : shift_right + col_count, :
            ],
            kernel[tap_index],
        )
    return running


def conv_kernel_grad(padded, upstream):
    row_count = upstream.shape[1]
    col_count = upstream.shape[2]
    widened = widen(padded)
    return jnp.stack(
        [
            outer_sum(
                widened[
                    :,
                    tap_index // 3 : tap_index // 3 + row_count,
                    tap_index % 3 : tap_index % 3 + col_count,
                    :,
                ],
                upstream,
            )
            for tap_index in range(9)
        ]
    )


def conv_input_grad(padded_grad, kernel):
    row_count = padded_grad.shape[1] - 2
    col_count = padded_grad.shape[2]
    widened = widen(padded_grad)
    running = jnp.zeros((padded_grad.shape[0], row_count, col_count, kernel.shape[1]), jnp.float32)
    for tap_index in range(9):
        shift_down = tap_index // 3
        shift_right = tap_index % 3
        running = running + project_back(
            widened[
                :,
                2 - shift_down : 2 - shift_down + row_count,
                2 - shift_right : 2 - shift_right + col_count,
                :,
            ],
            kernel[tap_index],
        )
    return running


def crop_mask(height, width, first_row, row_count, col_count):
    row_ids = first_row + jnp.arange(row_count, dtype=jnp.int32)
    col_ids = jnp.arange(col_count, dtype=jnp.int32)
    inside = (row_ids[None, :, None] < height[:, None, None]) & (
        col_ids[None, None, :] < width[:, None, None]
    )
    return inside.astype(jnp.float32)[..., None]


def norm_forward(pre_act, pixel_mask, gain_vec, shift_vec, valid_count):
    sums = jnp.sum(pre_act * pixel_mask, axis=(0, 1, 2))
    squares = jnp.sum(pre_act * pre_act * pixel_mask, axis=(0, 1, 2))
    sums, squares = lax.psum((sums, squares), ("batch", "rows"))
    mean_vec = sums / valid_count
    inv_std = lax.rsqrt(squares / valid_count - mean_vec * mean_vec + EPS)
    normal = (pre_act - mean_vec) * inv_std
    return (normal, inv_std, normal * gain_vec + shift_vec)


def norm_backward(upstream, normal, inv_std, gain_vec, pixel_mask, valid_count):
    shift_part = jnp.sum(upstream, axis=(0, 1, 2))
    gain_part = jnp.sum(upstream * normal, axis=(0, 1, 2))
    shift_part, gain_part = lax.psum((shift_part, gain_part), ("batch", "rows"))
    d_pre = (
        pixel_mask
        * gain_vec
        * inv_std
        * (upstream - shift_part / valid_count - normal * gain_part / valid_count)
    )
    return (d_pre, gain_part, shift_part)


def task_forward(padded_in, heads, messages, pixel_mask, pad_rows):
    pre_list = []
    feat_list = []
    padded_feats = []
    message_list = []
    for task in range(heads.shape[0]):
        pre_act = conv_apply(padded_in, heads[task])
        feature = (gelu_tanh(pre_act) * pixel_mask).astype(jnp.bfloat16)
        padded_feat = pad_rows(feature)
        pre_list.append(pre_act)
        feat_list.append(feature)
        padded_feats.append(padded_feat)
        message_list.append(conv_apply(padded_feat, messages[task]).astype(jnp.bfloat16))
    return (pre_list, feat_list, padded_feats, message_list)


def task_backward(
    padded_in,
    heads,
    messages,
    pixel_mask,
    pre_list,
    padded_feats,
    feat_grads,
    message_grads,
    pad_grad,
):
    input_grad = jnp.zeros(
        padded_in.shape[:1] + (padded_in.shape[1] - 2,) + padded_in.shape[2:], jnp.float32
    )
    head_grads = []
    kernel_grads = []
    for task in range(heads.shape[0]):
        low_message = message_grads[task].astype(jnp.bfloat16)
        kernel_grads.append(conv_kernel_grad(padded_feats[task], low_message))
        feat_grad = feat_grads[task] + conv_input_grad(pad_grad(low_message), messages[task])
        low_pre = gelu_slope(pre_list[task], feat_grad * pixel_mask).astype(jnp.bfloat16)
        head_grads.append(conv_kernel_grad(padded_in, low_pre))
        input_grad = input_grad + conv_input_grad(pad_grad(low_pre), heads[task])
    return (input_grad, jnp.stack(head_grads), jnp.stack(kernel_grads))


def streams_forward(features, messages, gates_all, classes_all, pixel_mask):
    gate_depth = jax.nn.sigmoid(project(features[0], gates_all[0]))
    gate_class = jax.nn.sigmoid(project(features[3], gates_all[1]))
    depth_sum = (
        messages[1].astype(jnp.float32)
        + messages[2].astype(jnp.float32)
        + messages[3].astype(jnp.float32)
    )
    class_sum = (
        messages[0].astype(jnp.float32)
        + messages[1].astype(jnp.float32)
        + messages[2].astype(jnp.float32)
    )
    depth_stream = (features[0].astype(jnp.float32) + gate_depth * depth_sum) * pixel_mask
    merged = (features[3].astype(jnp.float32) + gate_class * class_sum).astype(jnp.bfloat16)
    class_logits = project(merged, classes_all) * pixel_mask
    return (depth_stream, class_logits, merged, gate_depth, gate_class, depth_sum, class_sum)


def streams_backward(
    features,
    merged,
    gate_depth,
    gate_class,
    depth_sum,
    class_sum,
    depth_cot,
    class_cot,
    gates_all,
    classes_all,
    pixel_mask,
):
    depth_grad = depth_cot.astype(jnp.float32) * pixel_mask
    logit_grad = (class_cot.astype(jnp.float32) * pixel_mask).astype(jnp.bfloat16)
    grad_classes = outer_sum(merged, logit_grad)
    merged_grad = project_back(logit_grad, classes_all)
    gate_depth_grad = (depth_grad * depth_sum * gate_depth * (1.0 - gate_depth)).astype(
        jnp.bfloat16
    )
    gate_class_grad = (merged_grad * class_sum * gate_class * (1.0 - gate_class)).astype(
        jnp.bfloat16
    )
    grad_gates = jnp.stack(
        [outer_sum(features[0], gate_depth_grad), outer_sum(features[3], gate_class_grad)]
    )
    depth_feat = depth_grad + project_back(gate_depth_grad, gates_all[0])
    class_feat = merged_grad + project_back(gate_class_grad, gates_all[1])
    depth_message = depth_grad * gate_depth
    class_message = merged_grad * gate_class
    nothing = jnp.zeros_like(depth_grad)
    feat_grads = [depth_feat, nothing, nothing, class_feat]
    message_grads = [
        class_message,
        depth_message + class_message,
        depth_message + class_message,
        depth_message,
    ]
    return (feat_grads, message_grads, grad_gates, grad_classes)


def shards(
    images,
    crop_height,
    crop_width,
    w_first,
    gain_first,
    shift_first,
    w_middle,
    gain_middle,
    shift_middle,
    w_last,
    gain_last,
    shift_last,
    w_reduce,
    w_heads,
    w_message,
    w_gates,
    w_classes,
    depth_cot,
    class_cot,
):
    image_index = lax.axis_index("batch")
    batch_count = lax.axis_size("batch")
    row_count = images.shape[1]
    col_count = images.shape[2]
    height = lax.dynamic_slice_in_dim(crop_height, image_index, 1, 0)
    width = lax.dynamic_slice_in_dim(crop_width, image_index, 1, 0)
    pixel_mask = crop_mask(height, width, lax.axis_index("rows") * row_count, row_count, col_count)
    valid_count = jnp.sum(crop_height * crop_width).astype(jnp.float32)
    gathered = (
        lax.all_gather(w_first, "batch", axis=0, tiled=True),
        lax.all_gather(w_middle, "batch", axis=1, tiled=True),
        lax.all_gather(w_last, "batch", axis=0, tiled=True),
        lax.all_gather(w_reduce, "batch", axis=0, tiled=True),
        lax.all_gather(w_gates, "batch", axis=1, tiled=True),
        lax.all_gather(w_classes, "batch", axis=0, tiled=True),
        lax.all_gather(gain_first, "batch", axis=0, tiled=True),
        lax.all_gather(shift_first, "batch", axis=0, tiled=True),
        lax.all_gather(gain_middle, "batch", axis=0, tiled=True),
        lax.all_gather(shift_middle, "batch", axis=0, tiled=True),
        lax.all_gather(gain_last, "batch", axis=0, tiled=True),
        lax.all_gather(shift_last, "batch", axis=0, tiled=True),
        lax.all_gather(w_heads, "batch", axis=2, tiled=True),
        lax.all_gather(w_message, "batch", axis=2, tiled=True),
    )
    first_all = gathered[0]
    middle_all = gathered[1]
    last_all = gathered[2]
    reduce_all = gathered[3]
    gates_all = gathered[4]
    classes_all = gathered[5]
    gain_one = gathered[6].astype(jnp.float32)
    shift_one = gathered[7].astype(jnp.float32)
    gain_two = gathered[8].astype(jnp.float32)
    shift_two = gathered[9].astype(jnp.float32)
    gain_three = gathered[10].astype(jnp.float32)
    shift_three = gathered[11].astype(jnp.float32)
    heads_own = gathered[12]
    message_own = gathered[13]
    masked_in = images.astype(jnp.float32) * pixel_mask
    low_in = masked_in.astype(jnp.bfloat16)
    pre_first = project(low_in, first_all)
    normal_first, std_first, out_first = norm_forward(
        pre_first, pixel_mask, gain_one, shift_one, valid_count
    )
    act_first = (gelu_tanh(out_first) * pixel_mask).astype(jnp.bfloat16)
    padded_first = halo_value(act_first)
    pre_middle = conv_apply(padded_first, middle_all)
    normal_middle, std_middle, out_middle = norm_forward(
        pre_middle, pixel_mask, gain_two, shift_two, valid_count
    )
    act_middle = (gelu_tanh(out_middle) * pixel_mask).astype(jnp.bfloat16)
    pre_last = project(act_middle, last_all)
    normal_last, std_last, out_last = norm_forward(
        pre_last, pixel_mask, gain_three, shift_three, valid_count
    )
    summed = out_last + masked_in
    block_out = (gelu_tanh(summed) * pixel_mask).astype(jnp.bfloat16)
    low_reduced = project(block_out, reduce_all).astype(jnp.bfloat16)
    heads_all, message_all = (
        lax.all_gather(heads_own, "rows", axis=0, tiled=True),
        lax.all_gather(message_own, "rows", axis=0, tiled=True),
    )
    padded_in = halo_value(low_reduced)
    pre_list, feat_list, padded_feats, message_list = task_forward(
        padded_in, heads_all, message_all, pixel_mask, halo_value
    )
    depth_stream, class_logits, merged, gate_depth, gate_class, depth_sum, class_sum = (
        streams_forward(feat_list, message_list, gates_all, classes_all, pixel_mask)
    )
    feat_grads, message_grads, grad_gates, grad_classes = streams_backward(
        feat_list,
        merged,
        gate_depth,
        gate_class,
        depth_sum,
        class_sum,
        depth_cot,
        class_cot,
        gates_all,
        classes_all,
        pixel_mask,
    )
    reduced_grad, grad_heads, grad_message = task_backward(
        padded_in,
        heads_all,
        message_all,
        pixel_mask,
        pre_list,
        padded_feats,
        feat_grads,
        message_grads,
        halo_grad,
    )
    low_reduced_grad = reduced_grad.astype(jnp.bfloat16)
    grad_reduce = outer_sum(block_out, low_reduced_grad)
    block_grad = project_back(low_reduced_grad, reduce_all)
    sum_grad = gelu_slope(summed, block_grad * pixel_mask)
    d_last, gain_grad_three, shift_grad_three = norm_backward(
        sum_grad, normal_last, std_last, gain_three, pixel_mask, valid_count
    )
    low_last = d_last.astype(jnp.bfloat16)
    grad_last = outer_sum(act_middle, low_last)
    middle_grad = project_back(low_last, last_all)
    d_middle, gain_grad_two, shift_grad_two = norm_backward(
        gelu_slope(out_middle, middle_grad * pixel_mask),
        normal_middle,
        std_middle,
        gain_two,
        pixel_mask,
        valid_count,
    )
    low_middle = d_middle.astype(jnp.bfloat16)
    grad_middle = conv_kernel_grad(padded_first, low_middle)
    first_grad = conv_input_grad(halo_grad(low_middle), middle_all)
    d_first, gain_grad_one, shift_grad_one = norm_backward(
        gelu_slope(out_first, first_grad * pixel_mask),
        normal_first,
        std_first,
        gain_one,
        pixel_mask,
        valid_count,
    )
    low_first = d_first.astype(jnp.bfloat16)
    grad_first = outer_sum(low_in, low_first)
    image_grad = (project_back(low_first, first_all) + sum_grad) * pixel_mask
    summed_grads = (
        lax.psum_scatter(grad_first, "batch", scatter_dimension=0, tiled=True),
        lax.psum_scatter(grad_middle, "batch", scatter_dimension=1, tiled=True),
        lax.psum_scatter(grad_last, "batch", scatter_dimension=0, tiled=True),
        lax.psum_scatter(grad_reduce, "batch", scatter_dimension=0, tiled=True),
        lax.psum_scatter(grad_gates, "batch", scatter_dimension=1, tiled=True),
        lax.psum_scatter(grad_classes, "batch", scatter_dimension=0, tiled=True),
        lax.psum_scatter(grad_heads, "batch", scatter_dimension=2, tiled=True),
        lax.psum_scatter(grad_message, "batch", scatter_dimension=2, tiled=True),
    )
    shared = (
        lax.psum(summed_grads[0].astype(jnp.bfloat16), "rows").astype(jnp.float32),
        lax.psum(summed_grads[1].astype(jnp.bfloat16), "rows").astype(jnp.float32),
        lax.psum(summed_grads[2].astype(jnp.bfloat16), "rows").astype(jnp.float32),
        lax.psum(summed_grads[3].astype(jnp.bfloat16), "rows").astype(jnp.float32),
        lax.psum(summed_grads[4].astype(jnp.bfloat16), "rows").astype(jnp.float32),
        lax.psum(summed_grads[5].astype(jnp.bfloat16), "rows").astype(jnp.float32),
    )
    heads_out, message_out = (
        lax.psum_scatter(
            summed_grads[6].astype(jnp.bfloat16), "rows", scatter_dimension=0, tiled=True
        ).astype(jnp.float32),
        lax.psum_scatter(
            summed_grads[7].astype(jnp.bfloat16), "rows", scatter_dimension=0, tiled=True
        ).astype(jnp.float32),
    )

    def own_share(member):
        share = member.shape[0] // batch_count
        return lax.dynamic_slice_in_dim(member, image_index * share, share, 0)

    return (
        depth_stream.astype(jnp.bfloat16),
        class_logits.astype(jnp.bfloat16),
        image_grad,
        shared[0],
        own_share(gain_grad_one),
        own_share(shift_grad_one),
        shared[1],
        own_share(gain_grad_two),
        own_share(shift_grad_two),
        shared[2],
        own_share(gain_grad_three),
        own_share(shift_grad_three),
        shared[3],
        heads_out,
        message_out,
        shared[4],
        shared[5],
    )


def solution(mesh):
    placed = (
        P("batch", "rows", None, None),
        P(),
        P(),
        P("batch", None),
        P("batch"),
        P("batch"),
        P(None, "batch", None),
        P("batch"),
        P("batch"),
        P("batch", None),
        P("batch"),
        P("batch"),
        P("batch", None),
        P("rows", None, "batch", None),
        P("rows", None, "batch", None),
        P(None, "batch", None),
        P("batch", None),
        P("batch", "rows", None, None),
        P("batch", "rows", None, None),
    )
    return jax.shard_map(
        shards,
        mesh=mesh,
        in_specs=placed,
        out_specs=(
            P("batch", "rows", None, None),
            P("batch", "rows", None, None),
            P("batch", "rows", None, None),
            P("batch", None),
            P("batch"),
            P("batch"),
            P(None, "batch", None),
            P("batch"),
            P("batch"),
            P("batch", None),
            P("batch"),
            P("batch"),
            P("batch", None),
            P("rows", None, "batch", None),
            P("rows", None, "batch", None),
            P(None, "batch", None),
            P("batch", None),
        ),
        check_vma=False,
    )
```

profile of v0, /device:TPU:0, one launch (start us, length us, event | category | flops | bytes accessed | tf_op | source)
XLA Modules:
  0.0 2292.1 jit_solution(14122859209099037725)
XLA Ops:
  11.2 83.2 %all-gather.20.cloned.1.call-done = bf16[2,9,512,512]{3,2,1,0:T(8,128)(2,1)} async-done(((bf16[2,9,32,512]{3,2,1,0:T(8,128)(2,1)}), bf16[2,9,512,512]{3,2,1,0:T(8,128)(2,1)}) %all-gather.20.cloned.1.call-update) | async-done | bytes 9437200 | tf_op jit(solution)/shard_map/all_gather | solution.py:291
  95.3 80.9 %all-gather.26.cloned.1.call-done = bf16[2,9,512,512]{3,2,1,0:T(8,128)(2,1)} async-done(((bf16[2,9,32,512]{3,2,1,0:T(8,128)(2,1)}), bf16[2,9,512,512]{3,2,1,0:T(8,128)(2,1)}) %all-gather.26.cloned.1.call-update) | async-done | bytes 9437200 | tf_op jit(solution)/shard_map/all_gather | solution.py:292
  181.0 31.1 %all-reduce.24 = (bf16[512]{0:T(512)(128)(2,1)S(1)}, bf16[512]{0:T(512)(128)(2,1)S(1)}, bf16[512]{0:T(512)(128)(2,1)S(1)}, bf16[512]{0:T(512)(128)(2,1)S(1)}) all-reduce(bf16[512]{0:T(512)(128)(2,1)S(1)} %dynamic-update-slice.1, bf16[512]{0:T(512)(128)(2,1)S(1)} %dynamic-update-slice, ...), channel_id=1, replica_groups=mesh['batch'=16,'rows'=2] {'batch'}, use_global_device_ids=true, to_apply=%add.15 | all-reduce | flops 2048 | bytes 8192
  220.2 39.7 %all-reduce.23 = (f32[512]{0:T(512)S(1)}, f32[512]{0:T(512)S(1)}) all-reduce(f32[512]{0:T(512)S(1)} %get-tuple-element.24, f32[512]{0:T(512)S(1)} %get-tuple-element.23), channel_id=1, replica_groups=mesh['batch'=16,'rows'=2] {'batch','rows'}, use_global_device_ids=true, to_apply=%region_4.0 | all-reduce | flops 1024 | bytes 8192 | tf_op jit(solution)/shard_map/psum | solution.py:127
  265.7 18.9 all-gather
  284.7 17.3 all-gather.1
  302.0 19.2 all_gather.63
  333.2 38.6 %all-reduce.22 = (f32[512]{0:T(512)S(1)}, f32[512]{0:T(512)S(1)}) all-reduce(f32[512]{0:T(512)S(1)} %get-tuple-element.22, f32[512]{0:T(512)S(1)} %get-tuple-element.21), channel_id=1, replica_groups=mesh['batch'=16,'rows'=2] {'batch','rows'}, use_global_device_ids=true, to_apply=%region_8.9 | all-reduce | flops 1024 | bytes 8192 | tf_op jit(solution)/shard_map/psum | solution.py:127
  374.8 42.6 %all-reduce.21 = (f32[2048]{0:T(1024)S(1)}, f32[2048]{0:T(1024)S(1)}) all-reduce(f32[2048]{0:T(1024)S(1)} %get-tuple-element.18, f32[2048]{0:T(1024)S(1)} %get-tuple-element.17), channel_id=1, replica_groups=mesh['batch'=16,'rows'=2] {'batch','rows'}, use_global_device_ids=true, to_apply=%region_12.13 | all-reduce | flops 4096 | bytes 32768 | tf_op jit(solution)/shard_map/psum | solution.py:127
  434.2 151.5 %all-gather.22.cloned.1.call-done = bf16[4,9,512,512]{3,2,1,0:T(8,128)(2,1)} async-done(((bf16[2,9,512,512]{3,2,1,0:T(8,128)(2,1)}), bf16[4,9,512,512]{3,2,1,0:T(8,128)(2,1)}) %all-gather.22.cloned.1.call-update) | async-done | bytes 18874384 | tf_op jit(solution)/shard_map/all_gather | solution.py:329
  618.4 5.2 collective-permute-start.4
  632.4 5.1 collective-permute-start.10
  637.6 213.2 %all-gather.28.cloned.1.call-done = bf16[4,9,512,512]{3,2,1,0:T(8,128)(2,1)} async-done(((bf16[2,9,512,512]{3,2,1,0:T(8,128)(2,1)}), bf16[4,9,512,512]{3,2,1,0:T(8,128)(2,1)}) %all-gather.28.cloned.1.call-update) | async-done | bytes 18874384 | tf_op jit(solution)/shard_map/all_gather | solution.py:330
  887.6 5.8 collective-permute-start.16
  898.6 6.1 collective-permute-start.12
  924.9 4.6 collective-permute-start.20
  963.7 4.6 collective-permute-start.14
  983.3 4.6 collective-permute-start.24
  1005.1 42.0 %all-reduce.20 = (f32[2048]{0:T(1024)S(1)}, f32[2048]{0:T(1024)}) all-reduce(f32[2048]{0:T(1024)} %get-tuple-element.20, f32[2048]{0:T(1024)} %get-tuple-element.19), channel_id=1, replica_groups=mesh['batch'=16,'rows'=2] {'batch','rows'}, use_global_device_ids=true, to_apply=%region_16.17 | all-reduce | flops 4096 | bytes 32768 | tf_op jit(solution)/shard_map/psum | solution.py:137
  1062.3 41.1 %all-reduce.19 = (f32[512]{0:T(512)S(1)}, f32[512]{0:T(512)S(1)}) all-reduce(f32[512]{0:T(512)S(1)} %get-tuple-element.28, f32[512]{0:T(512)S(1)} %get-tuple-element.27), channel_id=1, replica_groups=mesh['batch'=16,'rows'=2] {'batch','rows'}, use_global_device_ids=true, to_apply=%region_20.21 | all-reduce | flops 1024 | bytes 8192 | tf_op jit(solution)/shard_map/psum | solution.py:137
  1128.5 39.0 %all-reduce.18 = (f32[512]{0:T(512)S(1)}, f32[512]{0:T(512)S(1)}) all-reduce(f32[512]{0:T(512)S(1)} %get-tuple-element.26, f32[512]{0:T(512)S(1)} %get-tuple-element.25), channel_id=1, replica_groups=mesh['batch'=16,'rows'=2] {'batch','rows'}, use_global_device_ids=true, to_apply=%region_24.25 | all-reduce | flops 1024 | bytes 8192 | tf_op jit(solution)/shard_map/psum | solution.py:137
  1207.5 17.1 pad_maximum_fusion.1
  1237.4 12.6 pad_maximum_fusion
  1256.8 23.1 %reduce-scatter.11.cloned.1.call-done = f32[128,512]{1,0:T(8,128)} async-done(((f32[2048,512]{1,0:T(8,128)}), f32[128,512]{1,0:T(8,128)}) %reduce-scatter.11.cloned.1.call-update) | async-done | bytes 262160 | tf_op jit(solution)/shard_map/reduce_scatter | solution.py:396
  1281.6 112.5 %reduce-scatter.13.cloned.1.call-done = f32[9,32,512]{2,1,0:T(8,128)} async-done(((f32[9,512,512]{2,1,0:T(8,128)}), f32[9,32,512]{2,1,0:T(8,128)}) %reduce-scatter.13.cloned.1.call-update) | async-done | bytes 589840 | tf_op jit(solution)/shard_map/reduce_scatter | solution.py:397
  1396.0 370.3 %reduce-scatter.23.cloned.1.call-done = f32[4,9,32,512]{3,2,1,0:T(8,128)} async-done(((f32[4,9,512,512]{3,2,1,0:T(8,128)}), f32[4,9,32,512]{3,2,1,0:T(8,128)}) %reduce-scatter.23.cloned.1.call-update) | async-done | bytes 2359312 | tf_op jit(solution)/shard_map/reduce_scatter | solution.py:403
  1769.3 368.7 %reduce-scatter.19.cloned.1.call-done = f32[4,9,32,512]{3,2,1,0:T(8,128)} async-done(((f32[4,9,512,512]{3,2,1,0:T(8,128)}), f32[4,9,32,512]{3,2,1,0:T(8,128)}) %reduce-scatter.19.cloned.1.call-update) | async-done | bytes 2359312 | tf_op jit(solution)/shard_map/reduce_scatter | solution.py:402
  2141.8 55.1 %reduce-scatter.29.cloned.1.call-done = f32[32,40]{1,0:T(8,128)} async-done(((f32[512,40]{1,0:T(8,128)}), f32[32,40]{1,0:T(8,128)}) %reduce-scatter.29.cloned.1.call-update) | async-done | bytes 5136 | tf_op jit(solution)/shard_map/reduce_scatter | solution.py:401
  2197.6 5.0 psum.143
  2210.9 22.6 all-reduce.28.cloned.1.call-done
  2241.7 16.5 reduce-scatter.25.cloned.1.call-done
  2260.4 22.2 reduce-scatter.21.cloned.1.call-done
  (592 shorter events, 353.2 us)
Async XLA Ops:
  7.2 87.2 %all-gather.20.cloned.1.call-start = ((), (), s32[]{:S(2)}) async-start(), calls=%async_computation.14 | async-start | bytes 10027008 | tf_op jit(solution)/shard_map/all_gather | solution.py:291
  7.9 168.3 %all-gather.26.cloned.1.call-start = ((), (), s32[]{:S(2)}) async-start(), calls=%async_computation.17 | async-start | bytes 10027008 | tf_op jit(solution)/shard_map/all_gather | solution.py:292
  8.7 209.4 %all-gather.12.cloned.1.call-start = ((), (), s32[]{:S(2)}) async-start(), calls=%async_computation.10 | async-start | bytes 2228224 | tf_op jit(solution)/shard_map/all_gather | solution.py:279
  9.4 311.9 %all-gather.14.cloned.1.call-start = ((), (), s32[]{:S(2)}) async-start(), calls=%async_computation.11 | async-start | bytes 5013504 | tf_op jit(solution)/shard_map/all_gather | solution.py:280
  10.0 361.9 %all-gather.16.cloned.1.call-start = ((), (), s32[]{:S(2)}) async-start(), calls=%async_computation.12 | async-start | bytes 2228224 | tf_op jit(solution)/shard_map/all_gather | solution.py:281
  10.6 408.8 %all-gather.18.cloned.1.call-start = ((), (), s32[]{:S(2)}) async-start(), calls=%async_computation.13 | async-start | bytes 2228224 | tf_op jit(solution)/shard_map/all_gather | solution.py:282
  11.2 574.5 %all-gather.22.cloned.1.call-start = ((), (), s32[]{:S(2)}) async-start(), calls=%async_computation.15 | async-start | bytes 28311552 | tf_op jit(solution)/shard_map/all_gather | solution.py:329
  94.5 531.7 %all-gather.24.cloned.1.call-start = ((), (), s32[]{:S(2)}) async-start(), calls=%async_computation.16 | async-start | bytes 1114112 | tf_op jit(solution)/shard_map/all_gather | solution.py:283
  95.3 755.6 %all-gather.28.cloned.1.call-start = ((), (), s32[]{:S(2)}) async-start(), calls=%async_computation.18 | async-start | bytes 28311552 | tf_op jit(solution)/shard_map/all_gather | solution.py:330
  176.3 1075.7 %reduce-scatter.27.cloned.1.call-start = ((), (), s32[]{:S(2)}) async-start(), calls=%async_computation.27 | async-start | bytes 2228224 | tf_op jit(solution)/shard_map/reduce_scatter | solution.py:400
  260.2 61.0 %collective-permute-start = (bf16[1,1,80,512]{3,2,1,0:T(8,128)(2,1)S(1)}, bf16[1,1,80,512]{3,2,1,0:T(8,128)(2,1)S(1)}, u32[]{:S(2)}, u32[]{:S(2)}) collective-permute-start(bf16[1,1,80,512]{3,2,1,0:T(8,128)(2,1)S(1)} %get-tuple-element.84), channel_id=1, source_target_pairs={{0,1},{2,3},{4,5},{6,7},{8,9},{10,11},{12,13},{14,15},{16,17},{18,... | collective-permute-start | bytes 245768 | tf_op jit(solution)/shard_map/ppermute | solution.py:17
  264.4 56.8 %collective-permute-start.1 = (bf16[1,1,80,512]{3,2,1,0:T(8,128)(2,1)S(1)}, bf16[1,1,80,512]{3,2,1,0:T(8,128)(2,1)S(1)}, u32[]{:S(2)}, u32[]{:S(2)}) collective-permute-start(bf16[1,1,80,512]{3,2,1,0:T(8,128)(2,1)S(1)} %get-tuple-element.85), channel_id=1, source_target_pairs={{1,0},{3,2},{5,4},{7,6},{9,8},{11,10},{13,12},{15,14},{17,16},{19,... | collective-permute-start | bytes 245768 | tf_op jit(solution)/shard_map/ppermute | solution.py:19
  614.8 245.1 %collective-permute-start.6 = (bf16[1,1,80,512]{3,2,1,0:T(8,128)(2,1)}, bf16[1,1,80,512]{3,2,1,0:T(8,128)(2,1)S(1)}, u32[]{:S(2)}, u32[]{:S(2)}) collective-permute-start(bf16[1,1,80,512]{3,2,1,0:T(8,128)(2,1)} %get-tuple-element.74), channel_id=1, source_target_pairs={{0,1},{2,3},{4,5},{6,7},{8,9},{10,11},{12,13},{14,15},{16,17},{18,... | collective-permute-start | bytes 245768 | tf_op jit(solution)/shard_map/ppermute | solution.py:17
  617.0 242.9 %collective-permute-start.7 = (bf16[1,1,80,512]{3,2,1,0:T(8,128)(2,1)}, bf16[1,1,80,512]{3,2,1,0:T(8,128)(2,1)}, u32[]{:S(2)}, u32[]{:S(2)}) collective-permute-start(bf16[1,1,80,512]{3,2,1,0:T(8,128)(2,1)} %get-tuple-element.75), channel_id=1, source_target_pairs={{1,0},{3,2},{5,4},{7,6},{9,8},{11,10},{13,12},{15,14},{17,16},{19,... | collective-permute-start | bytes 245768 | tf_op jit(solution)/shard_map/ppermute | solution.py:19
  618.4 235.2 %collective-permute-start.4 = (bf16[1,1,80,512]{3,2,1,0:T(8,128)(2,1)S(1)}, bf16[1,1,80,512]{3,2,1,0:T(8,128)(2,1)S(1)}, u32[]{:S(2)}, u32[]{:S(2)}) collective-permute-start(bf16[1,1,80,512]{3,2,1,0:T(8,128)(2,1)S(1)} %get-tuple-element.76), channel_id=1, source_target_pairs={{0,1},{2,3},{4,5},{6,7},{8,9},{10,11},{12,13},{14,15},{16,17},{18,... | collective-permute-start | bytes 245768 | tf_op jit(solution)/shard_map/ppermute | solution.py:17
  631.0 224.1 %collective-permute-start.5 = (bf16[1,1,80,512]{3,2,1,0:T(8,128)(2,1)S(1)}, bf16[1,1,80,512]{3,2,1,0:T(8,128)(2,1)}, u32[]{:S(2)}, u32[]{:S(2)}) collective-permute-start(bf16[1,1,80,512]{3,2,1,0:T(8,128)(2,1)S(1)} %get-tuple-element.77), channel_id=1, source_target_pairs={{1,0},{3,2},{5,4},{7,6},{9,8},{11,10},{13,12},{15,14},{17,16},{19,... | collective-permute-start | bytes 245768 | tf_op jit(solution)/shard_map/ppermute | solution.py:19
  632.4 261.0 %collective-permute-start.10 = (bf16[1,1,80,512]{3,2,1,0:T(8,128)(2,1)}, bf16[1,1,80,512]{3,2,1,0:T(8,128)(2,1)S(1)}, u32[]{:S(2)}, u32[]{:S(2)}) collective-permute-start(bf16[1,1,80,512]{3,2,1,0:T(8,128)(2,1)} %get-tuple-element.72), channel_id=1, source_target_pairs={{0,1},{2,3},{4,5},{6,7},{8,9},{10,11},{12,13},{14,15},{16,17},{18,... | collective-permute-start | bytes 245768 | tf_op jit(solution)/shard_map/ppermute | solution.py:17
  881.4 80.7 %collective-permute-start.22 = (bf16[1,1,80,512]{3,2,1,0:T(8,128)(2,1)}, bf16[1,1,80,512]{3,2,1,0:T(8,128)(2,1)}, u32[]{:S(2)}, u32[]{:S(2)}) collective-permute-start(bf16[1,1,80,512]{3,2,1,0:T(8,128)(2,1)} %get-tuple-element.70), channel_id=1, source_target_pairs={{0,1},{2,3},{4,5},{6,7},{8,9},{10,11},{12,13},{14,15},{16,17},{18,... | collective-permute-start | bytes 245768 | tf_op jit(solution)/shard_map/ppermute | solution.py:17
  885.6 78.0 %collective-permute-start.23 = (bf16[1,1,80,512]{3,2,1,0:T(8,128)(2,1)}, bf16[1,1,80,512]{3,2,1,0:T(8,128)(2,1)}, u32[]{:S(2)}, u32[]{:S(2)}) collective-permute-start(bf16[1,1,80,512]{3,2,1,0:T(8,128)(2,1)} %get-tuple-element.71), channel_id=1, source_target_pairs={{1,0},{3,2},{5,4},{7,6},{9,8},{11,10},{13,12},{15,14},{17,16},{19,... | collective-permute-start | bytes 245768 | tf_op jit(solution)/shard_map/ppermute | solution.py:19
  898.6 43.8 %collective-permute-start.12 = (bf16[1,1,80,512]{3,2,1,0:T(8,128)(2,1)}, bf16[1,1,80,512]{3,2,1,0:T(8,128)(2,1)}, u32[]{:S(2)}, u32[]{:S(2)}) collective-permute-start(bf16[1,1,80,512]{3,2,1,0:T(8,128)(2,1)} %get-tuple-element.60), channel_id=1, source_target_pairs={{0,1},{2,3},{4,5},{6,7},{8,9},{10,11},{12,13},{14,15},{16,17},{18,... | collective-permute-start | bytes 245768 | tf_op jit(solution)/shard_map/ppermute | solution.py:17
  907.0 346.6 %reduce-scatter.15.cloned.1.call-start = ((), (), s32[]{:S(2)}) async-start(), calls=%async_computation.21 | async-start | bytes 4456448 | tf_op jit(solution)/shard_map/reduce_scatter | solution.py:398
  924.9 65.7 %collective-permute-start.20 = (bf16[1,1,80,512]{3,2,1,0:T(8,128)(2,1)S(1)}, bf16[1,1,80,512]{3,2,1,0:T(8,128)(2,1)S(1)}, u32[]{:S(2)}, u32[]{:S(2)}) collective-permute-start(bf16[1,1,80,512]{3,2,1,0:T(8,128)(2,1)S(1)} %get-tuple-element.64), channel_id=1, source_target_pairs={{0,1},{2,3},{4,5},{6,7},{8,9},{10,11},{12,13},{14,15},{16,17},{18,... | collective-permute-start | bytes 245768 | tf_op jit(solution)/shard_map/ppermute | solution.py:17
  942.4 49.7 %collective-permute-start.21 = (bf16[1,1,80,512]{3,2,1,0:T(8,128)(2,1)S(1)}, bf16[1,1,80,512]{3,2,1,0:T(8,128)(2,1)S(1)}, u32[]{:S(2)}, u32[]{:S(2)}) collective-permute-start(bf16[1,1,80,512]{3,2,1,0:T(8,128)(2,1)S(1)} %get-tuple-element.65), channel_id=1, source_target_pairs={{1,0},{3,2},{5,4},{7,6},{9,8},{11,10},{13,12},{15,14},{17,16},{19,... | collective-permute-start | bytes 245768 | tf_op jit(solution)/shard_map/ppermute | solution.py:19
  1054.7 200.5 %reduce-scatter.17.cloned.1.call-start = ((), (), s32[]{:S(2)}) async-start(), calls=%async_computation.22 | async-start | bytes 4456448 | tf_op jit(solution)/shard_map/reduce_scatter | solution.py:399
  1058.7 221.3 %reduce-scatter.11.cloned.1.call-start = ((), (), s32[]{:S(2)}) async-start(), calls=%async_computation.19 | async-start | bytes 4456448 | tf_op jit(solution)/shard_map/reduce_scatter | solution.py:396
  1174.4 219.8 %reduce-scatter.13.cloned.1.call-start = ((), (), s32[]{:S(2)}) async-start(), calls=%async_computation.20 | async-start | bytes 10027008 | tf_op jit(solution)/shard_map/reduce_scatter | solution.py:397
  1188.6 577.8 %reduce-scatter.23.cloned.1.call-start = ((), (), s32[]{:S(2)}) async-start(), calls=%async_computation.25 | async-start | bytes 40108032 | tf_op jit(solution)/shard_map/reduce_scatter | solution.py:403
  1224.7 913.4 %reduce-scatter.19.cloned.1.call-start = ((), (), s32[]{:S(2)}) async-start(), calls=%async_computation.23 | async-start | bytes 40108032 | tf_op jit(solution)/shard_map/reduce_scatter | solution.py:402
  1250.1 946.8 %reduce-scatter.29.cloned.1.call-start = ((), (), s32[]{:S(2)}) async-start(), calls=%async_computation.28 | async-start | bytes 278528 | tf_op jit(solution)/shard_map/reduce_scatter | solution.py:401
  1251.9 981.6 %all-reduce.28.cloned.1.call-start = ((), (), s32[]{:S(2)}) async-start(), calls=%async_computation.29 | async-start | bytes 1507328 | tf_op jit(solution)/shard_map/psum | solution.py:406
  1396.0 862.2 %reduce-scatter.25.cloned.1.call-start = ((), (), s32[]{:S(2)}) async-start(), calls=%async_computation.26 | async-start | bytes 1769472 | tf_op jit(solution)/shard_map/reduce_scatter | solution.py:417
  1769.3 513.4 %reduce-scatter.21.cloned.1.call-start = ((), (), s32[]{:S(2)}) async-start(), calls=%async_computation.24 | async-start | bytes 1769472 | tf_op jit(solution)/shard_map/reduce_scatter | solution.py:414
  (90 other events, 6786.2 us)
Sparse Core Ops, SparseCore 0:
  10.2 84.1 all-gather.19
  96.6 79.5 all-gather.25
  178.4 39.5 all-gather.11
  220.1 53.0 all-gather.13
  275.2 40.1 all-gather.15
  317.4 40.3 all-gather.17
  359.3 226.3 all-gather.21
  587.9 37.9 all-gather.23
  627.5 223.3 all-gather.27
  907.1 61.9 reduce-scatter.26
  1054.8 73.2 reduce-scatter.14
  1131.8 72.0 reduce-scatter.16
  1208.2 71.7 reduce-scatter.10
  1283.9 110.1 reduce-scatter.12
  1398.8 367.5 reduce-scatter.22
  1771.0 366.9 reduce-scatter.18
  2142.4 54.4 reduce-scatter.28
  2200.1 33.3 all-reduce.27
  2236.4 21.7 reduce-scatter.24
  2260.8 21.7 reduce-scatter.20
where the time goes:
time: 2300 us; the launch traced here: 2290 us
  waiting for transfers between devices  1540 us (67%)
  blocking collectives  335 us (15%)
  matrix products  224 us (10%)
  starting transfers between devices  81 us (4%)
  other arithmetic  76.4 us (3%)
    reduce_scatter x1, waiting for transfers between devices, shards(): lax.psum_scatter(grad_message, 'batch', scatter_dimension=2, tiled=True)  370 us
    reduce_scatter x1, waiting for transfers between devices, shards(): lax.psum_scatter(grad_heads, 'batch', scatter_dimension=2, tiled=True)  369 us
    all_gather x1, waiting for transfers between devices, shards(): lax.all_gather(message_own, 'rows', axis=0, tiled=True)  213 us
    all_gather x1, waiting for transfers between devices, shards(): lax.all_gather(heads_own, 'rows', axis=0, tiled=True)  152 us
    psum x3, blocking collectives, norm_backward(): shift_part, gain_part = lax.psum((shift_part, gain_part), ('batch', 'rows'))  122 us
    psum x3, blocking collectives, norm_forward(): sums, squares = lax.psum((sums, squares), ('batch', 'rows'))  121 us
    reduce_scatter x1, waiting for transfers between devices, shards(): lax.psum_scatter(grad_middle, 'batch', scatter_dimension=1, tiled=True)  113 us
    dot_general x87, matrix products, project_back(): jnp.einsum('nrck,jk->nrcj', upstream, weight, preferred_element_type=jnp....  89.3 us
  transfers between devices with their start and end apart: 48, of which 17 were waited for; matrix products, arithmetic and copies ran while one was open for 13% of the time, Pallas kernels for 0%

commit v1 on v0

--- a/solution.py
+++ b/solution.py
@@ -1,9 +1,124 @@
+import functools
+from types import SimpleNamespace
+
+import numpy as np
 import jax
 import jax.numpy as jnp
 from jax import lax
 from jax.sharding import PartitionSpec as P
+from jax.experimental import pallas as pl
+from jax.experimental.pallas import tpu as pltpu
 
 EPS = 1e-05
+MESH = pl.DeviceIdType.MESH
+F32 = jnp.float32
+BF16 = jnp.bfloat16
+ROOT = 0.7978845608028654
+CUBE = 0.044715
+SEMS = 320
+
+
+def dot(left, right):
+    return jnp.dot(left, right, preferred_element_type=F32)
+
+
+def dot_last(left, right):
+    return lax.dot_general(left, right, (((1,), (1,)), ((), ())), preferred_element_type=F32)
+
+
+def dot_first(left, right):
+    return lax.dot_general(left, right, (((0,), (0,)), ((), ())), preferred_element_type=F32)
+
+
+def gelu_of(v):
+    return 0.5 * v * (1.0 + jnp.tanh(ROOT * (v + CUBE * v * v * v)))
+
+
+def slope_of(v):
+    t = jnp.tanh(ROOT * (v + CUBE * v * v * v))
+    return 0.5 * (1.0 + t) + 0.5 * v * (1.0 - t * t) * (ROOT * (1.0 + 3.0 * CUBE * v * v))
+
+
+def rows_loop(total, chunk, step):
+    def body(index, carry):
+        step(pl.multiple_of(index * chunk, chunk))
+        return carry
+
+    lax.fori_loop(0, total // chunk, body, 0)
+
+
+class Copy:
+    def __init__(self, remote, links, index, like):
+        self.remote, self.links, self.index, self.like = remote, links, index, like
+
+    def wait_recv(self):
+        if self.like is None:
+            self.remote.wait_recv()
+        else:
+            ref = self.like(1)
+            pltpu.make_async_copy(ref, ref, self.links.recv.at[self.index]).wait()
+
+    def wait_send(self):
+        if self.like is None:
+            self.remote.wait_send()
+        else:
+            ref = self.like(0)
+            pltpu.make_async_copy(ref, ref, self.links.send.at[self.index]).wait()
+
+
+class Links:
+    def __init__(self, send, recv, local):
+        self.send, self.recv, self.local = send, recv, local
+        self.used, self.local_used = 0, 0
+        self.open = []
+
+    def push(self, src, dst, device, when=None, like=None):
+        i = self.used
+        self.used += 1
+        send, recv = self.send.at[i], self.recv.at[i]
+        remote = pltpu.make_async_remote_copy(
+            src_ref=src, dst_ref=dst, send_sem=send, recv_sem=recv, device_id=device, device_id_type=MESH
+        )
+        if when is None:
+            remote.start()
+        else:
+            pl.when(when)(remote.start)
+        cp = Copy(remote, self, i, like)
+        self.open.append((cp, when))
+        return cp
+
+    def near(self, src, dst):
+        i = self.local_used
+        self.local_used += 1
+        cp = pltpu.make_async_copy(src, dst, self.local.at[i])
+        cp.start()
+        return cp
+
+    def drain(self, scoped=False):
+        kept = []
+        for cp, when in self.open:
+            if scoped and cp.like is not None:
+                kept.append((cp, when))
+            elif when is None:
+                cp.wait_send()
+            else:
+                pl.when(when)(cp.wait_send)
+        self.open = kept
+
+
+def wait(copies, when=None):
+    def run():
+        for cp in copies:
+            cp.wait_recv()
+
+    if when is None:
+        run()
+    else:
+        pl.when(when)(run)
+
+
+def lanes(mask, width):
+    return jnp.concatenate([mask] * (width // 128), axis=1) if width > 128 else mask
 
 
 def padded_2(cells, sides, width):
@@ -444,7 +559,1041 @@
     )
 
 
+SHAPES = dict(
+    wf=((4, 2, 2, 128, 256), BF16),
+    wm=((9, 4, 2, 2, 32, 256), BF16),
+    wl=((4, 2, 2, 32, 1024), BF16),
+    wr=((2, 2, 2, 128, 512), BF16),
+    wc=((16, 32, 128), BF16),
+    wh=((9, 4, 2, 2, 32, 256), BF16),
+    wq=((9, 4, 2, 2, 32, 256), BF16),
+    wg=((4, 2, 2, 32, 256), BF16),
+    xall=((320, 2048), BF16),
+    maskp=((1280, 128), F32),
+    pre1=((320, 256), F32),
+    pre2=((320, 256), F32),
+    pre3=((320, 1024), F32),
+    bnp1=((8, 256), F32),
+    bnp2=((8, 256), F32),
+    bnp3=((8, 1024), F32),
+    a1=((320, 512), BF16),
+    a2=((320, 512), BF16),
+    a3=((480, 1536), BF16),
+    blk=((320, 1024), BF16),
+    rps=((160, 512), BF16),
+    rpr=((160, 512), BF16),
+    rbuf=((1280, 512), BF16),
+    fown=((1280, 256), BF16),
+    ffull=((1280, 512), BF16),
+    msgb=((1280, 256), BF16),
+    gateb=((1280, 256), BF16),
+    frecv=((2, 160, 512), BF16),
+    grecv=((2, 160, 512), BF16),
+    mrecv=((4, 160, 512), BF16),
+    dcotv=((160, 512), BF16),
+    ccotv=((160, 128), BF16),
+    ods=((160, 512), BF16),
+    olg=((160, 128), BF16),
+    mrg=((160, 512), BF16),
+    dm=((4, 160, 512), BF16),
+    ex=((2, 2, 160, 512), BF16),
+    dmg=((1280, 256), BF16),
+    exg=((2, 1280, 256), BF16),
+    gm=((9, 4, 2, 2, 32, 256), BF16),
+    gh=((9, 4, 2, 2, 32, 256), BF16),
+    gg=((4, 2, 2, 32, 256), BF16),
+    rg=((3, 2, 2, 32, 256), BF16),
+    pg=((2, 2, 32, 256), BF16),
+    zst=((3, 3, 2, 2, 32, 256), BF16),
+    psm=((9, 2, 2, 32, 256), BF16),
+    psh=((9, 2, 2, 32, 256), BF16),
+    gcls=((16, 32, 128), BF16),
+    rcls=((15, 32, 128), BF16),
+    clss=((32, 128), F32),
+    clsr=((32, 128), F32),
+    clso=((32, 128), F32),
+    dfs=((1280, 256), BF16),
+    dfr=((1280, 256), BF16),
+    drs=((640, 512), BF16),
+    drr=((640, 512), BF16),
+    drq=((640, 512), BF16),
+    dro=((3, 160, 512), BF16),
+    dred=((320, 512), BF16),
+    dsr=((160, 1024), BF16),
+    par2=((320, 256), BF16),
+    par1=((320, 256), BF16),
+    dp1r=((160, 256), BF16),
+    rcr=((2, 2, 128, 512), BF16),
+    rcl=((4, 2, 32, 1024), BF16),
+    rcm=((9, 4, 2, 32, 256), BF16),
+    rcf=((4, 2, 128, 256), BF16),
+    ryr=((2, 128, 512), BF16),
+    ryl=((4, 32, 1024), BF16),
+    rym=((9, 4, 32, 256), BF16),
+    ryf=((4, 128, 256), BF16),
+    rzr=((3, 128, 512), BF16),
+    rzl=((3, 32, 1024), BF16),
+    rzm=((3, 9, 32, 256), BF16),
+    rzf=((3, 128, 256), BF16),
+    fnr=((128, 512), BF16),
+    fnl=((32, 1024), BF16),
+    fnm=((9, 32, 256), BF16),
+    fnf=((128, 256), BF16),
+)
+for _i, _w in enumerate((256, 256, 512, 512, 256, 256)):
+    SHAPES["am%d" % _i] = ((8, _w), F32)
+    SHAPES["as%d" % _i] = ((8, _w), F32)
+    SHAPES["at%d" % _i] = ((8, _w), F32)
+    SHAPES["ar%d" % _i] = ((3, 8, _w), F32)
+    SHAPES["az%d" % _i] = ((3, 8, _w), F32)
+
+INS = (
+    "crop_h", "crop_w", "images", "first", "middle", "last", "reduce", "gates",
+    "classes", "heads", "messages", "st1", "st2", "st3", "dcot", "ccot",
+)
+OUTS = dict(
+    o_depth=((160, 512), BF16),
+    o_logits=((160, 128), BF16),
+    o_img=((160, 2048), BF16),
+    o_first=((128, 512), BF16),
+    o_gs1=((2, 8, 256), F32),
+    o_mid=((9, 32, 512), BF16),
+    o_gs2=((2, 8, 256), F32),
+    o_last=((32, 2048), BF16),
+    o_gs3=((2, 8, 512), F32),
+    o_red=((128, 512), BF16),
+    o_heads=((2, 9, 32, 512), BF16),
+    o_mess=((2, 9, 32, 512), BF16),
+    o_gates=((2, 32, 512), BF16),
+    o_cls=((32, 128), F32),
+    rm=((3, 9, 2, 2, 32, 256), BF16),
+    rh=((3, 9, 2, 2, 32, 256), BF16),
+    wfo=((4, 2, 2, 128, 256), BF16),
+)
+
+
+def shift_columns(v):
+    rows, width = v.shape
+    col = lax.broadcasted_iota(jnp.int32, (rows, width), 0)
+    left = jnp.where(col == 0, 0.0, pltpu.roll(v, 1, 0))
+    right = jnp.where(col == rows - 1, 0.0, pltpu.roll(v, rows - 1, 0))
+    return left, right
+
+
+def spread(src, dst, n_img, width):
+    zero = jnp.zeros((80, 3 * width), BF16)
+    for pad in range(n_img + 1):
+        dst[pl.ds(pad * 400, 80), :] = zero
+
+    def body(i, carry):
+        v = src[pl.ds(pl.multiple_of(i * 80, 16), 80), :]
+        left, right = shift_columns(v.astype(F32))
+        row = pl.multiple_of((i + lax.div(i, np.int32(4)) + 1) * 80, 16)
+        dst[pl.ds(row, 80), 0:width] = left.astype(BF16)
+        dst[pl.ds(row, 80), width : 2 * width] = v
+        dst[pl.ds(row, 80), 2 * width : 3 * width] = right.astype(BF16)
+        return carry
+
+    lax.fori_loop(0, 4 * n_img, body, 0)
+
+
+def conv_rows(a3, w, img):
+    acc = None
+    for a in range(3):
+        base = pl.multiple_of((5 * img + a) * 80, 16)
+        part = dot(a3[pl.ds(base, 320), :], w[3 * a : 3 * a + 3].reshape(1536, 256))
+        acc = part if acc is None else acc + part
+    return acc
+
+
+def conv_back(d3, w, img):
+    acc = None
+    for a in range(3):
+        for q in range(3):
+            base = pl.multiple_of((5 * img + a) * 80, 16)
+            tap = 3 * (2 - a) + (2 - q)
+            part = dot_last(d3[pl.ds(base, 320), 256 * q : 256 * q + 256], w[tap].reshape(512, 256))
+            acc = part if acc is None else acc + part
+    return acc
+
+
+def conv_weight(a3, d3, out, n_img):
+    depth = (5 * n_img - 1) * 80
+
+    def body(tap, carry):
+        a = lax.div(tap, np.int32(3))
+        q = tap - 3 * a
+        left = a3[pl.ds(pl.multiple_of(a * 80, 16), depth), pl.ds(pl.multiple_of(q * 512, 128), 512)]
+        out[tap] = dot_first(left, d3[pl.ds(80, depth), 256:512]).astype(BF16).reshape(out.shape[1:])
+        return carry
+
+    lax.fori_loop(0, 9, body, 0)
+
+
+def body(names, *refs):
+    s = SimpleNamespace(**dict(zip(names, refs)))
+    b, r = lax.axis_index("batch"), lax.axis_index("rows")
+    z = lax.div(b, np.int32(4))
+    y = lax.rem(lax.div(b, np.int32(2)), np.int32(2))
+    c = lax.rem(b, np.int32(2))
+    ln = Links(s.send_sems, s.recv_sems, s.near_sems)
+    half, fhalf = 256 * r, 256 * c
+
+    def dev(zz, yy, cc, rr):
+        return (4 * zz + 2 * yy + cc, rr)
+
+    def zk(k):
+        return lax.rem(z + k, np.int32(4))
+
+    core, ypeer, xpeer = dev(z, y, 1 - c, r), dev(z, 1 - y, c, r), dev(z, y, c, 1 - r)
+    special = r == y
+    task = 2 * r + y
+    img = 2 * y + c
+    own_px = pl.multiple_of(320 * img + 160 * r, 16)
+    my_rows = pl.multiple_of(160 * r, 16)
+    other_rows = pl.multiple_of(160 * (1 - r), 16)
+    half = pl.multiple_of(half, 128)
+    ohalf = pl.multiple_of(256 * (1 - r), 128)
+    fhalf = pl.multiple_of(fhalf, 128)
+    offsets = [(dr, dy, dc) for dr in range(2) for dy in range(2) for dc in range(2) if dr + dy + dc]
+
+    def peer(dr, dy, dc):
+        rr = 1 - r if dr else r
+        yy = 1 - y if dy else y
+        cc = 1 - c if dc else c
+        return rr, yy, cc
+
+    def px_of(rr, yy, cc):
+        return pl.multiple_of(320 * (2 * yy + cc) + 160 * rr, 16)
+
+    near0 = [
+        ln.near(s.images, s.xall.at[pl.ds(my_rows, 160)]),
+        ln.near(s.first.at[:, pl.ds(half, 256)], s.wf.at[z, y, c]),
+        ln.near(s.middle.at[:, :, pl.ds(half, 256)], s.wm.at[:, z, y, c]),
+        ln.near(s.last.at[:, pl.ds(pl.multiple_of(1024 * r, 128), 1024)], s.wl.at[z, y, c]),
+        ln.near(s.classes, s.wc.at[b]),
+        ln.near(s.dcot, s.dcotv),
+        ln.near(s.ccot, s.ccotv),
+        ln.near(s.heads.at[y, :, :, pl.ds(fhalf, 256)], s.wh.at[:, z, y, c]),
+        ln.near(s.messages.at[y, :, :, pl.ds(fhalf, 256)], s.wq.at[:, z, y, c]),
+        ln.near(s.gates.at[r, :, pl.ds(fhalf, 256)], s.wg.at[z, y, c]),
+    ]
+    owner = lax.div(z, np.int32(2)) == r
+    zl = lax.rem(z, np.int32(2))
+    red_local = pltpu.make_async_copy(s.reduce, s.wr.at[zl, y, c], s.near_sems.at[SEMS - 1])
+    pl.when(owner)(red_local.start)
+
+    wf_z = [ln.push(s.first.at[:, pl.ds(half, 256)], s.wf.at[z, y, c], dev(zk(k), y, c, r)) for k in (1, 2, 3)]
+    img_x = ln.push(s.images, s.xall.at[pl.ds(my_rows, 160)], xpeer)
+    wm_z = [ln.push(s.middle.at[:, :, pl.ds(half, 256)], s.wm.at[:, z, y, c], dev(zk(k), y, c, r)) for k in (1, 2, 3)]
+
+    for i in range(4):
+        high, wide = s.crop_h[4 * z + i], s.crop_w[4 * z + i]
+        for row in range(4):
+            col = lax.broadcasted_iota(jnp.int32, (80, 128), 0)
+            inside = (col < wide) & (row < high)
+            s.maskp[pl.ds(320 * i + 80 * row, 80), :] = jnp.where(inside, 1.0, 0.0)
+    total = s.crop_h[0] * s.crop_w[0]
+    for i in range(1, 16):
+        total = total + s.crop_h[i] * s.crop_w[i]
+    count = total.astype(F32)
+    mine = pl.multiple_of(320 * img, 16)
+
+    def mask_at(base, rows, width):
+        return lanes(s.maskp[pl.ds(mine + base, rows), :], width)
+
+    for cp in near0:
+        cp.wait()
+    pl.when(owner)(red_local.wait)
+    wait(wf_z)
+    wf_y = ln.push(s.wf.at[:, y, c], s.wf.at[:, y, c], ypeer)
+    wf_c0 = ln.push(s.wf.at[:, y, c], s.wf.at[:, y, c], core)
+    lastl = pl.ds(pl.multiple_of(1024 * r, 128), 1024)
+    wl_z = [ln.push(s.last.at[:, lastl], s.wl.at[z, y, c], dev(zk(k), y, c, r)) for k in (1, 2, 3)]
+    wr_z = [ln.push(s.reduce, s.wr.at[zl, y, c], dev(zk(k), y, c, r), owner) for k in (1, 2, 3)]
+    wait([wf_y])
+    wf_c1 = ln.push(s.wf.at[:, 1 - y, c], s.wf.at[:, 1 - y, c], core)
+    wait([img_x])
+
+    def mask_x(base):
+        s.xall[pl.ds(base, 80), :] = (s.xall[pl.ds(base, 80), :].astype(F32) * mask_at(base, 80, 2048)).astype(BF16)
+
+    rows_loop(320, 80, mask_x)
+    wait(wm_z)
+    wm_y = ln.push(s.wm.at[:, :, y, c], s.wm.at[:, :, y, c], ypeer)
+    wm_c0 = ln.push(s.wm.at[:, :, y, c], s.wm.at[:, :, y, c], core)
+    wait([wf_c0, wf_c1])
+
+    def task_push(src, dst):
+        out = {}
+        for k in range(4):
+            for j in range(2):
+                for i in range(2):
+                    if k + j + i == 0:
+                        continue
+                    yy = 1 - y if j else y
+                    cc = 1 - c if i else c
+                    out[k, j, i] = ln.push(
+                        src.at[yy, :, :, pl.ds(pl.multiple_of(256 * cc, 128), 256)],
+                        dst.at[:, z, y, c],
+                        dev(zk(k) if k else z, yy, cc, r),
+                        mid_or_end(k),
+                    )
+        return out
+
+    ends = (z == 0) | (z == 3)
+
+    def mid_or_end(k):
+        return ends if k == 2 else None
+
+    def task_relay(got, dst):
+        wait([got[k, j, i] for k in (0, 1, 3) for j in range(2) for i in range(2) if k + j + i])
+        inner = jnp.logical_not(ends)
+        wait([got[2, j, i] for j in range(2) for i in range(2)], inner)
+        source = 3 - z
+        target = jnp.where(z == 1, 0, 3)
+        hand = ln.push(dst.at[:, source], dst.at[:, source], dev(target, y, c, r), inner)
+        return hand
+
+    def reduce_all(n, out):
+        m, sm, t, ar, az = (getattr(s, p + str(n)) for p in ("am", "as", "at", "ar", "az"))
+        one = []
+        for i in (1, 2, 3):
+            yy = 1 - y if i & 2 else y
+            cc = 1 - c if i & 1 else c
+            one.append(ln.push(m, ar.at[i - 1], dev(z, yy, cc, r)))
+        wait(one)
+        sm[...] = (m[...] + ar[0]) + (ar[1] + ar[2])
+        two = [ln.push(sm, az.at[k - 1], dev(zk(k), y, c, r)) for k in (1, 2, 3)]
+        wait(two)
+        t[...] = (sm[...] + az[0]) + (az[1] + az[2])
+        return t[...]
+
+    def stats_of(pre, width, msg):
+        m = lanes(s.maskp[pl.ds(mine, 320), :], width)
+        v = pre * m
+        sums = jnp.sum(v, axis=0, keepdims=True)
+        squares = jnp.sum(v * pre, axis=0, keepdims=True)
+        return sums, squares
+
+    def norm_terms(n, bnp, width):
+        t = reduce_all(n, None)
+        if width == 256:
+            rows = [t[i : i + 1] for i in range(4)]
+        else:
+            rows = [jnp.concatenate([t[2 * i : 2 * i + 1], t[2 * i + 1 : 2 * i + 2]], axis=1) for i in range(4)]
+        mean = rows[0] / count
+        inv = lax.rsqrt(rows[1] / count - mean * mean + EPS)
+        bnp[0:1], bnp[1:2], bnp[2:3], bnp[3:4] = mean, inv, rows[2], rows[3]
+
+    def put_stats(n, first, second, width, template):
+        m = getattr(s, "am%d" % n)
+        if template is None:
+            m[...] = jnp.zeros(m.shape, F32)
+        else:
+            m[...] = template[...]
+        if width == 256:
+            m[0:1], m[1:2] = first, second
+        else:
+            m[0:1], m[1:2] = first[:, :512], first[:, 512:]
+            m[2:3], m[3:4] = second[:, :512], second[:, 512:]
+
+    pre = dot(s.xall[...], s.wf[...].reshape(2048, 256))
+    s.pre1[...] = pre
+    first_sum, first_sq = stats_of(pre, 256, None)
+    put_stats(0, first_sum, first_sq, 256, s.st1)
+    wait([wm_y])
+    wm_c1 = ln.push(s.wm.at[:, :, 1 - y, c], s.wm.at[:, :, 1 - y, c], core)
+    norm_terms(0, s.bnp1, 256)
+    heads_got = task_push(s.heads, s.wh)
+
+    def act_from(prebuf, bnp, dst):
+        def step(base):
+            x = (prebuf[pl.ds(base, 80), :] - bnp[0:1]) * bnp[1:2] * bnp[2:3] + bnp[3:4]
+            dst[pl.ds(base, 80), pl.ds(half, 256)] = (gelu_of(x) * mask_at(base, 80, 256)).astype(BF16)
+
+        rows_loop(320, 80, step)
+
+    act_from(s.pre1, s.bnp1, s.a1)
+    a1_x = ln.push(s.a1.at[:, pl.ds(half, 256)], s.a1.at[:, pl.ds(half, 256)], xpeer)
+    wait(wl_z)
+    wl_y = ln.push(s.wl.at[:, y, c], s.wl.at[:, y, c], ypeer)
+    wl_c0 = ln.push(s.wl.at[:, y, c], s.wl.at[:, y, c], core)
+    wait([wm_c0, wm_c1])
+    wait([a1_x])
+    spread(s.a1, s.a3, 1, 512)
+    pre = conv_rows(s.a3, s.wm, 0)
+    s.pre2[...] = pre
+    first_sum, first_sq = stats_of(pre, 256, None)
+    put_stats(1, first_sum, first_sq, 256, s.st2)
+    norm_terms(1, s.bnp2, 256)
+    act_from(s.pre2, s.bnp2, s.a2)
+    a2_x = ln.push(s.a2.at[:, pl.ds(half, 256)], s.a2.at[:, pl.ds(half, 256)], xpeer)
+    wait([wr_z[0]], lax.div(zk(3), np.int32(2)) == r)
+    wait([wr_z[1]], lax.div(zk(2), np.int32(2)) == r)
+    wait([wr_z[2]], lax.div(zk(1), np.int32(2)) == r)
+    wr_y = ln.push(s.wr.at[:, y, c], s.wr.at[:, y, c], ypeer)
+    wr_c0 = ln.push(s.wr.at[:, y, c], s.wr.at[:, y, c], core)
+    wait([wl_y])
+    wl_c1 = ln.push(s.wl.at[:, 1 - y, c], s.wl.at[:, 1 - y, c], core)
+    wait([wl_c0, wl_c1, a2_x])
+    pre = dot(s.a2[...], s.wl[...].reshape(512, 1024))
+    s.pre3[...] = pre
+    first_sum, first_sq = stats_of(pre, 1024, None)
+    put_stats(2, first_sum, first_sq, 1024, s.st3)
+    norm_terms(2, s.bnp3, 1024)
+    mess_got = task_push(s.messages, s.wq)
+    gate_got = {}
+    cls_got = {}
+    for k in range(4):
+        for j in range(2):
+            for i in range(2):
+                if k + j + i == 0:
+                    continue
+                yy = 1 - y if j else y
+                cc = 1 - c if i else c
+                to = dev(zk(k) if k else z, yy, cc, r)
+                gate_got[k, j, i] = ln.push(
+                    s.gates.at[r, :, pl.ds(pl.multiple_of(256 * cc, 128), 256)], s.wg.at[z, y, c], to, yy == r
+                )
+                cls_got[k, j, i] = ln.push(s.classes, s.wc.at[b], to)
+    xhalf = pl.ds(pl.multiple_of(1024 * r, 128), 1024)
+
+    def summed_at(base, rows):
+        x = (s.pre3[pl.ds(base, rows), :] - s.bnp3[0:1]) * s.bnp3[1:2]
+        return x, x * s.bnp3[2:3] + s.bnp3[3:4] + s.xall[pl.ds(base, rows), xhalf].astype(F32)
+
+    def block_step(base):
+        _, v = summed_at(base, 32)
+        s.blk[pl.ds(base, 32), :] = (gelu_of(v) * mask_at(base, 32, 1024)).astype(BF16)
+
+    rows_loop(320, 32, block_step)
+    wait([wr_y])
+    wr_c1 = ln.push(s.wr.at[:, 1 - y, c], s.wr.at[:, 1 - y, c], core)
+    wait([wr_c0, wr_c1])
+    wred = s.wr[...].reshape(1024, 512)
+    s.rps[...] = dot(s.blk[pl.ds(other_rows, 160), :], wred).astype(BF16)
+    red_x = ln.push(s.rps, s.rpr, xpeer)
+    part = dot(s.blk[pl.ds(my_rows, 160), :], wred)
+    wait([red_x])
+    s.rbuf[pl.ds(own_px, 160), :] = (part + s.rpr[...].astype(F32)).astype(BF16)
+
+    def block_of(rr, yy, cc, lo=0, n=160):
+        return s.rbuf.at[pl.ds(pl.multiple_of(px_of(rr, yy, cc) + lo, 16), n)]
+
+    own = block_of(r, y, c)
+    g_x = ln.push(own, own, xpeer)
+    g_y = ln.push(own, own, ypeer)
+    g_c = ln.push(own, own, core)
+    wait([g_x])
+    bx = block_of(1 - r, y, c, 0, 80)
+    g_xy = ln.push(bx, bx, ypeer)
+    wait([g_y])
+    by = block_of(r, 1 - y, c, 80, 80)
+    g_yx = ln.push(by, by, xpeer)
+    bx = block_of(1 - r, y, c)
+    g_c1 = ln.push(bx, bx, core)
+    by = block_of(r, 1 - y, c)
+    g_c2 = ln.push(by, by, core)
+    wait([g_xy, g_yx])
+    bd = block_of(1 - r, 1 - y, c)
+    g_c3 = ln.push(bd, bd, core)
+    heads_hand = task_relay(heads_got, s.wh)
+    wait([heads_hand], ends)
+    wait([g_c, g_c1, g_c2, g_c3])
+
+    def tasks(r3, f3, d3, preh, dfull):
+        spread(s.rbuf, r3, 4, 512)
+
+        def head_step(i, carry):
+            v = conv_rows(r3, s.wh, i)
+            px = pl.multiple_of(i * 320, 16)
+            preh[pl.ds(px, 320), :] = v
+            return carry
+
+        lax.fori_loop(0, 4, head_step, 0)
+
+        def feat_step(base):
+            m = lanes(s.maskp[pl.ds(base, 80), :], 256)
+            s.fown[pl.ds(base, 80), :] = (gelu_of(preh[pl.ds(base, 80), :]) * m).astype(BF16)
+
+        rows_loop(1280, 80, feat_step)
+        f_c = ln.push(s.fown, s.ffull.at[:, pl.ds(fhalf, 256)], core)
+        f_n = ln.near(s.fown, s.ffull.at[:, pl.ds(fhalf, 256)])
+
+        def to_owners(src, dst_of, when):
+            got = {}
+            for o in offsets:
+                rr, yy, cc = peer(*o)
+                got[o] = ln.push(
+                    src.at[pl.ds(px_of(rr, yy, cc), 160)], dst_of().at[:, pl.ds(fhalf, 256)], dev(z, yy, cc, rr), when
+                )
+            return got
+
+        f_own = to_owners(s.fown, lambda: s.frecv.at[r], special)
+
+        def keep(dst, src):
+            def run():
+                dst[:, pl.ds(fhalf, 256)] = src[pl.ds(own_px, 160), :]
+
+            return run
+
+        pl.when(special)(keep(s.frecv.at[r], s.fown))
+        f_n.wait()
+        wait([f_c])
+
+        def gate_ready():
+            for key, cp in gate_got.items():
+                cp.wait_recv()
+
+        pl.when(special)(gate_ready)
+
+        @pl.when(special)
+        def _():
+            def gate_step(base):
+                v = dot(s.ffull[pl.ds(base, 320), :], s.wg[...].reshape(512, 256))
+                s.gateb[pl.ds(base, 320), :] = (1.0 / (1.0 + jnp.exp(-v))).astype(BF16)
+
+            rows_loop(1280, 320, gate_step)
+
+        g_own = to_owners(s.gateb, lambda: s.grecv.at[r], special)
+        pl.when(special)(keep(s.grecv.at[r], s.gateb))
+        spread(s.ffull, f3, 4, 512)
+        mess_hand = task_relay(mess_got, s.wq)
+        wait([mess_hand], ends)
+
+        def mess_step(i, carry):
+            px = pl.multiple_of(i * 320, 16)
+            s.msgb[pl.ds(px, 320), :] = conv_rows(f3, s.wq, i).astype(BF16)
+            return carry
+
+        lax.fori_loop(0, 4, mess_step, 0)
+        m_own = to_owners(s.msgb, lambda: s.mrecv.at[task], None)
+        keep(s.mrecv.at[task], s.msgb)()
+
+        for key, cp in cls_got.items():
+            cp.wait_recv()
+        for o in offsets:
+            wait([f_own[o], g_own[o]], (r != y) if (o[0] + o[1]) % 2 else special)
+            wait([m_own[o]])
+
+        def stream_step(base):
+            rows = pl.ds(base, 32)
+            m = lanes(s.maskp[pl.ds(own_px + base, 32), :], 512)
+            m0, m1, m2, m3 = (s.mrecv[t, rows, :].astype(F32) for t in range(4))
+            mid = m1 + m2
+            sd, sc = mid + m3, m0 + mid
+            gd, gc = s.grecv[0, rows, :].astype(F32), s.grecv[1, rows, :].astype(F32)
+            s.ods[rows, :] = ((s.frecv[0, rows, :].astype(F32) + gd * sd) * m).astype(BF16)
+            merged = (s.frecv[1, rows, :].astype(F32) + gc * sc).astype(BF16)
+            s.mrg[rows, :] = merged
+            m1l = m[:, :128]
+            wcls = s.wc[...].reshape(512, 128)
+            s.olg[rows, :] = (dot(merged, wcls) * m1l).astype(BF16)
+            dj = (s.ccotv[rows, :].astype(F32) * m1l).astype(BF16)
+            s.ccotv[rows, :] = dj
+            dd = s.dcotv[rows, :].astype(F32) * m
+            dmer = dot_last(dj, wcls)
+            s.ex[0, 0, rows, :] = dd.astype(BF16)
+            s.ex[1, 0, rows, :] = dmer.astype(BF16)
+            s.ex[0, 1, rows, :] = (dd * sd * gd * (1.0 - gd)).astype(BF16)
+            s.ex[1, 1, rows, :] = (dmer * sc * gc * (1.0 - gc)).astype(BF16)
+            down, up = dd * gd, dmer * gc
+            both = (down + up).astype(BF16)
+            s.dm[0, rows, :] = up.astype(BF16)
+            s.dm[1, rows, :] = both
+            s.dm[2, rows, :] = both
+            s.dm[3, rows, :] = down.astype(BF16)
+
+        rows_loop(160, 32, stream_step)
+        d_got = {}
+        e_got = {}
+        for o in offsets:
+            rr, yy, cc = peer(*o)
+            tt = 2 * rr + yy
+            ll = pl.ds(pl.multiple_of(256 * cc, 128), 256)
+            d_got[o] = ln.push(s.dm.at[tt, :, ll], s.dmg.at[pl.ds(own_px, 160)], dev(z, yy, cc, rr))
+        for o in offsets:
+            rr, yy, cc = peer(*o)
+            ll = pl.ds(pl.multiple_of(256 * cc, 128), 256)
+            e_got[o] = ln.push(s.ex.at[rr, :, :, ll], s.exg.at[:, pl.ds(own_px, 160)], dev(z, yy, cc, rr), rr == yy)
+        s.dmg[pl.ds(own_px, 160), :] = s.dm[task, :, pl.ds(fhalf, 256)]
+
+        @pl.when(special)
+        def _():
+            for e in range(2):
+                s.exg[e, pl.ds(own_px, 160), :] = s.ex[r, e, :, pl.ds(fhalf, 256)]
+
+        @pl.when(jnp.logical_not(special))
+        def _():
+            s.exg[...] = jnp.zeros(s.exg.shape, BF16)
+
+        out_near = [ln.near(s.ods, s.o_depth), ln.near(s.olg, s.o_logits)]
+        s.gcls[...] = dot_first(s.mrg[...], s.ccotv[...]).astype(BF16).reshape(16, 32, 128)
+        cg = []
+        for k in range(4):
+            for j in range(2):
+                for i in range(2):
+                    if k + j + i == 0:
+                        continue
+                    yy = 1 - y if j else y
+                    cc = 1 - c if i else c
+                    zz = zk(k) if k else z
+                    like = lambda side, n=len(cg): s.rcls.at[n] if side else s.gcls.at[0]
+                    cg.append(ln.push(s.gcls.at[4 * zz + 2 * yy + cc], s.rcls.at[len(cg)], dev(zz, yy, cc, r), None, like))
+        wait([d_got[o] for o in offsets])
+        spread(s.dmg, d3, 4, 256)
+        conv_weight(f3, d3, s.gm, 4)
+        gm_z = [ln.push(s.gm.at[:, zk(k)], s.rm.at[k - 1], dev(zk(k), y, c, r), None, lambda side, k=k: s.rm.at[k - 1] if side else s.gm.at[:, 0]) for k in (1, 2, 3)]
+        wait([e_got[o] for o in offsets], special)
+
+        def back_step(i, carry):
+            px = pl.multiple_of(i * 320, 16)
+            dfull[pl.ds(px, 320), :] = conv_back(d3, s.wq, i)
+            return carry
+
+        lax.fori_loop(0, 4, back_step, 0)
+
+        @pl.when(special)
+        def _():
+            def gate_back(base):
+                rows = pl.ds(base, 320)
+                dfull[rows, :] = dfull[rows, :] + dot_last(s.exg[1, rows, :], s.wg[...].reshape(512, 256))
+
+            rows_loop(1280, 320, gate_back)
+
+        chalf = pl.ds(pl.multiple_of(256 * (1 - c), 128), 256)
+
+        def give(base):
+            rows = pl.ds(base, 80)
+            s.dfs[rows, :] = dfull[rows, chalf].astype(BF16)
+
+        rows_loop(1280, 80, give)
+        df_c = ln.push(s.dfs, s.dfr, core)
+
+        @pl.when(special)
+        def _():
+            s.gg[...] = dot_first(s.ffull[...], s.exg[1]).astype(BF16).reshape(s.gg.shape)
+
+        gg_z = [ln.push(s.gg.at[zk(k)], s.rg.at[k - 1], dev(zk(k), y, c, r), special, lambda side, k=k: s.rg.at[k - 1] if side else s.gg.at[0]) for k in (1, 2, 3)]
+        wait([df_c])
+
+        def dhead_step(base):
+            rows = pl.ds(base, 80)
+            m = lanes(s.maskp[rows, :], 256)
+            d = dfull[rows, pl.ds(fhalf, 256)] + s.dfr[rows, :].astype(F32) + s.exg[0, rows, :].astype(F32)
+            s.dfs2[rows, :] = (slope_of(preh[rows, :]) * d * m).astype(BF16)
+
+        rows_loop(1280, 80, dhead_step)
+        spread(s.dfs2, d3, 4, 256)
+
+        def back_step2(i, carry):
+            px = pl.multiple_of(i * 320, 16)
+            dfull[pl.ds(px, 320), :] = conv_back(d3, s.wh, i)
+            return carry
+
+        lax.fori_loop(0, 4, back_step2, 0)
+        for yy in range(2):
+            src = pl.multiple_of(320 * (2 * yy) + 320 * (1 - c), 16)
+            s.drs[pl.ds(320 * yy, 320), :] = dfull[pl.ds(src, 320), :].astype(BF16)
+        dr_c = ln.push(s.drs, s.drr, core)
+        conv_weight(r3, d3, s.gh, 4)
+        gh_z = [ln.push(s.gh.at[:, zk(k)], s.rh.at[k - 1], dev(zk(k), y, c, r), None, lambda side, k=k: s.rh.at[k - 1] if side else s.gh.at[:, 0]) for k in (1, 2, 3)]
+        wait([dr_c])
+        for yy in range(2):
+            src = pl.multiple_of(320 * (2 * yy) + 320 * c, 16)
+            rows = pl.ds(320 * yy, 320)
+            s.drq[rows, :] = (dfull[pl.ds(src, 320), :] + s.drr[rows, :].astype(F32)).astype(BF16)
+        ro = []
+        for dr, dy in ((1, 0), (0, 1), (1, 1)):
+            rr, yy, _ = peer(dr, dy, 0)
+            src = s.drq.at[pl.ds(pl.multiple_of(320 * yy + 160 * rr, 16), 160)]
+            ro.append(ln.push(src, s.dro.at[len(ro)], dev(z, yy, c, rr)))
+        wait(ro)
+        keep_rows = pl.ds(pl.multiple_of(320 * y + 160 * r, 16), 160)
+        total_red = s.drq[keep_rows, :].astype(F32)
+        for i in range(3):
+            total_red = total_red + s.dro[i].astype(F32)
+        s.dred[pl.ds(my_rows, 160), :] = total_red.astype(BF16)
+        for cp in out_near:
+            cp.wait()
+        ln.drain(scoped=True)
+        return cg, gm_z, gg_z, gh_z
+
+    state = {}
+
+    def scope_tasks(*scr):
+        state["t"] = tasks(*scr)
+
+    pl.run_scoped(
+        scope_tasks,
+        pltpu.VMEM((1680, 1536), BF16),
+        pltpu.VMEM((1680, 1536), BF16),
+        pltpu.VMEM((1680, 768), BF16),
+        pltpu.VMEM((1280, 256), F32),
+        pltpu.VMEM((1280, 512), F32),
+    )
+    cg, gm_z, gg_z, gh_z = state["t"]
+
+    dr_x = ln.push(s.dred.at[pl.ds(my_rows, 160)], s.dred.at[pl.ds(my_rows, 160)], xpeer)
+    wfo_x = ln.push(s.wf, s.wfo, xpeer)
+
+    def block_back(*late):
+        for name, ref in zip(LATE, late):
+            setattr(s, name, ref)
+        gr, gl, gq, gf = s.gr, s.gl, s.gq, s.gf
+
+        def to_core(g, rc, lead):
+            at = g.at[:, :, :, 1 - c] if lead else g.at[:, :, 1 - c]
+            return ln.push(at, rc, core)
+
+        def add_core(g, rc, lead):
+            if lead:
+                for t in range(9):
+                    rc[t] = (rc[t].astype(F32) + g[t, :, :, c].astype(F32)).astype(BF16)
+            else:
+                for t in range(rc.shape[0]):
+                    rc[t] = (rc[t].astype(F32) + g[t, :, c].astype(F32)).astype(BF16)
+
+        def to_y(rc, ry, lead):
+            return ln.push(rc.at[:, :, 1 - y] if lead else rc.at[:, 1 - y], ry, ypeer)
+
+        def add_y(rc, ry, lead):
+            for t in range(ry.shape[0]):
+                mine_y = rc[t, :, y] if lead else rc[t, y]
+                ry[t] = (ry[t].astype(F32) + mine_y.astype(F32)).astype(BF16)
+
+        def to_z(ry, rz, lead):
+            return [
+                ln.push(ry.at[:, zk(k)] if lead else ry.at[zk(k)], rz.at[k - 1], dev(zk(k), y, c, r)) for k in (1, 2, 3)
+            ]
+
+        def add_z(ry, rz, fin, lead):
+            mine_z = (ry[:, z] if lead else ry[z]).astype(F32)
+            fin[...] = ((mine_z + rz[0].astype(F32)) + (rz[1].astype(F32) + rz[2].astype(F32))).astype(BF16)
+
+        wait([dr_x])
+
+        def d3_step(i, carry):
+            su, sux = carry
+            rows = pl.ds(pl.multiple_of(i * 32, 16), 32)
+            x, v = summed_at(i * 32, 32)
+            u = slope_of(v) * s.u3[rows, :] * mask_at(i * 32, 32, 1024)
+            s.u3[rows, :] = u
+            s.dsum[rows, :] = u.astype(BF16)
+            return su + jnp.sum(u, axis=0, keepdims=True), sux + jnp.sum(u * x, axis=0, keepdims=True)
+
+        s.u3[...] = dot_last(s.dred[...], s.wr[...].reshape(1024, 512))
+        nil = jnp.zeros((1, 1024), F32)
+        su, sux = lax.fori_loop(0, 10, d3_step, (nil, nil))
+        put_stats(3, su, sux, 1024, None)
+        ds_x = ln.push(s.dsum.at[pl.ds(other_rows, 160)], s.dsr, xpeer)
+        gr[...] = dot_first(s.blk[...], s.dred[...]).astype(BF16).reshape(gr.shape)
+        gr_c = to_core(gr, s.rcr, False)
+        t = reduce_all(3, None)
+        gs3 = ln.push(s.at3, s.o_gs3.at[r], xpeer)
+        gs3n = ln.near(s.at3, s.o_gs3.at[r])
+        mu = jnp.concatenate([t[0:1], t[1:2]], axis=1) / count
+        mux = jnp.concatenate([t[2:3], t[3:4]], axis=1) / count
+
+        def dp3_step(base):
+            rows = pl.ds(base, 32)
+            x = (s.pre3[rows, :] - s.bnp3[0:1]) * s.bnp3[1:2]
+            d = mask_at(base, 32, 1024) * (s.bnp3[2:3] * s.bnp3[1:2]) * (s.u3[rows, :] - mu - x * mux)
+            s.dp3[rows, :] = d.astype(BF16)
+
+        rows_loop(320, 32, dp3_step)
+
+        def partial_out(pas, value_of):
+            pas[...] = value_of(ohalf).astype(BF16)
+
+        wlast = s.wl
+        s.u3[:, 0:512] = dot_last(s.dp3[...], wlast[...].reshape(512, 1024))
+        s.pas2[...] = s.u3[:, pl.ds(ohalf, 256)].astype(BF16)
+        pa2 = ln.push(s.pas2, s.par2, xpeer)
+        gl[...] = dot_first(s.a2[...], s.dp3[...]).astype(BF16).reshape(gl.shape)
+        gl_c = to_core(gl, s.rcl, False)
+        wait([gr_c])
+        add_core(gr, s.rcr, False)
+        gr_y = to_y(s.rcr, s.ryr, False)
+        wait([pa2])
+
+        def norm_back(n, par, prebuf, bnp, dst, out_gs):
+            def u_step(i, carry):
+                su_, sux_ = carry
+                base = pl.multiple_of(i * 80, 16)
+                rows = pl.ds(base, 80)
+                x = (prebuf[rows, :] - bnp[0:1]) * bnp[1:2]
+                v = x * bnp[2:3] + bnp[3:4]
+                d = s.u3[rows, pl.ds(half, 256)] + par[rows, :].astype(F32)
+                u = slope_of(v) * d * mask_at(base, 80, 256)
+                s.u3[rows, 512:768] = u
+                return su_ + jnp.sum(u, axis=0, keepdims=True), sux_ + jnp.sum(u * x, axis=0, keepdims=True)
+
+            nil_ = jnp.zeros((1, 256), F32)
+            su_, sux_ = lax.fori_loop(0, 4, u_step, (nil_, nil_))
+            put_stats(n, su_, sux_, 256, None)
+            t_ = reduce_all(n, None)
+            gsx = ln.push(getattr(s, "at%d" % n), out_gs.at[r], xpeer)
+            gsn = ln.near(getattr(s, "at%d" % n), out_gs.at[r])
+            mu_, mux_ = t_[0:1] / count, t_[1:2] / count
+
+            def d_step(base):
+                rows = pl.ds(base, 80)
+                x = (prebuf[rows, :] - bnp[0:1]) * bnp[1:2]
+                d = mask_at(base, 80, 256) * (bnp[2:3] * bnp[1:2]) * (s.u3[rows, 512:768] - mu_ - x * mux_)
+                dst[rows, :] = d.astype(BF16)
+
+            rows_loop(320, 80, d_step)
+            return gsx, gsn
+
+        gs2, gs2n = norm_back(4, s.par2, s.pre2, s.bnp2, s.dp2, s.o_gs2)
+        spread(s.dp2, s.d3m, 1, 256)
+        s.u3[:, 0:512] = conv_back(s.d3m, s.wm, 0)
+        s.pas1[...] = s.u3[:, pl.ds(ohalf, 256)].astype(BF16)
+        pa1 = ln.push(s.pas1, s.par1, xpeer)
+        conv_weight(s.a3, s.d3m, gq, 1)
+        gq_c = to_core(gq, s.rcm, True)
+        wait([gl_c])
+        add_core(gl, s.rcl, False)
+        gl_y = to_y(s.rcl, s.ryl, False)
+        wait([pa1])
+        gs1, gs1n = norm_back(5, s.par1, s.pre1, s.bnp1, s.dp1, s.o_gs1)
+        dp_x = ln.push(s.dp1.at[pl.ds(other_rows, 160)], s.dp1r, xpeer)
+        gf[...] = dot_first(s.xall[...], s.dp1[...]).astype(BF16).reshape(gf.shape)
+        gf_c = to_core(gf, s.rcf, False)
+        wait([gq_c])
+        add_core(gq, s.rcm, True)
+        gq_y = to_y(s.rcm, s.rym, True)
+        wait([gf_c])
+        add_core(gf, s.rcf, False)
+        gf_y = to_y(s.rcf, s.ryf, False)
+
+        wait([gr_y])
+        add_y(s.rcr, s.ryr, False)
+        gr_z = [
+            ln.push(s.ryr.at[lax.rem(zk(k), np.int32(2))], s.rzr.at[k - 1], dev(zk(k), y, c, r),
+                    lax.div(zk(k), np.int32(2)) == r)
+            for k in (1, 2, 3)
+        ]
+        wait([gl_y])
+        add_y(s.rcl, s.ryl, False)
+        gl_z = to_z(s.ryl, s.rzl, False)
+        wait([gq_y])
+        add_y(s.rcm, s.rym, True)
+        gq_z = to_z(s.rym, s.rzm, True)
+        wait([gf_y])
+        add_y(s.rcf, s.ryf, False)
+        gf_z = to_z(s.ryf, s.rzf, False)
+
+        wait([wfo_x])
+        wfo_n = ln.near(s.wfo, s.wfov)
+        wait([dp_x, ds_x])
+        wfo_n.wait()
+        mine_d = s.dp1[pl.ds(my_rows, 160), :]
+        other_d = s.dp1r[...]
+        for q in range(2):
+            cols = slice(1024 * q, 1024 * q + 1024)
+            wa = s.wf[2 * q : 2 * q + 2].reshape(1024, 256)
+            wb = s.wfov[2 * q : 2 * q + 2].reshape(1024, 256)
+            s.u3[pl.ds(0, 160), :] = dot_last(mine_d, wa) + dot_last(other_d, wb)
+
+            def img_step(base):
+                rows = pl.ds(base, 32)
+                m = mask_at(my_rows + base, 32, 1024)
+                own_d = s.dsum[pl.ds(my_rows + base, 32), :].astype(F32)
+                far_d = s.dsr[rows, :].astype(F32)
+                d = jnp.where(r == q, own_d, far_d)
+                s.oimg[rows, cols] = ((s.u3[rows, :] + d) * m).astype(BF16)
+
+            rows_loop(160, 32, img_step)
+        img_n = ln.near(s.oimg, s.o_img)
+
+        def task_out(got, rm, g, ps, out):
+            wait(got)
+            for part in range(3):
+                cps = [ln.near(rm.at[k, 3 * part : 3 * part + 3], s.zst.at[k]) for k in range(3)]
+                for cp in cps:
+                    cp.wait()
+                for t in range(3):
+                    v = g[3 * part + t, z].astype(F32) + s.zst[0, t].astype(F32)
+                    v = v + (s.zst[1, t].astype(F32) + s.zst[2, t].astype(F32))
+                    ps[3 * part + t] = v.astype(BF16)
+            lanes_out = pl.ds(fhalf, 256)
+            sent = []
+            for i in (1, 2, 3):
+                yy = 1 - y if i & 2 else y
+                cc = 1 - c if i & 1 else c
+                sent.append(ln.push(ps.at[:, yy, cc], out.at[y, :, :, lanes_out], dev(z, yy, cc, r)))
+            return sent, ln.near(ps.at[:, y, c], out.at[y, :, :, lanes_out])
+
+        ms, mn = task_out(gm_z, s.rm, s.gm, s.psm, s.o_mess)
+        hs, hn = task_out(gh_z, s.rh, s.gh, s.psh, s.o_heads)
+
+        @pl.when(special)
+        def _():
+            for cp in gg_z:
+                cp.wait_recv()
+            v = (s.gg[z].astype(F32) + s.rg[0].astype(F32)) + (s.rg[1].astype(F32) + s.rg[2].astype(F32))
+            s.pg[...] = v.astype(BF16)
+
+        gx = {}
+        for o in offsets:
+            rr, yy, cc = peer(*o)
+            gx[o] = ln.push(s.pg.at[yy, cc], s.o_gates.at[r, :, pl.ds(fhalf, 256)], dev(z, yy, cc, rr), special)
+        gate_near = pltpu.make_async_copy(
+            s.pg.at[y, c], s.o_gates.at[r, :, pl.ds(fhalf, 256)], s.near_sems.at[SEMS - 2]
+        )
+        pl.when(special)(gate_near.start)
+
+        wait(cg)
+        v = s.gcls[b].astype(F32)
+        for i in range(15):
+            v = v + s.rcls[i].astype(F32)
+        s.clss[...] = v
+        cls_x = ln.push(s.clss, s.clsr, xpeer)
+
+        wait([gr_z[0], gr_z[1], gr_z[2]], owner)
+
+        @pl.when(owner)
+        def _():
+            v_ = s.ryr[zl].astype(F32) + s.rzr[0].astype(F32)
+            s.fnr[...] = (v_ + (s.rzr[1].astype(F32) + s.rzr[2].astype(F32))).astype(BF16)
+
+        gr_x = ln.push(s.fnr, s.o_red, xpeer, owner)
+        red_near = pltpu.make_async_copy(s.fnr, s.o_red, s.near_sems.at[SEMS - 3])
+        pl.when(owner)(red_near.start)
+        wait(gl_z)
+        add_z(s.ryl, s.rzl, s.fnl, False)
+        gl_x = ln.push(s.fnl, s.o_last.at[:, lastl], xpeer)
+        n1 = ln.near(s.fnl, s.o_last.at[:, lastl])
+        wait(gq_z)
+        add_z(s.rym, s.rzm, s.fnm, True)
+        gq_x = ln.push(s.fnm, s.o_mid.at[:, :, pl.ds(half, 256)], xpeer)
+        n2 = ln.near(s.fnm, s.o_mid.at[:, :, pl.ds(half, 256)])
+        wait(gf_z)
+        add_z(s.ryf, s.rzf, s.fnf, False)
+        gf_x = ln.push(s.fnf, s.o_first.at[:, pl.ds(half, 256)], xpeer)
+        n3 = ln.near(s.fnf, s.o_first.at[:, pl.ds(half, 256)])
+        wait([cls_x])
+        s.clso[...] = s.clss[...] + s.clsr[...]
+        n4 = ln.near(s.clso, s.o_cls)
+        wait([gr_x], jnp.logical_not(owner))
+        wait([gl_x, gq_x, gf_x, gs1, gs2, gs3])
+        wait(ms + hs)
+        for o in offsets:
+            wait([gx[o]], (r != y) if (o[0] + o[1]) % 2 else special)
+        pl.when(special)(gate_near.wait)
+        pl.when(owner)(red_near.wait)
+        for cp in (gs1n, gs2n, gs3n, img_n, mn, hn, n1, n2, n3, n4):
+            cp.wait()
+        ln.drain()
+
+    pl.run_scoped(block_back, *[pltpu.VMEM(*v) for v in LATE.values()])
+
+
+SHAPES["dfs2"] = ((1280, 256), BF16)
+
+
+LATE = dict(
+    u3=((320, 1024), F32),
+    dp3=((320, 1024), BF16),
+    d3m=((480, 768), BF16),
+    dsum=((320, 1024), BF16),
+    oimg=((160, 2048), BF16),
+    pas1=((320, 256), BF16),
+    pas2=((320, 256), BF16),
+    dp1=((320, 256), BF16),
+    dp2=((320, 256), BF16),
+    wfov=((4, 2, 2, 128, 256), BF16),
+    gr=((2, 2, 2, 128, 512), BF16),
+    gl=((4, 2, 2, 32, 1024), BF16),
+    gq=((9, 4, 2, 2, 32, 256), BF16),
+    gf=((4, 2, 2, 128, 256), BF16),
+)
+
+
+def fast(args):
+    (
+        images, crop_height, crop_width, w_first, gain_first, shift_first, w_middle, gain_middle, shift_middle,
+        w_last, gain_last, shift_last, w_reduce, w_heads, w_message, w_gates, w_classes, depth_cot, class_cot,
+    ) = args
+    b, r = lax.axis_index("batch"), lax.axis_index("rows")
+    batch = lax.axis_size("batch")
+    classes = w_classes.shape[1]
+
+    def placed(vec):
+        share = vec.shape[0]
+        full = jnp.tile(vec.astype(F32), batch)
+        owner = lax.iota(jnp.int32, share * batch) // share
+        return lax.dynamic_slice_in_dim(jnp.where(owner == b, full, 0.0), r * (share * batch // 2), share * batch // 2)
+
+    def small(gain, shift):
+        zero = jnp.zeros((256,), F32)
+        return jnp.stack([zero, zero, placed(gain), placed(shift), zero, zero, zero, zero])
+
+    st3 = jnp.concatenate(
+        [jnp.zeros((4, 512), F32), placed(gain_last).reshape(2, 512), placed(shift_last).reshape(2, 512)]
+    )
+    ins = (
+        crop_height, crop_width, images.reshape(160, 2048), w_first, w_middle, w_last, w_reduce, w_gates,
+        jnp.pad(w_classes, ((0, 0), (0, 128 - classes))), w_heads, w_message,
+        small(gain_first, shift_first), small(gain_middle, shift_middle), st3,
+        depth_cot.reshape(160, 512), jnp.pad(class_cot.reshape(160, classes), ((0, 0), (0, 128 - classes))),
+    )
+    names = list(INS) + list(OUTS) + list(SHAPES) + ["send_sems", "recv_sems", "near_sems"]
+    smem, hbm, vmem = (pl.BlockSpec(memory_space=m) for m in (pltpu.SMEM, pl.ANY, pltpu.VMEM))
+    spec = {"crop_h": smem, "crop_w": smem, "st1": vmem, "st2": vmem, "st3": vmem}
+    outs = pl.pallas_call(
+        functools.partial(body, names),
+        out_shape=[jax.ShapeDtypeStruct(*v) for v in OUTS.values()],
+        in_specs=[spec.get(n, hbm) for n in INS],
+        out_specs=[hbm] * len(OUTS),
+        scratch_shapes=[pltpu.VMEM(*v) for v in SHAPES.values()]
+        + [pltpu.SemaphoreType.DMA((SEMS,)) for _ in range(3)],
+        compiler_params=pltpu.CompilerParams(has_side_effects=True, vmem_limit_bytes=64 * 2**20),
+        name="residual_distill",
+    )(*ins)
+    o = dict(zip(OUTS, outs))
+
+    def share_of(v, axis):
+        return v.astype(F32)
+
+    def vector(gs, gain):
+        per = gs.shape[2] * (gs.shape[1] // 8)
+        width = 256 if gs.shape[2] == 256 else 1024
+        rows = 1 if width == 256 else 2
+        first = gs[:, rows * (1 if gain else 0) : rows * (2 if gain else 1)].reshape(2 * width)
+        share = 2 * width // batch
+        return lax.dynamic_slice_in_dim(first, b * share, share)
+
+    return (
+        o["o_depth"].reshape(1, 2, 80, 512),
+        o["o_logits"][:, :classes].reshape(1, 2, 80, classes),
+        o["o_img"].astype(F32).reshape(1, 2, 80, 2048),
+        o["o_first"].astype(F32),
+        vector(o["o_gs1"], True),
+        vector(o["o_gs1"], False),
+        o["o_mid"].astype(F32),
+        vector(o["o_gs2"], True),
+        vector(o["o_gs2"], False),
+        o["o_last"].astype(F32),
+        vector(o["o_gs3"], True),
+        vector(o["o_gs3"], False),
+        o["o_red"].astype(F32),
+        o["o_heads"].astype(F32),
+        o["o_mess"].astype(F32),
+        o["o_gates"].astype(F32),
+        o["o_cls"][:, :classes],
+    )
+
+
 def solution(mesh):
+    def step(*args):
+        if mesh.shape["batch"] == 16 and mesh.shape["rows"] == 2:
+            return fast(args)
+        return shards(*args)
+
     placed = (
         P("batch", "rows", None, None),
         P(),
@@ -467,7 +1616,7 @@
         P("batch", "rows", None, None),
     )
     return jax.shard_map(
-        shards,
+        step,
         mesh=mesh,
         in_specs=placed,
         out_specs=(

time: 2300 us -> 409 us (0.18)
  waiting for transfers between devices: 1540 us -> 0 us
  Pallas kernels: 0 us -> 383 us
  blocking collectives: 335 us -> 0 us
  matrix products: 224 us -> 0 us
  starting transfers between devices: 81 us -> 0 us
  other arithmetic: 76.4 us -> 11.1 us
    reduce_scatter x10 -> x0, waiting for transfers between devices: 969 us -> none  [the longest x1 370 us: shards(): lax.psum_scatter(grad_message, 'batch', scatter_dimension=2, tiled=True)]
    all_gather x9 -> x0, waiting for transfers between devices: 533 us -> none  [the longest x1 213 us: shards(): lax.all_gather(message_own, 'rows', axis=0, tiled=True)]
    pallas_call x0 -> x1, Pallas kernels: none -> 383 us  [fast(): pl.pallas_call(functools.partial(body, names), out_shape=[jax.ShapeDtypeS...]
    psum x7 -> x0, blocking collectives: 248 us -> none  [the longest x3 122 us: norm_backward(): shift_part, gain_part = lax.psum((shift_part, gain_part), ('batch', 'rows'))]
    dot_general x261 -> x0, matrix products: 224 us -> none  [the longest x87 89.3 us: project_back(): jnp.einsum('nrck,jk->nrcj', upstream, weight, preferred_element_type=jnp....]
    ppermute x28 -> x0, starting transfers between devices: 80 us -> none  [the longest x14 60.8 us: padded_2(): lax.ppermute(tail, axis, [(i, (i + 1) % count) for i in range(ends)])]
    all_gather x3 -> x0, blocking collectives: 55.4 us -> none  [the longest x1 19.2 us: shards(): lax.all_gather(w_classes, 'batch', axis=0, tiled=True)]
    unnamed x1 -> x0, blocking collectives: 31.1 us -> none
  transfers between devices with their start and end apart: 48 -> 0, of which waited for: 17 -> 0; matrix products, arithmetic and copies ran while one was open for 13% -> 0% of each run, Pallas kernels for 0% -> 0%
where the time goes in v1:
time: 409 us; the launch traced here: 408 us
  Pallas kernels  383 us (94%)
  local copies, waits for them, and re-layouts  13.2 us (3%)
  other arithmetic  11.1 us (3%)
    pallas_call x1, Pallas kernels, fast(): pl.pallas_call(functools.partial(body, names), out_shape=[jax.ShapeDtypeS...  383 us

profile of v1, /device:TPU:0, one launch (start us, length us, event | category | flops | bytes accessed | tf_op | source)
XLA Modules:
  0.0 407.7 jit_solution(10823205492907990971)
XLA Ops:
  0.7 0.7 tile.24
  1.3 0.1 tile.25
  1.4 0.7 tile.26
  2.3 0.7 tile.28
  3.0 0.7 tile.60
  4.0 0.7 maximum_maximum_fusion.1
  4.7 0.7 convert_element_type.48
  5.4 0.7 convert_element_type.49
  6.1 0.7 pad_maximum_fusion.refs_13_
  6.7 0.8 copy.36
  7.6 0.6 pad.9.refs_15_
  8.2 1.3 pad.8.refs_8_
  9.5 382.6 %residual_distill.1 = (bf16[160,512]{1,0:T(8,128)(2,1)}, bf16[160,128]{1,0:T(8,128)(2,1)}, bf16[160,2048]{1,0:T(8,128)(2,1)}, bf16[128,512]{1,0:T(8,128)(2,1)}, ...) custom-call(s32[16]{0:T(128)} %refs_0_.1, ...), custom_call_target="tpu_custom_call" | custom-call | tf_op jit(solution)/shard_map/residual_distill/pallas_call | solution.py:1547
  392.1 2.3 convert.1
  394.5 1.2 convert_element_type.54
  395.7 1.2 convert_element_type.55
  396.9 0.9 convert_element_type.51
  397.8 0.7 convert_element_type.50
  398.5 0.7 convert_element_type.52
  399.2 0.7 convert_element_type.53
  399.9 0.7 convert_element_type.56
  400.6 0.6 dynamic_slice.46
  401.2 0.6 dynamic_slice.47
  401.8 0.7 copy.37
  402.5 0.8 fusion.9
  403.3 0.6 dynamic_slice.42
  403.9 0.6 dynamic_slice.43
  404.5 0.8 fusion.8
  405.3 0.6 dynamic_slice.44
  405.8 0.6 dynamic_slice.45
  406.4 0.7 copy.42
  407.1 0.6 copy.43
  (43 shorter events, 0.7 us)
Async XLA Ops:
  392.1 2.4 copy-start.1
  394.5 1.2 copy-start
  395.6 1.2 copy-start.2
  395.7 2.1 copy-start.6
  395.7 2.8 copy-start.5
  395.7 3.5 copy-start.4
  396.8 3.1 copy-start.7
  396.8 3.8 copy-start.10
  396.8 5.0 %copy-start.8 = (bf16[160,128]{1,0:T(8,128)(2,1)S(1)}, bf16[160,128]{1,0:T(8,128)(2,1)}, u32[]{:S(2)}) copy-start(bf16[160,128]{1,0:T(8,128)(2,1)} %get-tuple-element.32) | copy-start | bytes 122884
  396.8 9.6 %copy-start.3 = (bf16[160,512]{1,0:T(8,128)(2,1)S(1)}, bf16[160,512]{1,0:T(8,128)(2,1)}, u32[]{:S(2)}) copy-start(bf16[160,512]{1,0:T(8,128)(2,1)} %get-tuple-element.31) | copy-start | bytes 491524
  396.9 10.2 %copy-start.9 = (f32[32,128]{1,0:T(8,128)S(1)}, f32[32,128]{1,0:T(8,128)}, u32[]{:S(2)}) copy-start(f32[32,128]{1,0:T(8,128)} %get-tuple-element.44) | copy-start | bytes 49156

commit v2 on v1

--- a/solution.py
+++ b/solution.py
@@ -15,7 +15,8 @@
 BF16 = jnp.bfloat16
 ROOT = 0.7978845608028654
 CUBE = 0.044715
-SEMS = 320
+SENDS = 240
+NEAR = 54
 
 
 def dot(left, right):
@@ -64,6 +65,35 @@
         else:
             ref = self.like(0)
             pltpu.make_async_copy(ref, ref, self.links.send.at[self.index]).wait()
+
+
+class Group:
+    scoped = True
+
+    def __init__(self, links, index, like):
+        self.links, self.index, self.like = links, index, like
+
+    def push(self, src, dst, device, when=None):
+        remote = pltpu.make_async_remote_copy(
+            src_ref=src,
+            dst_ref=dst,
+            send_sem=self.links.send.at[self.index],
+            recv_sem=self.links.recv.at[self.index],
+            device_id=device,
+            device_id_type=MESH,
+        )
+        if when is None:
+            remote.start()
+        else:
+            pl.when(when)(remote.start)
+
+    def wait_recv(self):
+        ref = self.like()
+        pltpu.make_async_copy(ref, ref, self.links.recv.at[self.index]).wait()
+
+    def wait_send(self):
+        ref = self.like()
+        pltpu.make_async_copy(ref, ref, self.links.send.at[self.index]).wait()
 
 
 class Links:
@@ -87,6 +117,12 @@
         self.open.append((cp, when))
         return cp
 
+    def group(self, like, when=None):
+        cp = Group(self, self.used, like)
+        self.used += 1
+        self.open.append((cp, when))
+        return cp
+
     def near(self, src, dst):
         i = self.local_used
         self.local_used += 1
@@ -97,7 +133,7 @@
     def drain(self, scoped=False):
         kept = []
         for cp, when in self.open:
-            if scoped and cp.like is not None:
+            if scoped and isinstance(cp, Copy) and cp.like is not None:
                 kept.append((cp, when))
             elif when is None:
                 cp.wait_send()
@@ -563,8 +599,13 @@
     wf=((4, 2, 2, 128, 256), BF16),
     wm=((9, 4, 2, 2, 32, 256), BF16),
     wl=((4, 2, 2, 32, 1024), BF16),
-    wr=((2, 2, 2, 128, 512), BF16),
+    wr=((4, 2, 128, 512), BF16),
     wc=((16, 32, 128), BF16),
+    wcs=((32, 128), BF16),
+    wcv=((32, 40), BF16),
+    cct=((2, 40, 80), BF16),
+    ctf=((128, 128), F32),
+    xh=((320, 1024), BF16),
     wh=((9, 4, 2, 2, 32, 256), BF16),
     wq=((9, 4, 2, 2, 32, 256), BF16),
     wg=((4, 2, 2, 32, 256), BF16),
@@ -587,47 +628,39 @@
     ffull=((1280, 512), BF16),
     msgb=((1280, 256), BF16),
     gateb=((1280, 256), BF16),
-    frecv=((2, 160, 512), BF16),
-    grecv=((2, 160, 512), BF16),
     mrecv=((4, 160, 512), BF16),
     dcotv=((160, 512), BF16),
     ccotv=((160, 128), BF16),
+    olt=((2, 40, 80), BF16),
     ods=((160, 512), BF16),
     olg=((160, 128), BF16),
     mrg=((160, 512), BF16),
-    dm=((4, 160, 512), BF16),
-    ex=((2, 2, 160, 512), BF16),
+    fg=((2, 2, 160, 512), BF16),
     dmg=((1280, 256), BF16),
     exg=((2, 1280, 256), BF16),
     gm=((9, 4, 2, 2, 32, 256), BF16),
     gh=((9, 4, 2, 2, 32, 256), BF16),
     gg=((4, 2, 2, 32, 256), BF16),
     rg=((3, 2, 2, 32, 256), BF16),
-    pg=((2, 2, 32, 256), BF16),
-    zst=((3, 3, 2, 2, 32, 256), BF16),
-    psm=((9, 2, 2, 32, 256), BF16),
-    psh=((9, 2, 2, 32, 256), BF16),
+    hop=((2, 9, 2, 2, 32, 256), BF16),
     gcls=((16, 32, 128), BF16),
     rcls=((15, 32, 128), BF16),
-    clss=((32, 128), F32),
     clsr=((32, 128), F32),
-    clso=((32, 128), F32),
     dfs=((1280, 256), BF16),
     dfr=((1280, 256), BF16),
     drs=((640, 512), BF16),
     drr=((640, 512), BF16),
-    drq=((640, 512), BF16),
     dro=((3, 160, 512), BF16),
     dred=((320, 512), BF16),
     dsr=((160, 1024), BF16),
     par2=((320, 256), BF16),
     par1=((320, 256), BF16),
     dp1r=((160, 256), BF16),
-    rcr=((2, 2, 128, 512), BF16),
+    rcr=((4, 2, 128, 512), BF16),
     rcl=((4, 2, 32, 1024), BF16),
     rcm=((9, 4, 2, 32, 256), BF16),
     rcf=((4, 2, 128, 256), BF16),
-    ryr=((2, 128, 512), BF16),
+    ryr=((4, 128, 512), BF16),
     ryl=((4, 32, 1024), BF16),
     rym=((9, 4, 32, 256), BF16),
     ryf=((4, 128, 256), BF16),
@@ -635,10 +668,6 @@
     rzl=((3, 32, 1024), BF16),
     rzm=((3, 9, 32, 256), BF16),
     rzf=((3, 128, 256), BF16),
-    fnr=((128, 512), BF16),
-    fnl=((32, 1024), BF16),
-    fnm=((9, 32, 256), BF16),
-    fnf=((128, 256), BF16),
 )
 for _i, _w in enumerate((256, 256, 512, 512, 256, 256)):
     SHAPES["am%d" % _i] = ((8, _w), F32)
@@ -649,17 +678,17 @@
 
 INS = (
     "crop_h", "crop_w", "images", "first", "middle", "last", "reduce", "gates",
-    "classes", "heads", "messages", "st1", "st2", "st3", "dcot", "ccot",
+    "classes", "heads", "messages", "gains", "dcot", "ccot",
 )
 OUTS = dict(
     o_depth=((160, 512), BF16),
-    o_logits=((160, 128), BF16),
+    o_logits=((2, 40, 80), BF16),
     o_img=((160, 2048), BF16),
     o_first=((128, 512), BF16),
     o_gs1=((2, 8, 256), F32),
     o_mid=((9, 32, 512), BF16),
     o_gs2=((2, 8, 256), F32),
-    o_last=((32, 2048), BF16),
+    o_last=((2, 32, 1024), BF16),
     o_gs3=((2, 8, 512), F32),
     o_red=((128, 512), BF16),
     o_heads=((2, 9, 32, 512), BF16),
@@ -669,6 +698,8 @@
     rm=((3, 9, 2, 2, 32, 256), BF16),
     rh=((3, 9, 2, 2, 32, 256), BF16),
     wfo=((4, 2, 2, 128, 256), BF16),
+    st_h=((9, 32, 512), BF16),
+    st_m=((9, 32, 512), BF16),
 )
 
 
@@ -717,7 +748,7 @@
     return acc
 
 
-def conv_weight(a3, d3, out, n_img):
+def conv_weight(a3, d3, out, n_img, first, last):
     depth = (5 * n_img - 1) * 80
 
     def body(tap, carry):
@@ -727,7 +758,7 @@
         out[tap] = dot_first(left, d3[pl.ds(80, depth), 256:512]).astype(BF16).reshape(out.shape[1:])
         return carry
 
-    lax.fori_loop(0, 9, body, 0)
+    lax.fori_loop(first, last, body, 0)
 
 
 def body(names, *refs):
@@ -766,26 +797,96 @@
     def px_of(rr, yy, cc):
         return pl.multiple_of(320 * (2 * yy + cc) + 160 * rr, 16)
 
-    near0 = [
-        ln.near(s.images, s.xall.at[pl.ds(my_rows, 160)]),
-        ln.near(s.first.at[:, pl.ds(half, 256)], s.wf.at[z, y, c]),
-        ln.near(s.middle.at[:, :, pl.ds(half, 256)], s.wm.at[:, z, y, c]),
-        ln.near(s.last.at[:, pl.ds(pl.multiple_of(1024 * r, 128), 1024)], s.wl.at[z, y, c]),
-        ln.near(s.classes, s.wc.at[b]),
+    ends = (z == 0) | (z == 3)
+    inner = jnp.logical_not(ends)
+    not_first, not_last = z != 0, z != 3
+    far_end = dev(jnp.where(z == 1, 0, 3), y, c, r)
+    odd = c == r
+
+    def both(p, q):
+        return q if p is None else (p if q is None else p & q)
+
+    def line_start(src, at, when=None):
+        got = {q: ln.push(src, at(z), dev(zk(q), y, c, r), when) for q in (1, 3)}
+        got[2] = ln.push(src, at(z), dev(zk(2), y, c, r), both(when, ends))
+        return got, [ln.push(src, at(z), ypeer, when)]
+
+    def line_relay(state, at, when=None):
+        got, ys = state
+        wait([got[1], got[3]], when)
+        got[0] = ln.push(at(3 - z), at(3 - z), far_end, both(when, inner))
+        ys.append(ln.push(at(zk(3)), at(zk(3)), ypeer, when))
+        ys.append(ln.push(at(zk(1)), at(zk(1)), ypeer, when))
+
+    def line_last(state, at, col, when=None):
+        got, ys = state
+        wait([got[2]], both(when, inner))
+        wait([got[0]], both(when, ends))
+        ys.append(ln.push(at(zk(2)), at(zk(2)), ypeer, when))
+        return [ln.push(col(y), col(y), core, when)]
+
+    def line_core(state, col, cores, when=None):
+        wait(state[1], when)
+        cores.append(ln.push(col(1 - y), col(1 - y), core, when))
+
+    def at_wf(zz):
+        return s.wf.at[zz, y, c]
+
+    def at_wm(zz):
+        return s.wm.at[:, zz, y, c]
+
+    def at_wl(zz):
+        return s.wl.at[zz, y, c]
+
+    def at_wr(zz):
+        return s.wr.at[zz, y]
+
+    def col_wf(yy):
+        return s.wf.at[:, yy, c]
+
+    def col_wm(yy):
+        return s.wm.at[:, :, yy, c]
+
+    def col_wl(yy):
+        return s.wl.at[:, yy, c]
+
+    def col_wr(yy):
+        return s.wr.at[:, yy]
+
+    near_last = [
+        ln.near(s.last.at[:, pl.ds(pl.multiple_of((2 * i + r) * 128, 128), 128)], s.wl.at[z, y, c, :, 128 * i : 128 * i + 128])
+        for i in range(8)
+    ]
+    near_own = ln.near(s.images, s.xall.at[pl.ds(my_rows, 160)])
+    near_cls = ln.near(s.classes, s.wcv)
+    near_wf = ln.near(s.first.at[:, pl.ds(half, 256)], s.wf.at[z, y, c])
+    near_wm = ln.near(s.middle.at[:, :, pl.ds(half, 256)], s.wm.at[:, z, y, c])
+    red_local = pltpu.make_async_copy(s.reduce, s.wr.at[z, y], s.near_sems.at[NEAR - 1])
+    pl.when(odd)(red_local.start)
+    near_late = [
         ln.near(s.dcot, s.dcotv),
-        ln.near(s.ccot, s.ccotv),
+        ln.near(s.ccot, s.cct),
         ln.near(s.heads.at[y, :, :, pl.ds(fhalf, 256)], s.wh.at[:, z, y, c]),
         ln.near(s.messages.at[y, :, :, pl.ds(fhalf, 256)], s.wq.at[:, z, y, c]),
         ln.near(s.gates.at[r, :, pl.ds(fhalf, 256)], s.wg.at[z, y, c]),
     ]
-    owner = lax.div(z, np.int32(2)) == r
-    zl = lax.rem(z, np.int32(2))
-    red_local = pltpu.make_async_copy(s.reduce, s.wr.at[zl, y, c], s.near_sems.at[SEMS - 1])
-    pl.when(owner)(red_local.start)
-
-    wf_z = [ln.push(s.first.at[:, pl.ds(half, 256)], s.wf.at[z, y, c], dev(zk(k), y, c, r)) for k in (1, 2, 3)]
+    barrier = pltpu.get_barrier_semaphore()
+    friends = [
+        dev(zk(q), 1 - y if j else y, 1 - c if i else c, r) for q in range(4) for j in range(2) for i in range(2) if q + j + i
+    ] + [dev(z, 1 - y if j else y, 1 - c if i else c, 1 - r) for j in range(2) for i in range(2)]
+    for friend in friends:
+        pl.semaphore_signal(barrier, inc=1, device_id=friend, device_id_type=MESH)
+    pl.semaphore_wait(barrier, len(friends))
+
+    go_wf = line_start(s.first.at[:, pl.ds(half, 256)], at_wf)
     img_x = ln.push(s.images, s.xall.at[pl.ds(my_rows, 160)], xpeer)
-    wm_z = [ln.push(s.middle.at[:, :, pl.ds(half, 256)], s.wm.at[:, z, y, c], dev(zk(k), y, c, r)) for k in (1, 2, 3)]
+    go_wm = line_start(s.middle.at[:, :, pl.ds(half, 256)], at_wm)
+    for cp in near_last:
+        cp.wait()
+    got_wl = {q: ln.push(at_wl(z), at_wl(z), dev(zk(q), y, c, r)) for q in (1, 3)}
+    got_wl[2] = ln.push(at_wl(z), at_wl(z), dev(zk(2), y, c, r), ends)
+    got_wr = {q: ln.push(s.reduce, at_wr(z), dev(zk(q), y, c, r), odd) for q in (1, 3)}
+    got_wr[2] = ln.push(s.reduce, at_wr(z), dev(zk(2), y, c, r), odd & ends)
 
     for i in range(4):
         high, wide = s.crop_h[4 * z + i], s.crop_w[4 * z + i]
@@ -802,70 +903,85 @@
     def mask_at(base, rows, width):
         return lanes(s.maskp[pl.ds(mine + base, rows), :], width)
 
-    for cp in near0:
-        cp.wait()
-    pl.when(owner)(red_local.wait)
-    wait(wf_z)
-    wf_y = ln.push(s.wf.at[:, y, c], s.wf.at[:, y, c], ypeer)
-    wf_c0 = ln.push(s.wf.at[:, y, c], s.wf.at[:, y, c], core)
-    lastl = pl.ds(pl.multiple_of(1024 * r, 128), 1024)
-    wl_z = [ln.push(s.last.at[:, lastl], s.wl.at[z, y, c], dev(zk(k), y, c, r)) for k in (1, 2, 3)]
-    wr_z = [ln.push(s.reduce, s.wr.at[zl, y, c], dev(zk(k), y, c, r), owner) for k in (1, 2, 3)]
-    wait([wf_y])
-    wf_c1 = ln.push(s.wf.at[:, 1 - y, c], s.wf.at[:, 1 - y, c], core)
+    near_cls.wait()
+    s.wcs[...] = jnp.zeros(s.wcs.shape, BF16)
+    s.wcs[:, 0:40] = s.wcv[...]
+    s.wc[b] = s.wcs[...]
+    near_own.wait()
+    near_wf.wait()
+    line_relay(go_wf, at_wf)
+    cores_wf = line_last(go_wf, at_wf, col_wf)
+    near_wm.wait()
+    line_relay(go_wm, at_wm)
+    line_core(go_wf, col_wf, cores_wf)
     wait([img_x])
 
     def mask_x(base):
-        s.xall[pl.ds(base, 80), :] = (s.xall[pl.ds(base, 80), :].astype(F32) * mask_at(base, 80, 2048)).astype(BF16)
+        rows = pl.ds(base, 80)
+        v = (s.xall[rows, :].astype(F32) * mask_at(base, 80, 2048)).astype(BF16)
+        s.xall[rows, :] = v
+        for i in range(8):
+            pick = jnp.where(r == 0, v[:, 256 * i : 256 * i + 128].astype(F32), v[:, 256 * i + 128 : 256 * i + 256].astype(F32))
+            s.xh[rows, 128 * i : 128 * i + 128] = pick.astype(BF16)
 
     rows_loop(320, 80, mask_x)
-    wait(wm_z)
-    wm_y = ln.push(s.wm.at[:, :, y, c], s.wm.at[:, :, y, c], ypeer)
-    wm_c0 = ln.push(s.wm.at[:, :, y, c], s.wm.at[:, :, y, c], core)
-    wait([wf_c0, wf_c1])
-
-    def task_push(src, dst):
-        out = {}
-        for k in range(4):
-            for j in range(2):
-                for i in range(2):
-                    if k + j + i == 0:
-                        continue
-                    yy = 1 - y if j else y
-                    cc = 1 - c if i else c
-                    out[k, j, i] = ln.push(
-                        src.at[yy, :, :, pl.ds(pl.multiple_of(256 * cc, 128), 256)],
-                        dst.at[:, z, y, c],
-                        dev(zk(k) if k else z, yy, cc, r),
-                        mid_or_end(k),
-                    )
-        return out
-
-    ends = (z == 0) | (z == 3)
-
-    def mid_or_end(k):
-        return ends if k == 2 else None
-
-    def task_relay(got, dst):
-        wait([got[k, j, i] for k in (0, 1, 3) for j in range(2) for i in range(2) if k + j + i])
-        inner = jnp.logical_not(ends)
-        wait([got[2, j, i] for j in range(2) for i in range(2)], inner)
-        source = 3 - z
-        target = jnp.where(z == 1, 0, 3)
-        hand = ln.push(dst.at[:, source], dst.at[:, source], dev(target, y, c, r), inner)
-        return hand
-
-    def reduce_all(n, out):
-        m, sm, t, ar, az = (getattr(s, p + str(n)) for p in ("am", "as", "at", "ar", "az"))
-        one = []
+    wait(cores_wf)
+
+    def task_push(src, dst, lo, hi, staged):
+        yy = 1 - y if staged else y
+        got = {}
+        for q in (1, 3, 2, 0):
+            def like(q=q):
+                return dst.at[lo:hi, 0, 0] if q else dst.at[lo:hi, 0, 0, 0]
+
+            when = ends if q == 2 else None
+            got[q] = ln.group(like, when)
+            for i in range(2):
+                if q + i == 0:
+                    continue
+                cc = 1 - c if i else c
+                got[q].push(
+                    src.at[lo:hi, :, pl.ds(pl.multiple_of(256 * cc, 128), 256)],
+                    dst.at[lo:hi, z, yy, c],
+                    dev(zk(q) if q else z, y, cc, r),
+                    when,
+                )
+        return got, lo, hi, yy
+
+    def task_relay(state, dst):
+        got, lo, hi, yy = state
+        wait([got[0], got[1], got[3]])
+        hand = ln.push(dst.at[lo:hi, 3 - z, yy], dst.at[lo:hi, 3 - z, yy], far_end, inner)
+        return got, hand
+
+    def task_ready(state):
+        got, hand = state
+        wait([got[2]], inner)
+        wait([hand], ends)
+
+    def plane_start(n):
+        m, ar = (getattr(s, p + str(n)) for p in ("am", "ar"))
+        one = ln.group(lambda: ar)
         for i in (1, 2, 3):
             yy = 1 - y if i & 2 else y
             cc = 1 - c if i & 1 else c
-            one.append(ln.push(m, ar.at[i - 1], dev(z, yy, cc, r)))
-        wait(one)
+            one.push(m, ar.at[i - 1], dev(z, yy, cc, r))
+        return one
+
+    def plane_end(n, one):
+        m, sm, ar = (getattr(s, p + str(n)) for p in ("am", "as", "ar"))
+        wait([one])
         sm[...] = (m[...] + ar[0]) + (ar[1] + ar[2])
-        two = [ln.push(sm, az.at[k - 1], dev(zk(k), y, c, r)) for k in (1, 2, 3)]
-        wait(two)
+
+    def reduce_plane(n):
+        plane_end(n, plane_start(n))
+
+    def reduce_line(n):
+        sm, t, az = (getattr(s, p + str(n)) for p in ("as", "at", "az"))
+        two = ln.group(lambda: az)
+        for q in (1, 2, 3):
+            two.push(sm, az.at[q - 1], dev(zk(q), y, c, r))
+        wait([two])
         t[...] = (sm[...] + az[0]) + (az[1] + az[2])
         return t[...]
 
@@ -877,7 +993,7 @@
         return sums, squares
 
     def norm_terms(n, bnp, width):
-        t = reduce_all(n, None)
+        t = reduce_line(n)
         if width == 256:
             rows = [t[i : i + 1] for i in range(4)]
         else:
@@ -886,26 +1002,58 @@
         inv = lax.rsqrt(rows[1] / count - mean * mean + EPS)
         bnp[0:1], bnp[1:2], bnp[2:3], bnp[3:4] = mean, inv, rows[2], rows[3]
 
-    def put_stats(n, first, second, width, template):
+    quarter = lax.div(b, np.int32(4))
+    spot = 32 * lax.rem(b, np.int32(4))
+
+    def placed(n):
+        lane = lax.broadcasted_iota(jnp.int32, (8, 128), 1)
+        out = []
+        for p in range(2):
+            if n < 2:
+                v = jnp.broadcast_to(s.gains[0:1, :], (8, 128))
+                v = pltpu.roll(v, lax.rem(spot + 128 - 32 * (2 * n + p), np.int32(128)), 1)
+                v = jnp.where((lane >= spot) & (lane < spot + 32), v, 0.0)
+                out.append(jnp.concatenate([jnp.where(quarter == 2 * r + i, v[0:1], 0.0) for i in range(2)], axis=1))
+            else:
+                v = s.gains[1 + p : 2 + p, :]
+                out.append(
+                    [
+                        jnp.concatenate(
+                            [jnp.where(odd & (lax.div(b, np.int32(2)) == 4 * h + i), v, 0.0) for i in range(4)], axis=1
+                        )
+                        for h in range(2)
+                    ]
+                )
+        return out
+
+    def put_stats(n, first, second, width, layer):
         m = getattr(s, "am%d" % n)
-        if template is None:
-            m[...] = jnp.zeros(m.shape, F32)
-        else:
-            m[...] = template[...]
+        m[...] = jnp.zeros(m.shape, F32)
         if width == 256:
             m[0:1], m[1:2] = first, second
+            if layer is not None:
+                m[2:3], m[3:4] = placed(layer)
         else:
             m[0:1], m[1:2] = first[:, :512], first[:, 512:]
             m[2:3], m[3:4] = second[:, :512], second[:, 512:]
+            if layer is not None:
+                gain, shift = placed(layer)
+                m[4:5], m[5:6] = gain
+                m[6:7], m[7:8] = shift
 
     pre = dot(s.xall[...], s.wf[...].reshape(2048, 256))
     s.pre1[...] = pre
     first_sum, first_sq = stats_of(pre, 256, None)
-    put_stats(0, first_sum, first_sq, 256, s.st1)
-    wait([wm_y])
-    wm_c1 = ln.push(s.wm.at[:, :, 1 - y, c], s.wm.at[:, :, 1 - y, c], core)
+    put_stats(0, first_sum, first_sq, 256, 0)
+    cores_wm = line_last(go_wm, at_wm, col_wm)
+    reduce_plane(0)
+    go_wl = (got_wl, [ln.push(at_wl(z), at_wl(z), ypeer)])
+    go_wr = (got_wr, [ln.push(s.reduce, at_wr(z), ypeer, odd)])
+    pl.when(odd)(red_local.wait)
+    line_relay(go_wl, at_wl)
+    line_relay(go_wr, at_wr, odd)
     norm_terms(0, s.bnp1, 256)
-    heads_got = task_push(s.heads, s.wh)
+    heads_a = task_push(s.heads.at[y], s.wh, 0, 4, False)
 
     def act_from(prebuf, bnp, dst):
         def step(base):
@@ -916,61 +1064,69 @@
 
     act_from(s.pre1, s.bnp1, s.a1)
     a1_x = ln.push(s.a1.at[:, pl.ds(half, 256)], s.a1.at[:, pl.ds(half, 256)], xpeer)
-    wait(wl_z)
-    wl_y = ln.push(s.wl.at[:, y, c], s.wl.at[:, y, c], ypeer)
-    wl_c0 = ln.push(s.wl.at[:, y, c], s.wl.at[:, y, c], core)
-    wait([wm_c0, wm_c1])
+    line_core(go_wm, col_wm, cores_wm)
+    cores_wl = line_last(go_wl, at_wl, col_wl)
+    cores_wr = line_last(go_wr, at_wr, col_wr, odd)
+    wait(cores_wm)
     wait([a1_x])
     spread(s.a1, s.a3, 1, 512)
     pre = conv_rows(s.a3, s.wm, 0)
     s.pre2[...] = pre
     first_sum, first_sq = stats_of(pre, 256, None)
-    put_stats(1, first_sum, first_sq, 256, s.st2)
+    put_stats(1, first_sum, first_sq, 256, 1)
+    reduce_plane(1)
+    over_h = ln.push(s.heads.at[1 - y], s.st_h, ypeer)
     norm_terms(1, s.bnp2, 256)
+    relay_a = task_relay(heads_a, s.wh)
+    heads_b = task_push(s.heads.at[y], s.wh, 4, 8, False)
     act_from(s.pre2, s.bnp2, s.a2)
     a2_x = ln.push(s.a2.at[:, pl.ds(half, 256)], s.a2.at[:, pl.ds(half, 256)], xpeer)
-    wait([wr_z[0]], lax.div(zk(3), np.int32(2)) == r)
-    wait([wr_z[1]], lax.div(zk(2), np.int32(2)) == r)
-    wait([wr_z[2]], lax.div(zk(1), np.int32(2)) == r)
-    wr_y = ln.push(s.wr.at[:, y, c], s.wr.at[:, y, c], ypeer)
-    wr_c0 = ln.push(s.wr.at[:, y, c], s.wr.at[:, y, c], core)
-    wait([wl_y])
-    wl_c1 = ln.push(s.wl.at[:, 1 - y, c], s.wl.at[:, 1 - y, c], core)
-    wait([wl_c0, wl_c1, a2_x])
+    line_core(go_wl, col_wl, cores_wl)
+    line_core(go_wr, col_wr, cores_wr, odd)
+    wait(cores_wl)
+    wait([a2_x])
     pre = dot(s.a2[...], s.wl[...].reshape(512, 1024))
     s.pre3[...] = pre
     first_sum, first_sq = stats_of(pre, 1024, None)
-    put_stats(2, first_sum, first_sq, 1024, s.st3)
+    put_stats(2, first_sum, first_sq, 1024, 2)
+    reduce_plane(2)
+    over_m = ln.push(s.messages.at[1 - y], s.st_m, ypeer)
     norm_terms(2, s.bnp3, 1024)
-    mess_got = task_push(s.messages, s.wq)
+    relay_b = task_relay(heads_b, s.wh)
+    heads_c = task_push(s.heads.at[y], s.wh, 8, 9, False)
+    wait([over_h])
+    staged_h = ln.near(s.st_h.at[:, :, pl.ds(fhalf, 256)], s.wh.at[:, z, 1 - y, c])
+    heads_d = task_push(s.st_h, s.wh, 0, 5, True)
+    heads_e = task_push(s.st_h, s.wh, 5, 9, True)
     gate_got = {}
-    cls_got = {}
-    for k in range(4):
+    cls_got = ln.group(lambda: s.wc.at[0:15])
+    for q in range(4):
         for j in range(2):
+            if q + j:
+                gate_got[q, j] = ln.group(lambda: s.wg.at[0, 0], (y == r) if j == 0 else (y != r))
             for i in range(2):
-                if k + j + i == 0:
+                if q + j + i == 0:
                     continue
                 yy = 1 - y if j else y
                 cc = 1 - c if i else c
-                to = dev(zk(k) if k else z, yy, cc, r)
-                gate_got[k, j, i] = ln.push(
-                    s.gates.at[r, :, pl.ds(pl.multiple_of(256 * cc, 128), 256)], s.wg.at[z, y, c], to, yy == r
-                )
-                cls_got[k, j, i] = ln.push(s.classes, s.wc.at[b], to)
-    xhalf = pl.ds(pl.multiple_of(1024 * r, 128), 1024)
+                to = dev(zk(q) if q else z, yy, cc, r)
+                cls_got.push(s.wcs, s.wc.at[b], to)
+                src = s.gates.at[r, :, pl.ds(pl.multiple_of(256 * cc, 128), 256)]
+                if q + j:
+                    gate_got[q, j].push(src, s.wg.at[z, y, c], to, (y == r) if j == 0 else (y != r))
+                else:
+                    gate_got[0, 0] = ln.push(src, s.wg.at[z, y, c], to, y == r)
 
     def summed_at(base, rows):
         x = (s.pre3[pl.ds(base, rows), :] - s.bnp3[0:1]) * s.bnp3[1:2]
-        return x, x * s.bnp3[2:3] + s.bnp3[3:4] + s.xall[pl.ds(base, rows), xhalf].astype(F32)
+        return x, x * s.bnp3[2:3] + s.bnp3[3:4] + s.xh[pl.ds(base, rows), :].astype(F32)
 
     def block_step(base):
         _, v = summed_at(base, 32)
         s.blk[pl.ds(base, 32), :] = (gelu_of(v) * mask_at(base, 32, 1024)).astype(BF16)
 
     rows_loop(320, 32, block_step)
-    wait([wr_y])
-    wr_c1 = ln.push(s.wr.at[:, 1 - y, c], s.wr.at[:, 1 - y, c], core)
-    wait([wr_c0, wr_c1])
+    wait(cores_wr, jnp.logical_not(odd))
     wred = s.wr[...].reshape(1024, 512)
     s.rps[...] = dot(s.blk[pl.ds(other_rows, 160), :], wred).astype(BF16)
     red_x = ln.push(s.rps, s.rpr, xpeer)
@@ -981,10 +1137,13 @@
     def block_of(rr, yy, cc, lo=0, n=160):
         return s.rbuf.at[pl.ds(pl.multiple_of(px_of(rr, yy, cc) + lo, 16), n)]
 
+    for cp in near_late:
+        cp.wait()
     own = block_of(r, y, c)
     g_x = ln.push(own, own, xpeer)
     g_y = ln.push(own, own, ypeer)
     g_c = ln.push(own, own, core)
+    relay_c = task_relay(heads_c, s.wh)
     wait([g_x])
     bx = block_of(1 - r, y, c, 0, 80)
     g_xy = ln.push(bx, bx, ypeer)
@@ -998,12 +1157,64 @@
     wait([g_xy, g_yx])
     bd = block_of(1 - r, 1 - y, c)
     g_c3 = ln.push(bd, bd, core)
-    heads_hand = task_relay(heads_got, s.wh)
-    wait([heads_hand], ends)
+    relay_d = task_relay(heads_d, s.wh)
+    wfo_x = ln.push(s.wf, s.wfo, xpeer)
     wait([g_c, g_c1, g_c2, g_c3])
+
+    near_end = dev(jnp.where(z == 0, 1, 2), y, c, r)
+    other_end = dev(jnp.where(z == 1, 3, 0), y, c, r)
+
+    def grad_push(n, g, rm, lo, hi):
+        def like(slot):
+            return lambda side: rm.at[slot, lo:hi] if side else g.at[lo:hi, 0]
+
+        got = {}
+        for q in (1, 2, 3):
+            direct = {1: not_last, 2: ends, 3: not_first}[q]
+            got[q] = ln.push(g.at[lo:hi, zk(q)], rm.at[q - 1, lo:hi], dev(zk(q), y, c, r), direct, like(q - 1))
+        hop = s.hop.at[n, lo:hi]
+        got[0] = ln.push(
+            g.at[lo:hi, 3 - z], hop, near_end, ends, lambda side: s.hop.at[n, lo:hi] if side else g.at[lo:hi, 0]
+        )
+        return got, n, g, rm, lo, hi
+
+    def grad_hop(state):
+        got, n, g, rm, lo, hi = state
+
+        def add():
+            got[0].wait_recv()
+            far = jnp.where(z == 1, 3, 0)
+            for t in range(lo, hi):
+                s.hop[n, t] = (s.hop[n, t].astype(F32) + g[t, far].astype(F32)).astype(BF16)
+
+        pl.when(inner)(add)
+        got[4] = ln.push(
+            s.hop.at[n, lo:hi], rm.at[1, lo:hi], other_end, inner,
+            lambda side: rm.at[1, lo:hi] if side else s.hop.at[n, lo:hi],
+        )
+
+    def grad_wait(state):
+        got = state[0]
+        wait([got[1]], not_first)
+        wait([got[3]], not_last)
+        wait([got[2]], inner)
+        wait([got[4]], ends)
 
     def tasks(r3, f3, d3, preh, dfull):
         spread(s.rbuf, r3, 4, 512)
+        relay_e = task_relay(heads_e, s.wh)
+        wait([over_m])
+        staged_m = ln.near(s.st_m.at[:, :, pl.ds(fhalf, 256)], s.wq.at[:, z, 1 - y, c])
+
+        def mess_push(a):
+            return [
+                task_push(s.st_m if staged else s.messages.at[y], s.wq, 3 * a, 3 * a + 3, staged) for staged in (False, True)
+            ]
+
+        mess = [mess_push(0), mess_push(1)]
+        for part in (relay_a, relay_b, relay_c, relay_d, relay_e):
+            task_ready(part)
+        staged_h.wait()
 
         def head_step(i, carry):
             v = conv_rows(r3, s.wh, i)
@@ -1020,6 +1231,9 @@
         rows_loop(1280, 80, feat_step)
         f_c = ln.push(s.fown, s.ffull.at[:, pl.ds(fhalf, 256)], core)
         f_n = ln.near(s.fown, s.ffull.at[:, pl.ds(fhalf, 256)])
+
+        def seven():
+            return s.dmg.at[0:1120]
 
         def to_owners(src, dst_of, when):
             got = {}
@@ -1030,7 +1244,7 @@
                 )
             return got
 
-        f_own = to_owners(s.fown, lambda: s.frecv.at[r], special)
+        f_own = to_owners(s.fown, lambda: s.fg.at[r, 0], special)
 
         def keep(dst, src):
             def run():
@@ -1038,12 +1252,12 @@
 
             return run
 
-        pl.when(special)(keep(s.frecv.at[r], s.fown))
+        pl.when(special)(keep(s.fg.at[r, 0], s.fown))
         f_n.wait()
         wait([f_c])
 
         def gate_ready():
-            for key, cp in gate_got.items():
+            for cp in gate_got.values():
                 cp.wait_recv()
 
         pl.when(special)(gate_ready)
@@ -1056,36 +1270,62 @@
 
             rows_loop(1280, 320, gate_step)
 
-        g_own = to_owners(s.gateb, lambda: s.grecv.at[r], special)
-        pl.when(special)(keep(s.grecv.at[r], s.gateb))
+        g_own = to_owners(s.gateb, lambda: s.fg.at[r, 1], special)
+        pl.when(special)(keep(s.fg.at[r, 1], s.gateb))
         spread(s.ffull, f3, 4, 512)
-        mess_hand = task_relay(mess_got, s.wq)
-        wait([mess_hand], ends)
-
-        def mess_step(i, carry):
-            px = pl.multiple_of(i * 320, 16)
-            s.msgb[pl.ds(px, 320), :] = conv_rows(f3, s.wq, i).astype(BF16)
-            return carry
-
-        lax.fori_loop(0, 4, mess_step, 0)
-        m_own = to_owners(s.msgb, lambda: s.mrecv.at[task], None)
+        relayed = [[task_relay(p, s.wq) for p in mess[0]]]
+        mess.append(mess_push(2))
+        relayed.append([task_relay(p, s.wq) for p in mess[1]])
+        staged_m.wait()
+        for a in range(3):
+            for p in relayed[a]:
+                task_ready(p)
+            if a == 0:
+                relayed.append(None)
+
+            def mess_step(i, carry, a=a):
+                rows = pl.ds(pl.multiple_of(i * 320, 16), 320)
+                base = pl.multiple_of((5 * i + a) * 80, 16)
+                v = dot(f3[pl.ds(base, 320), :], s.wq[3 * a : 3 * a + 3].reshape(1536, 256))
+                if a:
+                    v = dfull[rows, 0:256] + v
+                if a < 2:
+                    dfull[rows, 0:256] = v
+                else:
+                    s.msgb[rows, :] = v.astype(BF16)
+                return carry
+
+            lax.fori_loop(0, 4, mess_step, 0)
+            if a == 0:
+                relayed[2] = [task_relay(p, s.wq) for p in mess[2]]
+
+        m_own = ln.group(seven)
+        for o in offsets:
+            rr, yy, cc = peer(*o)
+            m_own.push(s.msgb.at[pl.ds(px_of(rr, yy, cc), 160)], s.mrecv.at[task, :, pl.ds(fhalf, 256)], dev(z, yy, cc, rr))
         keep(s.mrecv.at[task], s.msgb)()
 
-        for key, cp in cls_got.items():
-            cp.wait_recv()
+        wait([cls_got])
+        for i in range(2):
+            s.ctf[...] = jnp.zeros((128, 128), F32)
+            s.ctf[0:40, 0:80] = s.cct[i].astype(F32)
+            turned = s.ctf[...].T
+            s.ccotv[80 * i : 80 * i + 80, :] = turned[0:80, :].astype(BF16)
         for o in offsets:
             wait([f_own[o], g_own[o]], (r != y) if (o[0] + o[1]) % 2 else special)
-            wait([m_own[o]])
+
+        wait([m_own])
 
         def stream_step(base):
             rows = pl.ds(base, 32)
             m = lanes(s.maskp[pl.ds(own_px + base, 32), :], 512)
             m0, m1, m2, m3 = (s.mrecv[t, rows, :].astype(F32) for t in range(4))
+            f0, f3_ = s.fg[0, 0, rows, :].astype(F32), s.fg[1, 0, rows, :].astype(F32)
             mid = m1 + m2
             sd, sc = mid + m3, m0 + mid
-            gd, gc = s.grecv[0, rows, :].astype(F32), s.grecv[1, rows, :].astype(F32)
-            s.ods[rows, :] = ((s.frecv[0, rows, :].astype(F32) + gd * sd) * m).astype(BF16)
-            merged = (s.frecv[1, rows, :].astype(F32) + gc * sc).astype(BF16)
+            gd, gc = s.fg[0, 1, rows, :].astype(F32), s.fg[1, 1, rows, :].astype(F32)
+            s.ods[rows, :] = ((f0 + gd * sd) * m).astype(BF16)
+            merged = (f3_ + gc * sc).astype(BF16)
             s.mrg[rows, :] = merged
             m1l = m[:, :128]
             wcls = s.wc[...].reshape(512, 128)
@@ -1094,57 +1334,64 @@
             s.ccotv[rows, :] = dj
             dd = s.dcotv[rows, :].astype(F32) * m
             dmer = dot_last(dj, wcls)
-            s.ex[0, 0, rows, :] = dd.astype(BF16)
-            s.ex[1, 0, rows, :] = dmer.astype(BF16)
-            s.ex[0, 1, rows, :] = (dd * sd * gd * (1.0 - gd)).astype(BF16)
-            s.ex[1, 1, rows, :] = (dmer * sc * gc * (1.0 - gc)).astype(BF16)
+            s.fg[0, 0, rows, :] = dd.astype(BF16)
+            s.fg[1, 0, rows, :] = dmer.astype(BF16)
+            s.fg[0, 1, rows, :] = (dd * sd * gd * (1.0 - gd)).astype(BF16)
+            s.fg[1, 1, rows, :] = (dmer * sc * gc * (1.0 - gc)).astype(BF16)
             down, up = dd * gd, dmer * gc
             both = (down + up).astype(BF16)
-            s.dm[0, rows, :] = up.astype(BF16)
-            s.dm[1, rows, :] = both
-            s.dm[2, rows, :] = both
-            s.dm[3, rows, :] = down.astype(BF16)
+            s.mrecv[0, rows, :] = up.astype(BF16)
+            s.mrecv[1, rows, :] = both
+            s.mrecv[2, rows, :] = both
+            s.mrecv[3, rows, :] = down.astype(BF16)
 
         rows_loop(160, 32, stream_step)
-        d_got = {}
         e_got = {}
-        for o in offsets:
-            rr, yy, cc = peer(*o)
-            tt = 2 * rr + yy
-            ll = pl.ds(pl.multiple_of(256 * cc, 128), 256)
-            d_got[o] = ln.push(s.dm.at[tt, :, ll], s.dmg.at[pl.ds(own_px, 160)], dev(z, yy, cc, rr))
+        d_got = ln.group(seven)
         for o in offsets:
             rr, yy, cc = peer(*o)
             ll = pl.ds(pl.multiple_of(256 * cc, 128), 256)
-            e_got[o] = ln.push(s.ex.at[rr, :, :, ll], s.exg.at[:, pl.ds(own_px, 160)], dev(z, yy, cc, rr), rr == yy)
-        s.dmg[pl.ds(own_px, 160), :] = s.dm[task, :, pl.ds(fhalf, 256)]
+            d_got.push(s.mrecv.at[2 * rr + yy, :, ll], s.dmg.at[pl.ds(own_px, 160)], dev(z, yy, cc, rr))
+        for o in offsets:
+            rr, yy, cc = peer(*o)
+            ll = pl.ds(pl.multiple_of(256 * cc, 128), 256)
+            e_got[o] = ln.push(s.fg.at[rr, :, :, ll], s.exg.at[:, pl.ds(own_px, 160)], dev(z, yy, cc, rr), rr == yy)
+        s.dmg[pl.ds(own_px, 160), :] = s.mrecv[task, :, pl.ds(fhalf, 256)]
 
         @pl.when(special)
         def _():
             for e in range(2):
-                s.exg[e, pl.ds(own_px, 160), :] = s.ex[r, e, :, pl.ds(fhalf, 256)]
+                s.exg[e, pl.ds(own_px, 160), :] = s.fg[r, e, :, pl.ds(fhalf, 256)]
 
         @pl.when(jnp.logical_not(special))
         def _():
             s.exg[...] = jnp.zeros(s.exg.shape, BF16)
 
-        out_near = [ln.near(s.ods, s.o_depth), ln.near(s.olg, s.o_logits)]
+        for i in range(2):
+            s.ctf[...] = jnp.zeros((128, 128), F32)
+            s.ctf[0:80, :] = s.olg[80 * i : 80 * i + 80, :].astype(F32)
+            turned = s.ctf[...].T
+            s.olt[i] = turned[0:40, 0:80].astype(BF16)
+        out_near = [ln.near(s.ods, s.o_depth), ln.near(s.olt, s.o_logits)]
         s.gcls[...] = dot_first(s.mrg[...], s.ccotv[...]).astype(BF16).reshape(16, 32, 128)
-        cg = []
-        for k in range(4):
+        cg = ln.group(lambda: s.rcls)
+        n_cls = 0
+        for q in range(4):
             for j in range(2):
                 for i in range(2):
-                    if k + j + i == 0:
+                    if q + j + i == 0:
                         continue
                     yy = 1 - y if j else y
                     cc = 1 - c if i else c
-                    zz = zk(k) if k else z
-                    like = lambda side, n=len(cg): s.rcls.at[n] if side else s.gcls.at[0]
-                    cg.append(ln.push(s.gcls.at[4 * zz + 2 * yy + cc], s.rcls.at[len(cg)], dev(zz, yy, cc, r), None, like))
-        wait([d_got[o] for o in offsets])
+                    zz = zk(q) if q else z
+                    cg.push(s.gcls.at[4 * zz + 2 * yy + cc], s.rcls.at[n_cls], dev(zz, yy, cc, r))
+                    n_cls += 1
+        wait([d_got])
         spread(s.dmg, d3, 4, 256)
-        conv_weight(f3, d3, s.gm, 4)
-        gm_z = [ln.push(s.gm.at[:, zk(k)], s.rm.at[k - 1], dev(zk(k), y, c, r), None, lambda side, k=k: s.rm.at[k - 1] if side else s.gm.at[:, 0]) for k in (1, 2, 3)]
+        gm_z = []
+        for a in range(3):
+            conv_weight(f3, d3, s.gm, 4, 3 * a, 3 * a + 3)
+            gm_z.append(grad_push(0, s.gm, s.rm, 3 * a, 3 * a + 3))
         wait([e_got[o] for o in offsets], special)
 
         def back_step(i, carry):
@@ -1182,10 +1429,10 @@
             rows = pl.ds(base, 80)
             m = lanes(s.maskp[rows, :], 256)
             d = dfull[rows, pl.ds(fhalf, 256)] + s.dfr[rows, :].astype(F32) + s.exg[0, rows, :].astype(F32)
-            s.dfs2[rows, :] = (slope_of(preh[rows, :]) * d * m).astype(BF16)
+            s.dmg[rows, :] = (slope_of(preh[rows, :]) * d * m).astype(BF16)
 
         rows_loop(1280, 80, dhead_step)
-        spread(s.dfs2, d3, 4, 256)
+        spread(s.dmg, d3, 4, 256)
 
         def back_step2(i, carry):
             px = pl.multiple_of(i * 320, 16)
@@ -1197,28 +1444,28 @@
             src = pl.multiple_of(320 * (2 * yy) + 320 * (1 - c), 16)
             s.drs[pl.ds(320 * yy, 320), :] = dfull[pl.ds(src, 320), :].astype(BF16)
         dr_c = ln.push(s.drs, s.drr, core)
-        conv_weight(r3, d3, s.gh, 4)
-        gh_z = [ln.push(s.gh.at[:, zk(k)], s.rh.at[k - 1], dev(zk(k), y, c, r), None, lambda side, k=k: s.rh.at[k - 1] if side else s.gh.at[:, 0]) for k in (1, 2, 3)]
         wait([dr_c])
         for yy in range(2):
             src = pl.multiple_of(320 * (2 * yy) + 320 * c, 16)
             rows = pl.ds(320 * yy, 320)
-            s.drq[rows, :] = (dfull[pl.ds(src, 320), :] + s.drr[rows, :].astype(F32)).astype(BF16)
+            s.drr[rows, :] = (dfull[pl.ds(src, 320), :] + s.drr[rows, :].astype(F32)).astype(BF16)
         ro = []
         for dr, dy in ((1, 0), (0, 1), (1, 1)):
             rr, yy, _ = peer(dr, dy, 0)
-            src = s.drq.at[pl.ds(pl.multiple_of(320 * yy + 160 * rr, 16), 160)]
+            src = s.drr.at[pl.ds(pl.multiple_of(320 * yy + 160 * rr, 16), 160)]
             ro.append(ln.push(src, s.dro.at[len(ro)], dev(z, yy, c, rr)))
+        conv_weight(r3, d3, s.gh, 4, 0, 9)
+        grad_hop(gm_z[0])
         wait(ro)
         keep_rows = pl.ds(pl.multiple_of(320 * y + 160 * r, 16), 160)
-        total_red = s.drq[keep_rows, :].astype(F32)
+        total_red = s.drr[keep_rows, :].astype(F32)
         for i in range(3):
             total_red = total_red + s.dro[i].astype(F32)
         s.dred[pl.ds(my_rows, 160), :] = total_red.astype(BF16)
         for cp in out_near:
             cp.wait()
         ln.drain(scoped=True)
-        return cg, gm_z, gg_z, gh_z
+        return cg, gm_z, gg_z
 
     state = {}
 
@@ -1233,10 +1480,9 @@
         pltpu.VMEM((1280, 256), F32),
         pltpu.VMEM((1280, 512), F32),
     )
-    cg, gm_z, gg_z, gh_z = state["t"]
+    cg, gm_z, gg_z = state["t"]
 
     dr_x = ln.push(s.dred.at[pl.ds(my_rows, 160)], s.dred.at[pl.ds(my_rows, 160)], xpeer)
-    wfo_x = ln.push(s.wf, s.wfo, xpeer)
 
     def block_back(*late):
         for name, ref in zip(LATE, late):
@@ -1271,6 +1517,29 @@
         def add_z(ry, rz, fin, lead):
             mine_z = (ry[:, z] if lead else ry[z]).astype(F32)
             fin[...] = ((mine_z + rz[0].astype(F32)) + (rz[1].astype(F32) + rz[2].astype(F32))).astype(BF16)
+
+        def task_out(states, rm, g, ps, out):
+            for part in states:
+                grad_wait(part)
+            loads = [[ln.near(rm.at[q, 3 * part : 3 * part + 3], s.zst.at[part % 2, q]) for q in range(3)] for part in range(2)]
+            for part in range(3):
+                for cp in loads[part]:
+                    cp.wait()
+                v0 = s.zst.at[part % 2]
+                for t in range(3):
+                    first_in = jnp.where(z == 0, 0.0, v0[0, t].astype(F32))
+                    third_in = jnp.where(z == 3, 0.0, v0[2, t].astype(F32))
+                    v = g[3 * part + t, z].astype(F32) + first_in + (v0[1, t].astype(F32) + third_in)
+                    ps[3 * part + t] = v.astype(BF16)
+                if part == 0:
+                    loads.append([ln.near(rm.at[q, 6:9], s.zst.at[0, q]) for q in range(3)])
+            lanes_out = pl.ds(fhalf, 256)
+            sent = []
+            for i in (1, 2, 3):
+                yy = 1 - y if i & 2 else y
+                cc = 1 - c if i & 1 else c
+                sent.append(ln.push(ps.at[:, yy, cc], out.at[y, :, :, lanes_out], dev(z, yy, cc, r)))
+            return sent, ln.near(ps.at[:, y, c], out.at[y, :, :, lanes_out])
 
         wait([dr_x])
 
@@ -1287,10 +1556,15 @@
         nil = jnp.zeros((1, 1024), F32)
         su, sux = lax.fori_loop(0, 10, d3_step, (nil, nil))
         put_stats(3, su, sux, 1024, None)
+        ar3 = plane_start(3)
         ds_x = ln.push(s.dsum.at[pl.ds(other_rows, 160)], s.dsr, xpeer)
         gr[...] = dot_first(s.blk[...], s.dred[...]).astype(BF16).reshape(gr.shape)
-        gr_c = to_core(gr, s.rcr, False)
-        t = reduce_all(3, None)
+        gr_c = ln.push(gr, s.rcr, core, jnp.logical_not(odd))
+        plane_end(3, ar3)
+        t = reduce_line(3)
+        for part in gm_z[1:]:
+            grad_hop(part)
+        gh_z = [grad_push(1, s.gh, s.rh, 0, 2)]
         gs3 = ln.push(s.at3, s.o_gs3.at[r], xpeer)
         gs3n = ln.near(s.at3, s.o_gs3.at[r])
         mu = jnp.concatenate([t[0:1], t[1:2]], axis=1) / count
@@ -1313,12 +1587,29 @@
         pa2 = ln.push(s.pas2, s.par2, xpeer)
         gl[...] = dot_first(s.a2[...], s.dp3[...]).astype(BF16).reshape(gl.shape)
         gl_c = to_core(gl, s.rcl, False)
-        wait([gr_c])
-        add_core(gr, s.rcr, False)
-        gr_y = to_y(s.rcr, s.ryr, False)
+        wait([gr_c], odd)
+
+        @pl.when(odd)
+        def _():
+            for q in range(4):
+                s.rcr[q] = (s.rcr[q].astype(F32) + gr[q].astype(F32)).astype(BF16)
+
+        later = {}
+
+        def after_plane_two():
+            later["gr_y"] = ln.push(s.rcr.at[:, 1 - y], s.ryr, ypeer, odd)
+            wait([gl_c])
+            add_core(gl, s.rcl, False)
+            later["gl_y"] = to_y(s.rcl, s.ryl, False)
+
+        def after_plane_one():
+            wait([gq_c])
+            add_core(gq, s.rcm, True)
+            later["gq_y"] = to_y(s.rcm, s.rym, True)
+
         wait([pa2])
 
-        def norm_back(n, par, prebuf, bnp, dst, out_gs):
+        def norm_back(n, par, prebuf, bnp, dst, out_gs, middle, after):
             def u_step(i, carry):
                 su_, sux_ = carry
                 base = pl.multiple_of(i * 80, 16)
@@ -1333,7 +1624,10 @@
             nil_ = jnp.zeros((1, 256), F32)
             su_, sux_ = lax.fori_loop(0, 4, u_step, (nil_, nil_))
             put_stats(n, su_, sux_, 256, None)
-            t_ = reduce_all(n, None)
+            reduce_plane(n)
+            middle()
+            t_ = reduce_line(n)
+            after()
             gsx = ln.push(getattr(s, "at%d" % n), out_gs.at[r], xpeer)
             gsn = ln.near(getattr(s, "at%d" % n), out_gs.at[r])
             mu_, mux_ = t_[0:1] / count, t_[1:2] / count
@@ -1347,35 +1641,34 @@
             rows_loop(320, 80, d_step)
             return gsx, gsn
 
-        gs2, gs2n = norm_back(4, s.par2, s.pre2, s.bnp2, s.dp2, s.o_gs2)
+        gs2, gs2n = norm_back(4, s.par2, s.pre2, s.bnp2, s.dp2, s.o_gs2, after_plane_two, lambda: gh_z.append(grad_push(1, s.gh, s.rh, 2, 4)))
         spread(s.dp2, s.d3m, 1, 256)
         s.u3[:, 0:512] = conv_back(s.d3m, s.wm, 0)
         s.pas1[...] = s.u3[:, pl.ds(ohalf, 256)].astype(BF16)
         pa1 = ln.push(s.pas1, s.par1, xpeer)
-        conv_weight(s.a3, s.d3m, gq, 1)
+        conv_weight(s.a3, s.d3m, gq, 1, 0, 9)
         gq_c = to_core(gq, s.rcm, True)
-        wait([gl_c])
-        add_core(gl, s.rcl, False)
-        gl_y = to_y(s.rcl, s.ryl, False)
         wait([pa1])
-        gs1, gs1n = norm_back(5, s.par1, s.pre1, s.bnp1, s.dp1, s.o_gs1)
+        gs1, gs1n = norm_back(5, s.par1, s.pre1, s.bnp1, s.dp1, s.o_gs1, after_plane_one, lambda: gh_z.append(grad_push(1, s.gh, s.rh, 4, 9)))
         dp_x = ln.push(s.dp1.at[pl.ds(other_rows, 160)], s.dp1r, xpeer)
         gf[...] = dot_first(s.xall[...], s.dp1[...]).astype(BF16).reshape(gf.shape)
         gf_c = to_core(gf, s.rcf, False)
-        wait([gq_c])
-        add_core(gq, s.rcm, True)
-        gq_y = to_y(s.rcm, s.rym, True)
         wait([gf_c])
         add_core(gf, s.rcf, False)
         gf_y = to_y(s.rcf, s.ryf, False)
-
-        wait([gr_y])
-        add_y(s.rcr, s.ryr, False)
-        gr_z = [
-            ln.push(s.ryr.at[lax.rem(zk(k), np.int32(2))], s.rzr.at[k - 1], dev(zk(k), y, c, r),
-                    lax.div(zk(k), np.int32(2)) == r)
-            for k in (1, 2, 3)
-        ]
+        gr_y, gl_y, gq_y = later["gr_y"], later["gl_y"], later["gq_y"]
+        ms, mn = task_out(gm_z, s.rm, s.gm, s.psm, s.o_mess)
+
+        wait([gr_y], odd)
+
+        @pl.when(odd)
+        def _():
+            for q in range(4):
+                s.ryr[q] = (s.ryr[q].astype(F32) + s.rcr[q, y].astype(F32)).astype(BF16)
+
+        for part in gh_z[:2]:
+            grad_hop(part)
+        gr_z = [ln.push(s.ryr.at[zk(q)], s.rzr.at[q - 1], dev(zk(q), y, c, r), odd) for q in (1, 2, 3)]
         wait([gl_y])
         add_y(s.rcl, s.ryl, False)
         gl_z = to_z(s.ryl, s.rzl, False)
@@ -1401,33 +1694,21 @@
             def img_step(base):
                 rows = pl.ds(base, 32)
                 m = mask_at(my_rows + base, 32, 1024)
-                own_d = s.dsum[pl.ds(my_rows + base, 32), :].astype(F32)
-                far_d = s.dsr[rows, :].astype(F32)
-                d = jnp.where(r == q, own_d, far_d)
+                own_d = s.dsum[pl.ds(my_rows + base, 32), 512 * q : 512 * q + 512].astype(F32)
+                far_d = s.dsr[rows, 512 * q : 512 * q + 512].astype(F32)
+                d = jnp.concatenate(
+                    [
+                        jnp.where(r == j % 2, own_d[:, 64 * (j - j % 2) :][:, :128], far_d[:, 64 * (j - j % 2) :][:, :128])
+                        for j in range(8)
+                    ],
+                    axis=1,
+                )
                 s.oimg[rows, cols] = ((s.u3[rows, :] + d) * m).astype(BF16)
 
             rows_loop(160, 32, img_step)
         img_n = ln.near(s.oimg, s.o_img)
 
-        def task_out(got, rm, g, ps, out):
-            wait(got)
-            for part in range(3):
-                cps = [ln.near(rm.at[k, 3 * part : 3 * part + 3], s.zst.at[k]) for k in range(3)]
-                for cp in cps:
-                    cp.wait()
-                for t in range(3):
-                    v = g[3 * part + t, z].astype(F32) + s.zst[0, t].astype(F32)
-                    v = v + (s.zst[1, t].astype(F32) + s.zst[2, t].astype(F32))
-                    ps[3 * part + t] = v.astype(BF16)
-            lanes_out = pl.ds(fhalf, 256)
-            sent = []
-            for i in (1, 2, 3):
-                yy = 1 - y if i & 2 else y
-                cc = 1 - c if i & 1 else c
-                sent.append(ln.push(ps.at[:, yy, cc], out.at[y, :, :, lanes_out], dev(z, yy, cc, r)))
-            return sent, ln.near(ps.at[:, y, c], out.at[y, :, :, lanes_out])
-
-        ms, mn = task_out(gm_z, s.rm, s.gm, s.psm, s.o_mess)
+        grad_hop(gh_z[2])
         hs, hn = task_out(gh_z, s.rh, s.gh, s.psh, s.o_heads)
 
         @pl.when(special)
@@ -1442,31 +1723,31 @@
             rr, yy, cc = peer(*o)
             gx[o] = ln.push(s.pg.at[yy, cc], s.o_gates.at[r, :, pl.ds(fhalf, 256)], dev(z, yy, cc, rr), special)
         gate_near = pltpu.make_async_copy(
-            s.pg.at[y, c], s.o_gates.at[r, :, pl.ds(fhalf, 256)], s.near_sems.at[SEMS - 2]
+            s.pg.at[y, c], s.o_gates.at[r, :, pl.ds(fhalf, 256)], s.near_sems.at[NEAR - 2]
         )
         pl.when(special)(gate_near.start)
 
-        wait(cg)
+        wait([cg])
         v = s.gcls[b].astype(F32)
         for i in range(15):
             v = v + s.rcls[i].astype(F32)
         s.clss[...] = v
         cls_x = ln.push(s.clss, s.clsr, xpeer)
 
-        wait([gr_z[0], gr_z[1], gr_z[2]], owner)
-
-        @pl.when(owner)
+        wait(gr_z, odd)
+
+        @pl.when(odd)
         def _():
-            v_ = s.ryr[zl].astype(F32) + s.rzr[0].astype(F32)
+            v_ = s.ryr[z].astype(F32) + s.rzr[0].astype(F32)
             s.fnr[...] = (v_ + (s.rzr[1].astype(F32) + s.rzr[2].astype(F32))).astype(BF16)
 
-        gr_x = ln.push(s.fnr, s.o_red, xpeer, owner)
-        red_near = pltpu.make_async_copy(s.fnr, s.o_red, s.near_sems.at[SEMS - 3])
-        pl.when(owner)(red_near.start)
+        gr_x = ln.push(s.fnr, s.o_red, xpeer, odd)
+        red_near = pltpu.make_async_copy(s.fnr, s.o_red, s.near_sems.at[NEAR - 3])
+        pl.when(odd)(red_near.start)
         wait(gl_z)
         add_z(s.ryl, s.rzl, s.fnl, False)
-        gl_x = ln.push(s.fnl, s.o_last.at[:, lastl], xpeer)
-        n1 = ln.near(s.fnl, s.o_last.at[:, lastl])
+        gl_x = ln.push(s.fnl, s.o_last.at[r], xpeer)
+        n1 = ln.near(s.fnl, s.o_last.at[r])
         wait(gq_z)
         add_z(s.rym, s.rzm, s.fnm, True)
         gq_x = ln.push(s.fnm, s.o_mid.at[:, :, pl.ds(half, 256)], xpeer)
@@ -1478,13 +1759,13 @@
         wait([cls_x])
         s.clso[...] = s.clss[...] + s.clsr[...]
         n4 = ln.near(s.clso, s.o_cls)
-        wait([gr_x], jnp.logical_not(owner))
+        wait([gr_x], jnp.logical_not(odd))
         wait([gl_x, gq_x, gf_x, gs1, gs2, gs3])
         wait(ms + hs)
         for o in offsets:
             wait([gx[o]], (r != y) if (o[0] + o[1]) % 2 else special)
         pl.when(special)(gate_near.wait)
-        pl.when(owner)(red_near.wait)
+        pl.when(odd)(red_near.wait)
         for cp in (gs1n, gs2n, gs3n, img_n, mn, hn, n1, n2, n3, n4):
             cp.wait()
         ln.drain()
@@ -1492,10 +1773,17 @@
     pl.run_scoped(block_back, *[pltpu.VMEM(*v) for v in LATE.values()])
 
 
-SHAPES["dfs2"] = ((1280, 256), BF16)
-
-
 LATE = dict(
+    zst=((2, 3, 3, 2, 2, 32, 256), BF16),
+    psm=((9, 2, 2, 32, 256), BF16),
+    psh=((9, 2, 2, 32, 256), BF16),
+    fnr=((128, 512), BF16),
+    fnl=((32, 1024), BF16),
+    fnm=((9, 32, 256), BF16),
+    fnf=((128, 256), BF16),
+    pg=((2, 2, 32, 256), BF16),
+    clss=((32, 128), F32),
+    clso=((32, 128), F32),
     u3=((320, 1024), F32),
     dp3=((320, 1024), BF16),
     d3m=((480, 768), BF16),
@@ -1506,11 +1794,88 @@
     dp1=((320, 256), BF16),
     dp2=((320, 256), BF16),
     wfov=((4, 2, 2, 128, 256), BF16),
-    gr=((2, 2, 2, 128, 512), BF16),
+    gr=((4, 2, 128, 512), BF16),
     gl=((4, 2, 2, 32, 1024), BF16),
     gq=((9, 4, 2, 2, 32, 256), BF16),
     gf=((4, 2, 2, 128, 256), BF16),
 )
+
+
+FINAL = dict(
+    depth=((160, 512), BF16),
+    logits=((2, 40, 80), BF16),
+    img=((160, 2048), F32),
+    first=((128, 512), F32),
+    gain1=((1, 32), F32),
+    shift1=((1, 32), F32),
+    mid=((9, 32, 512), F32),
+    gain2=((1, 32), F32),
+    shift2=((1, 32), F32),
+    last=((32, 2048), F32),
+    gain3=((1, 128), F32),
+    shift3=((1, 128), F32),
+    red=((128, 512), F32),
+    heads=((2, 9, 32, 512), F32),
+    mess=((2, 9, 32, 512), F32),
+    gates=((2, 32, 512), F32),
+    cls=((32, 40), F32),
+)
+
+
+def widen_out(names, *refs):
+    s = SimpleNamespace(**dict(zip(names, refs)))
+    b = lax.axis_index("batch")
+    used = [0]
+
+    def move(src, dst):
+        cp = pltpu.make_async_copy(src, dst, s.sems.at[used[0]])
+        used[0] += 1
+        cp.start()
+        return cp
+
+    done = [move(s.o_depth, s.depth), move(s.o_logits, s.logits)]
+    wide = ["mess", "heads", "mid", "img", "last", "red", "first", "gates"]
+    loads = {n: move(getattr(s, "o_" + n), getattr(s, "i_" + n)) for n in wide}
+    small = [move(getattr(s, "o_" + n), getattr(s, "i_" + n)) for n in ("gs1", "gs2", "gs3", "cls")]
+    for n in wide:
+        loads[n].wait()
+        src, dst = getattr(s, "i_" + n), getattr(s, "v_" + n)
+        if n == "last":
+            for i in range(8):
+                for h in range(2):
+                    lane = 128 * (2 * i + h)
+                    dst[:, lane : lane + 128] = src[h, :, 128 * i : 128 * i + 128].astype(F32)
+        elif n == "img":
+            for i in range(0, 160, 32):
+                dst[i : i + 32, :] = src[i : i + 32, :].astype(F32)
+        elif len(src.shape) > 2:
+            for i in range(src.shape[0]):
+                dst[i] = src[i].astype(F32)
+        else:
+            dst[...] = src[...].astype(F32)
+        done.append(move(dst, getattr(s, n)))
+    for cp in small:
+        cp.wait()
+    quarter, spot = lax.div(b, np.int32(4)), lax.rem(b, np.int32(4))
+    at = pl.ds(pl.multiple_of(128 * lax.rem(quarter, np.int32(2)), 128), 128)
+    for n, layer in ((1, s.i_gs1), (2, s.i_gs2)):
+        v = pltpu.roll(layer[lax.div(quarter, np.int32(2)), :, at], lax.rem(128 - 32 * spot, np.int32(128)), 1)
+        for row, kind in ((1, "gain"), (0, "shift")):
+            keep = getattr(s, "v_%s%d" % (kind, n))
+            keep[...] = v[row : row + 1, 0:32]
+            done.append(move(keep, getattr(s, "%s%d" % (kind, n))))
+    block = lax.div(b, np.int32(2))
+    at = pl.ds(pl.multiple_of(128 * lax.rem(block, np.int32(4)), 128), 128)
+    v = s.i_gs3[lax.rem(b, np.int32(2)), :, at]
+    low = lax.div(block, np.int32(4)) == 0
+    s.v_shift3[...] = jnp.where(low, v[0:1], v[1:2])
+    s.v_gain3[...] = jnp.where(low, v[2:3], v[3:4])
+    done.append(move(s.v_shift3, s.shift3))
+    done.append(move(s.v_gain3, s.gain3))
+    s.v_cls[...] = s.i_cls[:, 0:40]
+    done.append(move(s.v_cls, s.cls))
+    for cp in done:
+        cp.wait()
 
 
 def fast(args):
@@ -1518,74 +1883,45 @@
         images, crop_height, crop_width, w_first, gain_first, shift_first, w_middle, gain_middle, shift_middle,
         w_last, gain_last, shift_last, w_reduce, w_heads, w_message, w_gates, w_classes, depth_cot, class_cot,
     ) = args
-    b, r = lax.axis_index("batch"), lax.axis_index("rows")
-    batch = lax.axis_size("batch")
-    classes = w_classes.shape[1]
-
-    def placed(vec):
-        share = vec.shape[0]
-        full = jnp.tile(vec.astype(F32), batch)
-        owner = lax.iota(jnp.int32, share * batch) // share
-        return lax.dynamic_slice_in_dim(jnp.where(owner == b, full, 0.0), r * (share * batch // 2), share * batch // 2)
-
-    def small(gain, shift):
-        zero = jnp.zeros((256,), F32)
-        return jnp.stack([zero, zero, placed(gain), placed(shift), zero, zero, zero, zero])
-
-    st3 = jnp.concatenate(
-        [jnp.zeros((4, 512), F32), placed(gain_last).reshape(2, 512), placed(shift_last).reshape(2, 512)]
-    )
+    narrow = jnp.concatenate([gain_first, shift_first, gain_middle, shift_middle])
+    gains = jnp.stack([narrow, gain_last, shift_last]).astype(F32)
     ins = (
-        crop_height, crop_width, images.reshape(160, 2048), w_first, w_middle, w_last, w_reduce, w_gates,
-        jnp.pad(w_classes, ((0, 0), (0, 128 - classes))), w_heads, w_message,
-        small(gain_first, shift_first), small(gain_middle, shift_middle), st3,
-        depth_cot.reshape(160, 512), jnp.pad(class_cot.reshape(160, classes), ((0, 0), (0, 128 - classes))),
+        crop_height, crop_width, images.reshape(160, 2048), w_first, w_middle, w_last, w_reduce, w_gates, w_classes,
+        w_heads, w_message, gains, depth_cot.reshape(160, 512), class_cot.transpose(0, 1, 3, 2).reshape(2, 40, 80),
     )
     names = list(INS) + list(OUTS) + list(SHAPES) + ["send_sems", "recv_sems", "near_sems"]
-    smem, hbm, vmem = (pl.BlockSpec(memory_space=m) for m in (pltpu.SMEM, pl.ANY, pltpu.VMEM))
-    spec = {"crop_h": smem, "crop_w": smem, "st1": vmem, "st2": vmem, "st3": vmem}
+    smem, hbm, vmem = (pl.BlockSpec(memory_space=m) for m in (pltpu.SMEM, pltpu.HBM, pltpu.VMEM))
+    spec = {"crop_h": smem, "crop_w": smem, "gains": vmem}
     outs = pl.pallas_call(
         functools.partial(body, names),
         out_shape=[jax.ShapeDtypeStruct(*v) for v in OUTS.values()],
         in_specs=[spec.get(n, hbm) for n in INS],
         out_specs=[hbm] * len(OUTS),
         scratch_shapes=[pltpu.VMEM(*v) for v in SHAPES.values()]
-        + [pltpu.SemaphoreType.DMA((SEMS,)) for _ in range(3)],
-        compiler_params=pltpu.CompilerParams(has_side_effects=True, vmem_limit_bytes=64 * 2**20),
+        + [pltpu.SemaphoreType.DMA((n,)) for n in (SENDS, SENDS, NEAR)],
+        compiler_params=pltpu.CompilerParams(has_side_effects=True, collective_id=0, vmem_limit_bytes=64 * 2**20),
         name="residual_distill",
     )(*ins)
     o = dict(zip(OUTS, outs))
-
-    def share_of(v, axis):
-        return v.astype(F32)
-
-    def vector(gs, gain):
-        per = gs.shape[2] * (gs.shape[1] // 8)
-        width = 256 if gs.shape[2] == 256 else 1024
-        rows = 1 if width == 256 else 2
-        first = gs[:, rows * (1 if gain else 0) : rows * (2 if gain else 1)].reshape(2 * width)
-        share = 2 * width // batch
-        return lax.dynamic_slice_in_dim(first, b * share, share)
-
-    return (
-        o["o_depth"].reshape(1, 2, 80, 512),
-        o["o_logits"][:, :classes].reshape(1, 2, 80, classes),
-        o["o_img"].astype(F32).reshape(1, 2, 80, 2048),
-        o["o_first"].astype(F32),
-        vector(o["o_gs1"], True),
-        vector(o["o_gs1"], False),
-        o["o_mid"].astype(F32),
-        vector(o["o_gs2"], True),
-        vector(o["o_gs2"], False),
-        o["o_last"].astype(F32),
-        vector(o["o_gs3"], True),
-        vector(o["o_gs3"], False),
-        o["o_red"].astype(F32),
-        o["o_heads"].astype(F32),
-        o["o_mess"].astype(F32),
-        o["o_gates"].astype(F32),
-        o["o_cls"][:, :classes],
-    )
+    taken = [n for n in OUTS if n.startswith("o_")]
+    staged = {"i_" + n[2:]: OUTS[n] for n in taken if n not in ("o_depth", "o_logits")}
+    staged.update({"v_" + n: v for n, v in FINAL.items() if n not in ("depth", "logits")})
+    final = pl.pallas_call(
+        functools.partial(widen_out, taken + list(FINAL) + list(staged) + ["sems"]),
+        out_shape=[jax.ShapeDtypeStruct(*v) for v in FINAL.values()],
+        in_specs=[hbm] * len(taken),
+        out_specs=[hbm] * len(FINAL),
+        scratch_shapes=[pltpu.VMEM(*v) for v in staged.values()] + [pltpu.SemaphoreType.DMA((40,))],
+        compiler_params=pltpu.CompilerParams(vmem_limit_bytes=32 * 2**20),
+        name="widen_out",
+    )(*[o[n] for n in taken])
+    f = dict(zip(FINAL, final))
+    f["depth"] = f["depth"].reshape(1, 2, 80, 512)
+    f["logits"] = f["logits"].reshape(1, 2, 40, 80).transpose(0, 1, 3, 2)
+    f["img"] = f["img"].reshape(1, 2, 80, 2048)
+    for n in ("gain1", "shift1", "gain2", "shift2", "gain3", "shift3"):
+        f[n] = f[n].reshape(-1)
+    return tuple(f.values())
 
 
 def solution(mesh):

time: 409 us -> 332 us (0.81)
  Pallas kernels: 383 us -> 314 us
  other arithmetic: 11.1 us -> 2.04 us
    pallas_call x1, Pallas kernels: 383 us -> 310 us  [fast(): pl.pallas_call(functools.partial(body, names), out_shape=[jax.ShapeDtypeS...]
    unnamed x29 -> x28, local copies, waits for them, and re-layouts: 2.84 us -> 12.3 us
    convert_element_type x9 -> x1, other arithmetic: 7.37 us -> 1.26 us  [fast(): gains = jnp.stack([narrow, gain_last, shift_last]).astype(F32)]
where the time goes in v2:
time: 332 us; the launch traced here: 329 us
  Pallas kernels  314 us (95%)
  local copies, waits for them, and re-layouts  12.3 us (4%)
    pallas_call x1, Pallas kernels, fast(): pl.pallas_call(functools.partial(body, names), out_shape=[jax.ShapeDtypeS...  310 us
    unnamed x28, local copies, waits for them, and re-layouts  12.3 us

profile of v2, /device:TPU:0, one launch (start us, length us, event | category | flops | bytes accessed | tf_op | source)
XLA Modules:
  0.0 328.9 jit_solution(16498842675072708444)
XLA Ops:
  0.7 0.8 maximum_bitcast_fusion
  1.4 1.3 maximum_convert_fusion.refs_11_
  2.7 309.8 %residual_distill.1 = (bf16[160,512]{1,0:T(8,128)(2,1)}, bf16[2,40,80]{2,1,0:T(8,128)(2,1)}, bf16[160,2048]{1,0:T(8,128)(2,1)}, bf16[128,512]{1,0:T(8,128)(2,1)}...) custom-call(s32[16]{0:T(128)} %refs_0_.1, ...), custom_call_target="tpu_custom_call" | custom-call | tf_op jit(solution)/shard_map/residual_distill/pallas_call | solution.py:1895
  312.5 0.0 copy-start
  312.5 1.1 copy-done
  313.6 0.0 copy-start.1
  313.6 1.1 copy-done.1
  314.7 0.0 copy-start.2
  314.7 1.1 copy-done.2
  315.7 0.0 copy-start.3
  315.7 1.0 copy-done.3
  316.7 0.0 copy-start.4
  316.7 0.9 copy-done.4
  317.6 0.0 copy-start.5
  317.6 0.9 copy-done.5
  318.5 0.0 copy-start.6
  318.5 0.9 copy-done.6
  319.4 0.0 copy-start.7
  319.4 0.9 copy-done.7
  320.3 0.0 copy-start.8
  320.3 0.8 copy-done.8
  321.2 0.0 copy-start.9
  321.2 0.8 copy-done.9
  321.9 0.0 copy-start.10
  321.9 0.7 copy-done.10
  322.6 0.0 copy-start.11
  322.6 0.7 copy-done.11
  323.4 0.0 copy-start.12
  323.4 0.7 copy-done.12
  324.1 0.0 copy-start.13
  324.1 0.7 copy-done.13
  324.8 3.9 %widen_out.1 = (bf16[160,512]{1,0:T(8,128)(2,1)}, bf16[2,40,80]{2,1,0:T(8,128)(2,1)}, f32[160,2048]{1,0:T(8,128)}, f32[128,512]{1,0:T(8,128)}, f32[1,32]{1,0:T(1...) custom-call(bf16[160,512]{1,0:T(8,128)(2,1)S(1)} %copy-done.4, ...), custom_call_target="tpu_custom_call" | custom-call | tf_op jit(solution)/shard_map/widen_out/pallas_call | solution.py:1909
Async XLA Ops:
  312.5 1.1 copy-start
  313.6 1.1 copy-start.1
  314.7 1.1 copy-start.2
  315.7 1.0 copy-start.3
  316.7 0.9 copy-start.4
  317.6 0.9 copy-start.5
  318.5 0.9 copy-start.6
  319.4 0.9 copy-start.7
  320.3 0.8 copy-start.8
  321.2 0.8 copy-start.9
  321.9 0.7 copy-start.10
  322.6 0.7 copy-start.11
  323.4 0.7 copy-start.12
  324.1 0.7 copy-start.13

commit v3 on v2

--- a/solution.py
+++ b/solution.py
@@ -15,7 +15,7 @@
 BF16 = jnp.bfloat16
 ROOT = 0.7978845608028654
 CUBE = 0.044715
-SENDS = 240
+SENDS = 247
 NEAR = 54
 
 
@@ -629,6 +629,8 @@
     msgb=((1280, 256), BF16),
     gateb=((1280, 256), BF16),
     mrecv=((4, 160, 512), BF16),
+    dm=((4, 160, 512), BF16),
+    eu=((2, 160, 512), BF16),
     dcotv=((160, 512), BF16),
     ccotv=((160, 128), BF16),
     olt=((2, 40, 80), BF16),
@@ -1053,7 +1055,7 @@
     line_relay(go_wl, at_wl)
     line_relay(go_wr, at_wr, odd)
     norm_terms(0, s.bnp1, 256)
-    heads_a = task_push(s.heads.at[y], s.wh, 0, 4, False)
+    heads_a = task_push(s.heads.at[y], s.wh, 0, 5, False)
 
     def act_from(prebuf, bnp, dst):
         def step(base):
@@ -1078,7 +1080,7 @@
     over_h = ln.push(s.heads.at[1 - y], s.st_h, ypeer)
     norm_terms(1, s.bnp2, 256)
     relay_a = task_relay(heads_a, s.wh)
-    heads_b = task_push(s.heads.at[y], s.wh, 4, 8, False)
+    heads_b = task_push(s.heads.at[y], s.wh, 5, 9, False)
     act_from(s.pre2, s.bnp2, s.a2)
     a2_x = ln.push(s.a2.at[:, pl.ds(half, 256)], s.a2.at[:, pl.ds(half, 256)], xpeer)
     line_core(go_wl, col_wl, cores_wl)
@@ -1093,7 +1095,6 @@
     over_m = ln.push(s.messages.at[1 - y], s.st_m, ypeer)
     norm_terms(2, s.bnp3, 1024)
     relay_b = task_relay(heads_b, s.wh)
-    heads_c = task_push(s.heads.at[y], s.wh, 8, 9, False)
     wait([over_h])
     staged_h = ln.near(s.st_h.at[:, :, pl.ds(fhalf, 256)], s.wh.at[:, z, 1 - y, c])
     heads_d = task_push(s.st_h, s.wh, 0, 5, True)
@@ -1143,7 +1144,6 @@
     g_x = ln.push(own, own, xpeer)
     g_y = ln.push(own, own, ypeer)
     g_c = ln.push(own, own, core)
-    relay_c = task_relay(heads_c, s.wh)
     wait([g_x])
     bx = block_of(1 - r, y, c, 0, 80)
     g_xy = ln.push(bx, bx, ypeer)
@@ -1212,7 +1212,7 @@
             ]
 
         mess = [mess_push(0), mess_push(1)]
-        for part in (relay_a, relay_b, relay_c, relay_d, relay_e):
+        for part in (relay_a, relay_b, relay_d, relay_e):
             task_ready(part)
         staged_h.wait()
 
@@ -1272,16 +1272,70 @@
 
         g_own = to_owners(s.gateb, lambda: s.fg.at[r, 1], special)
         pl.when(special)(keep(s.fg.at[r, 1], s.gateb))
-        spread(s.ffull, f3, 4, 512)
         relayed = [[task_relay(p, s.wq) for p in mess[0]]]
         mess.append(mess_push(2))
+        spread(s.ffull, f3, 4, 512)
+
+        wait([cls_got])
+        for i in range(2):
+            s.ctf[...] = jnp.zeros((128, 128), F32)
+            s.ctf[0:40, 0:80] = s.cct[i].astype(F32)
+            turned = s.ctf[...].T
+            s.ccotv[80 * i : 80 * i + 80, :] = turned[0:80, :].astype(BF16)
+        for o in offsets:
+            wait([g_own[o]], (r != y) if (o[0] + o[1]) % 2 else special)
+
+        def early_step(base):
+            rows = pl.ds(base, 32)
+            m = lanes(s.maskp[pl.ds(own_px + base, 32), :], 512)
+            gd, gc = s.fg[0, 1, rows, :].astype(F32), s.fg[1, 1, rows, :].astype(F32)
+            dj = (s.ccotv[rows, :].astype(F32) * m[:, :128]).astype(BF16)
+            s.ccotv[rows, :] = dj
+            dd = s.dcotv[rows, :].astype(F32) * m
+            dmer = dot_last(dj, s.wc[...].reshape(512, 128))
+            s.eu[0, rows, :] = dd.astype(BF16)
+            s.eu[1, rows, :] = dmer.astype(BF16)
+            down, up = dd * gd, dmer * gc
+            both = (down + up).astype(BF16)
+            s.dm[0, rows, :] = up.astype(BF16)
+            s.dm[1, rows, :] = both
+            s.dm[2, rows, :] = both
+            s.dm[3, rows, :] = down.astype(BF16)
+
+        rows_loop(160, 32, early_step)
+        d_got = ln.group(seven)
+        for o in offsets:
+            rr, yy, cc = peer(*o)
+            ll = pl.ds(pl.multiple_of(256 * cc, 128), 256)
+            d_got.push(s.dm.at[2 * rr + yy, :, ll], s.dmg.at[pl.ds(own_px, 160)], dev(z, yy, cc, rr))
+        u_got = {}
+        for o in offsets:
+            rr, yy, cc = peer(*o)
+            ll = pl.ds(pl.multiple_of(256 * cc, 128), 256)
+            u_got[o] = ln.push(s.eu.at[rr, :, ll], s.exg.at[0, pl.ds(own_px, 160)], dev(z, yy, cc, rr), rr == yy)
+        s.dmg[pl.ds(own_px, 160), :] = s.dm[task, :, pl.ds(fhalf, 256)]
+
+        @pl.when(special)
+        def _():
+            s.exg[0, pl.ds(own_px, 160), :] = s.eu[r, :, pl.ds(fhalf, 256)]
+
+        @pl.when(jnp.logical_not(special))
+        def _():
+            s.exg[0] = jnp.zeros(s.exg.shape[1:], BF16)
+
         relayed.append([task_relay(p, s.wq) for p in mess[1]])
+        wait([d_got])
+        spread(s.dmg, d3, 4, 256)
+        conv_weight(f3, d3, s.gm, 4, 0, 9)
         staged_m.wait()
+        gm_z = []
         for a in range(3):
+            if a == 2:
+                relayed.append([task_relay(p, s.wq) for p in mess[2]])
+                for part in range(3):
+                    gm_z.append(grad_push(0, s.gm, s.rm, 3 * part, 3 * part + 3))
             for p in relayed[a]:
                 task_ready(p)
-            if a == 0:
-                relayed.append(None)
 
             def mess_step(i, carry, a=a):
                 rows = pl.ds(pl.multiple_of(i * 320, 16), 320)
@@ -1296,8 +1350,6 @@
                 return carry
 
             lax.fori_loop(0, 4, mess_step, 0)
-            if a == 0:
-                relayed[2] = [task_relay(p, s.wq) for p in mess[2]]
 
         m_own = ln.group(seven)
         for o in offsets:
@@ -1305,15 +1357,15 @@
             m_own.push(s.msgb.at[pl.ds(px_of(rr, yy, cc), 160)], s.mrecv.at[task, :, pl.ds(fhalf, 256)], dev(z, yy, cc, rr))
         keep(s.mrecv.at[task], s.msgb)()
 
-        wait([cls_got])
-        for i in range(2):
-            s.ctf[...] = jnp.zeros((128, 128), F32)
-            s.ctf[0:40, 0:80] = s.cct[i].astype(F32)
-            turned = s.ctf[...].T
-            s.ccotv[80 * i : 80 * i + 80, :] = turned[0:80, :].astype(BF16)
+        def back_step(i, carry):
+            px = pl.multiple_of(i * 320, 16)
+            dfull[pl.ds(px, 320), :] = conv_back(d3, s.wq, i)
+            return carry
+
+        lax.fori_loop(0, 4, back_step, 0)
+
         for o in offsets:
-            wait([f_own[o], g_own[o]], (r != y) if (o[0] + o[1]) % 2 else special)
-
+            wait([f_own[o]], (r != y) if (o[0] + o[1]) % 2 else special)
         wait([m_own])
 
         def stream_step(base):
@@ -1327,45 +1379,21 @@
             s.ods[rows, :] = ((f0 + gd * sd) * m).astype(BF16)
             merged = (f3_ + gc * sc).astype(BF16)
             s.mrg[rows, :] = merged
-            m1l = m[:, :128]
-            wcls = s.wc[...].reshape(512, 128)
-            s.olg[rows, :] = (dot(merged, wcls) * m1l).astype(BF16)
-            dj = (s.ccotv[rows, :].astype(F32) * m1l).astype(BF16)
-            s.ccotv[rows, :] = dj
-            dd = s.dcotv[rows, :].astype(F32) * m
-            dmer = dot_last(dj, wcls)
-            s.fg[0, 0, rows, :] = dd.astype(BF16)
-            s.fg[1, 0, rows, :] = dmer.astype(BF16)
+            s.olg[rows, :] = (dot(merged, s.wc[...].reshape(512, 128)) * m[:, :128]).astype(BF16)
+            dd, dmer = s.eu[0, rows, :].astype(F32), s.eu[1, rows, :].astype(F32)
             s.fg[0, 1, rows, :] = (dd * sd * gd * (1.0 - gd)).astype(BF16)
             s.fg[1, 1, rows, :] = (dmer * sc * gc * (1.0 - gc)).astype(BF16)
-            down, up = dd * gd, dmer * gc
-            both = (down + up).astype(BF16)
-            s.mrecv[0, rows, :] = up.astype(BF16)
-            s.mrecv[1, rows, :] = both
-            s.mrecv[2, rows, :] = both
-            s.mrecv[3, rows, :] = down.astype(BF16)
 
         rows_loop(160, 32, stream_step)
         e_got = {}
-        d_got = ln.group(seven)
         for o in offsets:
             rr, yy, cc = peer(*o)
             ll = pl.ds(pl.multiple_of(256 * cc, 128), 256)
-            d_got.push(s.mrecv.at[2 * rr + yy, :, ll], s.dmg.at[pl.ds(own_px, 160)], dev(z, yy, cc, rr))
-        for o in offsets:
-            rr, yy, cc = peer(*o)
-            ll = pl.ds(pl.multiple_of(256 * cc, 128), 256)
-            e_got[o] = ln.push(s.fg.at[rr, :, :, ll], s.exg.at[:, pl.ds(own_px, 160)], dev(z, yy, cc, rr), rr == yy)
-        s.dmg[pl.ds(own_px, 160), :] = s.mrecv[task, :, pl.ds(fhalf, 256)]
+            e_got[o] = ln.push(s.fg.at[rr, 1, :, ll], s.exg.at[1, pl.ds(own_px, 160)], dev(z, yy, cc, rr), rr == yy)
 
         @pl.when(special)
         def _():
-            for e in range(2):
-                s.exg[e, pl.ds(own_px, 160), :] = s.fg[r, e, :, pl.ds(fhalf, 256)]
-
-        @pl.when(jnp.logical_not(special))
-        def _():
-            s.exg[...] = jnp.zeros(s.exg.shape, BF16)
+            s.exg[1, pl.ds(own_px, 160), :] = s.fg[r, 1, :, pl.ds(fhalf, 256)]
 
         for i in range(2):
             s.ctf[...] = jnp.zeros((128, 128), F32)
@@ -1374,6 +1402,31 @@
             s.olt[i] = turned[0:40, 0:80].astype(BF16)
         out_near = [ln.near(s.ods, s.o_depth), ln.near(s.olt, s.o_logits)]
         s.gcls[...] = dot_first(s.mrg[...], s.ccotv[...]).astype(BF16).reshape(16, 32, 128)
+        wait([u_got[o] for o in offsets], special)
+        wait([e_got[o] for o in offsets], special)
+
+        @pl.when(special)
+        def _():
+            def gate_back(base):
+                rows = pl.ds(base, 320)
+                dfull[rows, :] = dfull[rows, :] + dot_last(s.exg[1, rows, :], s.wg[...].reshape(512, 256))
+
+            rows_loop(1280, 320, gate_back)
+
+        chalf = pl.ds(pl.multiple_of(256 * (1 - c), 128), 256)
+
+        def give(base):
+            rows = pl.ds(base, 80)
+            s.dfs[rows, :] = dfull[rows, chalf].astype(BF16)
+
+        rows_loop(1280, 80, give)
+        df_c = ln.push(s.dfs, s.dfr, core)
+
+        @pl.when(special)
+        def _():
+            s.gg[...] = dot_first(s.ffull[...], s.exg[1]).astype(BF16).reshape(s.gg.shape)
+
+        gg_z = [ln.push(s.gg.at[zk(k)], s.rg.at[k - 1], dev(zk(k), y, c, r), special, lambda side, k=k: s.rg.at[k - 1] if side else s.gg.at[0]) for k in (1, 2, 3)]
         cg = ln.group(lambda: s.rcls)
         n_cls = 0
         for q in range(4):
@@ -1386,43 +1439,6 @@
                     zz = zk(q) if q else z
                     cg.push(s.gcls.at[4 * zz + 2 * yy + cc], s.rcls.at[n_cls], dev(zz, yy, cc, r))
                     n_cls += 1
-        wait([d_got])
-        spread(s.dmg, d3, 4, 256)
-        gm_z = []
-        for a in range(3):
-            conv_weight(f3, d3, s.gm, 4, 3 * a, 3 * a + 3)
-            gm_z.append(grad_push(0, s.gm, s.rm, 3 * a, 3 * a + 3))
-        wait([e_got[o] for o in offsets], special)
-
-        def back_step(i, carry):
-            px = pl.multiple_of(i * 320, 16)
-            dfull[pl.ds(px, 320), :] = conv_back(d3, s.wq, i)
-            return carry
-
-        lax.fori_loop(0, 4, back_step, 0)
-
-        @pl.when(special)
-        def _():
-            def gate_back(base):
-                rows = pl.ds(base, 320)
-                dfull[rows, :] = dfull[rows, :] + dot_last(s.exg[1, rows, :], s.wg[...].reshape(512, 256))
-
-            rows_loop(1280, 320, gate_back)
-
-        chalf = pl.ds(pl.multiple_of(256 * (1 - c), 128), 256)
-
-        def give(base):
-            rows = pl.ds(base, 80)
-            s.dfs[rows, :] = dfull[rows, chalf].astype(BF16)
-
-        rows_loop(1280, 80, give)
-        df_c = ln.push(s.dfs, s.dfr, core)
-
-        @pl.when(special)
-        def _():
-            s.gg[...] = dot_first(s.ffull[...], s.exg[1]).astype(BF16).reshape(s.gg.shape)
-
-        gg_z = [ln.push(s.gg.at[zk(k)], s.rg.at[k - 1], dev(zk(k), y, c, r), special, lambda side, k=k: s.rg.at[k - 1] if side else s.gg.at[0]) for k in (1, 2, 3)]
         wait([df_c])
 
         def dhead_step(base):
@@ -1454,8 +1470,12 @@
             rr, yy, _ = peer(dr, dy, 0)
             src = s.drr.at[pl.ds(pl.multiple_of(320 * yy + 160 * rr, 16), 160)]
             ro.append(ln.push(src, s.dro.at[len(ro)], dev(z, yy, c, rr)))
-        conv_weight(r3, d3, s.gh, 4, 0, 9)
+        gh_z = []
+        conv_weight(r3, d3, s.gh, 4, 0, 2)
         grad_hop(gm_z[0])
+        gh_z.append(grad_push(1, s.gh, s.rh, 0, 2))
+        conv_weight(r3, d3, s.gh, 4, 2, 9)
+        grad_hop(gm_z[1])
         wait(ro)
         keep_rows = pl.ds(pl.multiple_of(320 * y + 160 * r, 16), 160)
         total_red = s.drr[keep_rows, :].astype(F32)
@@ -1465,7 +1485,7 @@
         for cp in out_near:
             cp.wait()
         ln.drain(scoped=True)
-        return cg, gm_z, gg_z
+        return cg, gm_z, gg_z, gh_z
 
     state = {}
 
@@ -1480,7 +1500,7 @@
         pltpu.VMEM((1280, 256), F32),
         pltpu.VMEM((1280, 512), F32),
     )
-    cg, gm_z, gg_z = state["t"]
+    cg, gm_z, gg_z, gh_z = state["t"]
 
     dr_x = ln.push(s.dred.at[pl.ds(my_rows, 160)], s.dred.at[pl.ds(my_rows, 160)], xpeer)
 
@@ -1561,10 +1581,9 @@
         gr[...] = dot_first(s.blk[...], s.dred[...]).astype(BF16).reshape(gr.shape)
         gr_c = ln.push(gr, s.rcr, core, jnp.logical_not(odd))
         plane_end(3, ar3)
+        grad_hop(gm_z[2])
         t = reduce_line(3)
-        for part in gm_z[1:]:
-            grad_hop(part)
-        gh_z = [grad_push(1, s.gh, s.rh, 0, 2)]
+        gh_z.append(grad_push(1, s.gh, s.rh, 2, 5))
         gs3 = ln.push(s.at3, s.o_gs3.at[r], xpeer)
         gs3n = ln.near(s.at3, s.o_gs3.at[r])
         mu = jnp.concatenate([t[0:1], t[1:2]], axis=1) / count
@@ -1641,7 +1660,16 @@
             rows_loop(320, 80, d_step)
             return gsx, gsn
 
-        gs2, gs2n = norm_back(4, s.par2, s.pre2, s.bnp2, s.dp2, s.o_gs2, after_plane_two, lambda: gh_z.append(grad_push(1, s.gh, s.rh, 2, 4)))
+        def window_two():
+            grad_hop(gh_z[0])
+            gh_z.append(grad_push(1, s.gh, s.rh, 5, 8))
+            grad_hop(gh_z[1])
+
+        def window_one():
+            gh_z.append(grad_push(1, s.gh, s.rh, 8, 9))
+            grad_hop(gh_z[2])
+
+        gs2, gs2n = norm_back(4, s.par2, s.pre2, s.bnp2, s.dp2, s.o_gs2, after_plane_two, window_two)
         spread(s.dp2, s.d3m, 1, 256)
         s.u3[:, 0:512] = conv_back(s.d3m, s.wm, 0)
         s.pas1[...] = s.u3[:, pl.ds(ohalf, 256)].astype(BF16)
@@ -1649,7 +1677,7 @@
         conv_weight(s.a3, s.d3m, gq, 1, 0, 9)
         gq_c = to_core(gq, s.rcm, True)
         wait([pa1])
-        gs1, gs1n = norm_back(5, s.par1, s.pre1, s.bnp1, s.dp1, s.o_gs1, after_plane_one, lambda: gh_z.append(grad_push(1, s.gh, s.rh, 4, 9)))
+        gs1, gs1n = norm_back(5, s.par1, s.pre1, s.bnp1, s.dp1, s.o_gs1, after_plane_one, window_one)
         dp_x = ln.push(s.dp1.at[pl.ds(other_rows, 160)], s.dp1r, xpeer)
         gf[...] = dot_first(s.xall[...], s.dp1[...]).astype(BF16).reshape(gf.shape)
         gf_c = to_core(gf, s.rcf, False)
@@ -1666,8 +1694,7 @@
             for q in range(4):
                 s.ryr[q] = (s.ryr[q].astype(F32) + s.rcr[q, y].astype(F32)).astype(BF16)
 
-        for part in gh_z[:2]:
-            grad_hop(part)
+        grad_hop(gh_z[3])
         gr_z = [ln.push(s.ryr.at[zk(q)], s.rzr.at[q - 1], dev(zk(q), y, c, r), odd) for q in (1, 2, 3)]
         wait([gl_y])
         add_y(s.rcl, s.ryl, False)
@@ -1708,7 +1735,6 @@
             rows_loop(160, 32, img_step)
         img_n = ln.near(s.oimg, s.o_img)
 
-        grad_hop(gh_z[2])
         hs, hn = task_out(gh_z, s.rh, s.gh, s.psh, s.o_heads)
 
         @pl.when(special)
@@ -1912,7 +1938,7 @@
         in_specs=[hbm] * len(taken),
         out_specs=[hbm] * len(FINAL),
         scratch_shapes=[pltpu.VMEM(*v) for v in staged.values()] + [pltpu.SemaphoreType.DMA((40,))],
-        compiler_params=pltpu.CompilerParams(vmem_limit_bytes=32 * 2**20),
+        compiler_params=pltpu.CompilerParams(vmem_limit_bytes=64 * 2**20),
         name="widen_out",
     )(*[o[n] for n in taken])
     f = dict(zip(FINAL, final))

time: 332 us -> 287 us (0.86)
  Pallas kernels: 314 us -> 283 us
  local copies, waits for them, and re-layouts: 12.3 us -> 0 us
    pallas_call x1, Pallas kernels: 310 us -> 276 us  [fast(): pl.pallas_call(functools.partial(body, names), out_shape=[jax.ShapeDtypeS...]
    unnamed x28 -> x0, local copies, waits for them, and re-layouts: 12.3 us -> none
where the time goes in v3:
time: 287 us; the launch traced here: 286 us
  Pallas kernels  283 us (99%)
    pallas_call x1, Pallas kernels, fast(): pl.pallas_call(functools.partial(body, names), out_shape=[jax.ShapeDtypeS...  276 us
    pallas_call x1, Pallas kernels, fast(): pl.pallas_call(functools.partial(widen_out, taken + list(FINAL) + list(st...  7.11 us

profile of v3, /device:TPU:0, one launch (start us, length us, event | category | flops | bytes accessed | tf_op | source)
XLA Modules:
  0.0 286.2 jit_solution(4461157602859561220)
XLA Ops:
  0.7 0.8 maximum_bitcast_fusion
  1.4 1.3 maximum_convert_fusion.refs_11_
  2.7 276.2 %residual_distill.1 = (bf16[160,512]{1,0:T(8,128)(2,1)}, bf16[2,40,80]{2,1,0:T(8,128)(2,1)}, bf16[160,2048]{1,0:T(8,128)(2,1)}, bf16[128,512]{1,0:T(8,128)(2,1)}...) custom-call(s32[16]{0:T(128)} %refs_0_.1, ...), custom_call_target="tpu_custom_call" | custom-call | tf_op jit(solution)/shard_map/residual_distill/pallas_call | solution.py:1921
  278.9 7.1 %widen_out.1 = (bf16[160,512]{1,0:T(8,128)(2,1)}, bf16[2,40,80]{2,1,0:T(8,128)(2,1)}, f32[160,2048]{1,0:T(8,128)}, f32[128,512]{1,0:T(8,128)}, f32[1,32]{1,0:T(1...) custom-call(bf16[160,512]{1,0:T(8,128)(2,1)} %get-tuple-element.48.r, ...), custom_call_target="tpu_custom_call" | custom-call | tf_op jit(solution)/shard_map/widen_out/pallas_call | solution.py:1935

commit v4 on v3

--- a/solution.py
+++ b/solution.py
@@ -15,8 +15,9 @@
 BF16 = jnp.bfloat16
 ROOT = 0.7978845608028654
 CUBE = 0.044715
-SENDS = 247
-NEAR = 54
+SENDS = 118
+RECVS = 183
+NEAR = 21
 
 
 def dot(left, right):
@@ -49,36 +50,68 @@
 
 
 class Copy:
-    def __init__(self, remote, links, index, like):
-        self.remote, self.links, self.index, self.like = remote, links, index, like
+    def __init__(self, remote, links, send, recv, like):
+        self.remote, self.links, self.send, self.recv, self.like = remote, links, send, recv, like
+        self.scoped = like is None
 
     def wait_recv(self):
         if self.like is None:
             self.remote.wait_recv()
         else:
             ref = self.like(1)
-            pltpu.make_async_copy(ref, ref, self.links.recv.at[self.index]).wait()
+            pltpu.make_async_copy(ref, ref, self.links.recv.at[self.recv]).wait()
 
     def wait_send(self):
         if self.like is None:
             self.remote.wait_send()
         else:
             ref = self.like(0)
-            pltpu.make_async_copy(ref, ref, self.links.send.at[self.index]).wait()
+            pltpu.make_async_copy(ref, ref, self.links.send.at[self.send]).wait()
 
 
 class Group:
     scoped = True
 
-    def __init__(self, links, index, like):
-        self.links, self.index, self.like = links, index, like
+    def __init__(self, links, send, recv, like):
+        self.links, self.send, self.recv, self.like = links, send, recv, like
 
     def push(self, src, dst, device, when=None):
+        self.links.start(src, dst, device, self.send, self.recv, when)
+
+    def wait_recv(self):
+        ref = self.like()
+        pltpu.make_async_copy(ref, ref, self.links.recv.at[self.recv]).wait()
+
+    def wait_send(self):
+        ref = self.like()
+        pltpu.make_async_copy(ref, ref, self.links.send.at[self.send]).wait()
+
+
+class Near:
+    def __init__(self, links, src, dst):
+        self.links, self.index = links, links.local_free.pop(0)
+        self.copy = pltpu.make_async_copy(src, dst, links.local.at[self.index])
+        self.copy.start()
+
+    def wait(self):
+        self.copy.wait()
+        self.links.local_free.insert(0, self.index)
+
+
+class Links:
+    def __init__(self, send, recv, local):
+        self.send, self.recv, self.local = send, recv, local
+        self.used = 0
+        self.send_free = list(range(SENDS))
+        self.local_free = list(range(NEAR - 4))
+        self.open = []
+
+    def start(self, src, dst, device, send, recv, when):
         remote = pltpu.make_async_remote_copy(
             src_ref=src,
             dst_ref=dst,
-            send_sem=self.links.send.at[self.index],
-            recv_sem=self.links.recv.at[self.index],
+            send_sem=self.send.at[send],
+            recv_sem=self.recv.at[recv],
             device_id=device,
             device_id_type=MESH,
         )
@@ -86,59 +119,37 @@
             remote.start()
         else:
             pl.when(when)(remote.start)
-
-    def wait_recv(self):
-        ref = self.like()
-        pltpu.make_async_copy(ref, ref, self.links.recv.at[self.index]).wait()
-
-    def wait_send(self):
-        ref = self.like()
-        pltpu.make_async_copy(ref, ref, self.links.send.at[self.index]).wait()
-
-
-class Links:
-    def __init__(self, send, recv, local):
-        self.send, self.recv, self.local = send, recv, local
-        self.used, self.local_used = 0, 0
-        self.open = []
+        return remote
+
+    def pair(self):
+        self.used += 1
+        return self.send_free.pop(0), self.used - 1
 
     def push(self, src, dst, device, when=None, like=None):
-        i = self.used
-        self.used += 1
-        send, recv = self.send.at[i], self.recv.at[i]
-        remote = pltpu.make_async_remote_copy(
-            src_ref=src, dst_ref=dst, send_sem=send, recv_sem=recv, device_id=device, device_id_type=MESH
-        )
-        if when is None:
-            remote.start()
-        else:
-            pl.when(when)(remote.start)
-        cp = Copy(remote, self, i, like)
+        send, recv = self.pair()
+        cp = Copy(self.start(src, dst, device, send, recv, when), self, send, recv, like)
         self.open.append((cp, when))
         return cp
 
     def group(self, like, when=None):
-        cp = Group(self, self.used, like)
-        self.used += 1
+        cp = Group(self, *self.pair(), like)
         self.open.append((cp, when))
         return cp
 
     def near(self, src, dst):
-        i = self.local_used
-        self.local_used += 1
-        cp = pltpu.make_async_copy(src, dst, self.local.at[i])
-        cp.start()
-        return cp
+        return Near(self, src, dst)
 
     def drain(self, scoped=False):
         kept = []
         for cp, when in self.open:
-            if scoped and isinstance(cp, Copy) and cp.like is not None:
+            if scoped and not cp.scoped:
                 kept.append((cp, when))
-            elif when is None:
+                continue
+            if when is None:
                 cp.wait_send()
             else:
                 pl.when(when)(cp.wait_send)
+            self.send_free.insert(0, cp.send)
         self.open = kept
 
 
@@ -663,6 +674,8 @@
     rcm=((9, 4, 2, 32, 256), BF16),
     rcf=((4, 2, 128, 256), BF16),
     ryr=((4, 128, 512), BF16),
+    hpr=((128, 512), BF16),
+    hpl=((32, 1024), BF16),
     ryl=((4, 32, 1024), BF16),
     rym=((9, 4, 32, 256), BF16),
     ryf=((4, 128, 256), BF16),
@@ -780,6 +793,7 @@
 
     core, ypeer, xpeer = dev(z, y, 1 - c, r), dev(z, 1 - y, c, r), dev(z, y, c, 1 - r)
     special = r == y
+    plain = r != y
     task = 2 * r + y
     img = 2 * y + c
     own_px = pl.multiple_of(320 * img + 160 * r, 16)
@@ -808,27 +822,40 @@
     def both(p, q):
         return q if p is None else (p if q is None else p & q)
 
-    def line_start(src, at, when=None):
-        got = {q: ln.push(src, at(z), dev(zk(q), y, c, r), when) for q in (1, 3)}
-        got[2] = ln.push(src, at(z), dev(zk(2), y, c, r), both(when, ends))
-        return got, [ln.push(src, at(z), ypeer, when)]
+    def line_start(src, at, pair, when=None, relay=True):
+        sides = ln.group(pair, when)
+        for q in (1, 3):
+            sides.push(src, at(z), dev(zk(q), y, c, r), when)
+        across = ln.push(src, at(z), dev(zk(2), y, c, r), both(when, ends) if relay else when)
+        return [sides, across, relay, None, None]
+
+    def line_y(state, src, at, four, when=None):
+        state[4] = ln.group(four, when)
+        state[4].push(src, at(z), ypeer, when)
 
     def line_relay(state, at, when=None):
-        got, ys = state
-        wait([got[1], got[3]], when)
-        got[0] = ln.push(at(3 - z), at(3 - z), far_end, both(when, inner))
-        ys.append(ln.push(at(zk(3)), at(zk(3)), ypeer, when))
-        ys.append(ln.push(at(zk(1)), at(zk(1)), ypeer, when))
+        sides, _, relay = state[:3]
+        wait([sides], when)
+        if relay:
+            state[3] = ln.push(at(3 - z), at(3 - z), far_end, both(when, inner))
+
+    def line_sides(state, at, when=None):
+        ys = state[4]
+        ys.push(at(zk(3)), at(zk(3)), ypeer, when)
+        ys.push(at(zk(1)), at(zk(1)), ypeer, when)
 
     def line_last(state, at, col, when=None):
-        got, ys = state
-        wait([got[2]], both(when, inner))
-        wait([got[0]], both(when, ends))
-        ys.append(ln.push(at(zk(2)), at(zk(2)), ypeer, when))
+        _, across, relay, hand, ys = state
+        if relay:
+            wait([across], both(when, inner))
+            wait([hand], both(when, ends))
+        else:
+            wait([across], when)
+        ys.push(at(zk(2)), at(zk(2)), ypeer, when)
         return [ln.push(col(y), col(y), core, when)]
 
     def line_core(state, col, cores, when=None):
-        wait(state[1], when)
+        wait([state[4]], when)
         cores.append(ln.push(col(1 - y), col(1 - y), core, when))
 
     def at_wf(zz):
@@ -880,15 +907,16 @@
         pl.semaphore_signal(barrier, inc=1, device_id=friend, device_id_type=MESH)
     pl.semaphore_wait(barrier, len(friends))
 
-    go_wf = line_start(s.first.at[:, pl.ds(half, 256)], at_wf)
+    src_wf, src_wm = s.first.at[:, pl.ds(half, 256)], s.middle.at[:, :, pl.ds(half, 256)]
+    go_wf = line_start(src_wf, at_wf, lambda: s.wf.at[0, 0], relay=False)
+    line_y(go_wf, src_wf, at_wf, lambda: s.wf.at[:, 0, 0])
     img_x = ln.push(s.images, s.xall.at[pl.ds(my_rows, 160)], xpeer)
-    go_wm = line_start(s.middle.at[:, :, pl.ds(half, 256)], at_wm)
+    go_wm = line_start(src_wm, at_wm, lambda: s.wm.at[:, 0, 0])
+    line_y(go_wm, src_wm, at_wm, lambda: s.wm.at[:, :, 0, 0])
     for cp in near_last:
         cp.wait()
-    got_wl = {q: ln.push(at_wl(z), at_wl(z), dev(zk(q), y, c, r)) for q in (1, 3)}
-    got_wl[2] = ln.push(at_wl(z), at_wl(z), dev(zk(2), y, c, r), ends)
-    got_wr = {q: ln.push(s.reduce, at_wr(z), dev(zk(q), y, c, r), odd) for q in (1, 3)}
-    got_wr[2] = ln.push(s.reduce, at_wr(z), dev(zk(2), y, c, r), odd & ends)
+    go_wl = line_start(at_wl(z), at_wl, lambda: s.wl.at[0, 0])
+    go_wr = line_start(s.reduce, at_wr, lambda: s.wr.at[0], odd)
 
     for i in range(4):
         high, wide = s.crop_h[4 * z + i], s.crop_w[4 * z + i]
@@ -912,6 +940,7 @@
     near_own.wait()
     near_wf.wait()
     line_relay(go_wf, at_wf)
+    line_sides(go_wf, at_wf)
     cores_wf = line_last(go_wf, at_wf, col_wf)
     near_wm.wait()
     line_relay(go_wm, at_wm)
@@ -928,37 +957,37 @@
 
     rows_loop(320, 80, mask_x)
     wait(cores_wf)
+    wfo_x = ln.group(lambda: s.wf)
+    for zz in (0, 1):
+        wfo_x.push(s.wf.at[zz], s.wfo.at[zz], xpeer)
 
     def task_push(src, dst, lo, hi, staged):
         yy = 1 - y if staged else y
-        got = {}
+        taps = hi - lo
+        sides = ln.group(lambda: s.rbuf.at[0 : 80 * taps])
+        across = ln.group(lambda: dst.at[lo:hi, 0, 0], ends)
         for q in (1, 3, 2, 0):
-            def like(q=q):
-                return dst.at[lo:hi, 0, 0] if q else dst.at[lo:hi, 0, 0, 0]
-
-            when = ends if q == 2 else None
-            got[q] = ln.group(like, when)
             for i in range(2):
                 if q + i == 0:
                     continue
                 cc = 1 - c if i else c
-                got[q].push(
+                (across if q == 2 else sides).push(
                     src.at[lo:hi, :, pl.ds(pl.multiple_of(256 * cc, 128), 256)],
                     dst.at[lo:hi, z, yy, c],
                     dev(zk(q) if q else z, y, cc, r),
-                    when,
+                    ends if q == 2 else None,
                 )
-        return got, lo, hi, yy
+        return sides, across, lo, hi, yy
 
     def task_relay(state, dst):
-        got, lo, hi, yy = state
-        wait([got[0], got[1], got[3]])
+        sides, across, lo, hi, yy = state
+        wait([sides])
         hand = ln.push(dst.at[lo:hi, 3 - z, yy], dst.at[lo:hi, 3 - z, yy], far_end, inner)
-        return got, hand
+        return across, hand
 
     def task_ready(state):
-        got, hand = state
-        wait([got[2]], inner)
+        across, hand = state
+        wait([across], inner)
         wait([hand], ends)
 
     def plane_start(n):
@@ -978,11 +1007,13 @@
     def reduce_plane(n):
         plane_end(n, plane_start(n))
 
-    def reduce_line(n):
+    def reduce_line(n, bulk=None):
         sm, t, az = (getattr(s, p + str(n)) for p in ("as", "at", "az"))
         two = ln.group(lambda: az)
         for q in (1, 2, 3):
             two.push(sm, az.at[q - 1], dev(zk(q), y, c, r))
+        if bulk is not None:
+            bulk()
         wait([two])
         t[...] = (sm[...] + az[0]) + (az[1] + az[2])
         return t[...]
@@ -994,8 +1025,8 @@
         squares = jnp.sum(v * pre, axis=0, keepdims=True)
         return sums, squares
 
-    def norm_terms(n, bnp, width):
-        t = reduce_line(n)
+    def norm_terms(n, bnp, width, bulk=None):
+        t = reduce_line(n, bulk)
         if width == 256:
             rows = [t[i : i + 1] for i in range(4)]
         else:
@@ -1047,15 +1078,17 @@
     s.pre1[...] = pre
     first_sum, first_sq = stats_of(pre, 256, None)
     put_stats(0, first_sum, first_sq, 256, 0)
+    plane_one = plane_start(0)
+    line_sides(go_wm, at_wm)
     cores_wm = line_last(go_wm, at_wm, col_wm)
-    reduce_plane(0)
-    go_wl = (got_wl, [ln.push(at_wl(z), at_wl(z), ypeer)])
-    go_wr = (got_wr, [ln.push(s.reduce, at_wr(z), ypeer, odd)])
+    plane_end(0, plane_one)
+    line_y(go_wl, at_wl(z), at_wl, lambda: s.wl.at[:, 0, 0])
     pl.when(odd)(red_local.wait)
     line_relay(go_wl, at_wl)
     line_relay(go_wr, at_wr, odd)
-    norm_terms(0, s.bnp1, 256)
-    heads_a = task_push(s.heads.at[y], s.wh, 0, 5, False)
+    line_sides(go_wl, at_wl)
+    heads = []
+    norm_terms(0, s.bnp1, 256, lambda: heads.append(task_push(s.heads.at[y], s.wh, 0, 9, False)))
 
     def act_from(prebuf, bnp, dst):
         def step(base):
@@ -1068,37 +1101,50 @@
     a1_x = ln.push(s.a1.at[:, pl.ds(half, 256)], s.a1.at[:, pl.ds(half, 256)], xpeer)
     line_core(go_wm, col_wm, cores_wm)
     cores_wl = line_last(go_wl, at_wl, col_wl)
-    cores_wr = line_last(go_wr, at_wr, col_wr, odd)
+    over_h = ln.push(s.heads.at[1 - y], s.st_h, ypeer)
     wait(cores_wm)
     wait([a1_x])
+    wfo_x.push(s.wf.at[2], s.wfo.at[2], xpeer)
     spread(s.a1, s.a3, 1, 512)
     pre = conv_rows(s.a3, s.wm, 0)
     s.pre2[...] = pre
     first_sum, first_sq = stats_of(pre, 256, None)
     put_stats(1, first_sum, first_sq, 256, 1)
     reduce_plane(1)
-    over_h = ln.push(s.heads.at[1 - y], s.st_h, ypeer)
-    norm_terms(1, s.bnp2, 256)
-    relay_a = task_relay(heads_a, s.wh)
-    heads_b = task_push(s.heads.at[y], s.wh, 5, 9, False)
+    line_y(go_wr, s.reduce, at_wr, lambda: s.wr.at[:, 0], odd)
+    line_sides(go_wr, at_wr, odd)
+    cores_wr = line_last(go_wr, at_wr, col_wr, odd)
+    relayed_h = []
+
+    def bulk_two():
+        relayed_h.append(task_relay(heads[0], s.wh))
+        wait([over_h])
+        heads.append(task_push(s.st_h, s.wh, 0, 5, True))
+
+    norm_terms(1, s.bnp2, 256, bulk_two)
     act_from(s.pre2, s.bnp2, s.a2)
     a2_x = ln.push(s.a2.at[:, pl.ds(half, 256)], s.a2.at[:, pl.ds(half, 256)], xpeer)
     line_core(go_wl, col_wl, cores_wl)
-    line_core(go_wr, col_wr, cores_wr, odd)
     wait(cores_wl)
     wait([a2_x])
+    wfo_x.push(s.wf.at[3], s.wfo.at[3], xpeer)
     pre = dot(s.a2[...], s.wl[...].reshape(512, 1024))
     s.pre3[...] = pre
     first_sum, first_sq = stats_of(pre, 1024, None)
     put_stats(2, first_sum, first_sq, 1024, 2)
     reduce_plane(2)
     over_m = ln.push(s.messages.at[1 - y], s.st_m, ypeer)
-    norm_terms(2, s.bnp3, 1024)
-    relay_b = task_relay(heads_b, s.wh)
-    wait([over_h])
+    mess = []
+
+    def mess_push(a, staged):
+        return task_push(s.st_m if staged else s.messages.at[y], s.wq, 3 * a, 3 * a + 3, staged)
+
+    def bulk_three():
+        heads.append(task_push(s.st_h, s.wh, 5, 9, True))
+        mess.extend([[mess_push(a, False)] for a in range(2)])
+
+    norm_terms(2, s.bnp3, 1024, bulk_three)
     staged_h = ln.near(s.st_h.at[:, :, pl.ds(fhalf, 256)], s.wh.at[:, z, 1 - y, c])
-    heads_d = task_push(s.st_h, s.wh, 0, 5, True)
-    heads_e = task_push(s.st_h, s.wh, 5, 9, True)
     gate_got = {}
     cls_got = ln.group(lambda: s.wc.at[0:15])
     for q in range(4):
@@ -1127,6 +1173,8 @@
         s.blk[pl.ds(base, 32), :] = (gelu_of(v) * mask_at(base, 32, 1024)).astype(BF16)
 
     rows_loop(320, 32, block_step)
+    relayed_h.append(task_relay(heads[1], s.wh))
+    line_core(go_wr, col_wr, cores_wr, odd)
     wait(cores_wr, jnp.logical_not(odd))
     wred = s.wr[...].reshape(1024, 512)
     s.rps[...] = dot(s.blk[pl.ds(other_rows, 160), :], wred).astype(BF16)
@@ -1157,8 +1205,12 @@
     wait([g_xy, g_yx])
     bd = block_of(1 - r, 1 - y, c)
     g_c3 = ln.push(bd, bd, core)
-    relay_d = task_relay(heads_d, s.wh)
-    wfo_x = ln.push(s.wf, s.wfo, xpeer)
+    relayed_h.append(task_relay(heads[2], s.wh))
+    wait([over_m])
+    staged_m = ln.near(s.st_m.at[:, :, pl.ds(fhalf, 256)], s.wq.at[:, z, 1 - y, c])
+    mess[0].append(mess_push(0, True))
+    mess[1].append(mess_push(1, True))
+    mess.append([mess_push(2, False)])
     wait([g_c, g_c1, g_c2, g_c3])
 
     near_end = dev(jnp.where(z == 0, 1, 2), y, c, r)
@@ -1202,17 +1254,7 @@
 
     def tasks(r3, f3, d3, preh, dfull):
         spread(s.rbuf, r3, 4, 512)
-        relay_e = task_relay(heads_e, s.wh)
-        wait([over_m])
-        staged_m = ln.near(s.st_m.at[:, :, pl.ds(fhalf, 256)], s.wq.at[:, z, 1 - y, c])
-
-        def mess_push(a):
-            return [
-                task_push(s.st_m if staged else s.messages.at[y], s.wq, 3 * a, 3 * a + 3, staged) for staged in (False, True)
-            ]
-
-        mess = [mess_push(0), mess_push(1)]
-        for part in (relay_a, relay_b, relay_d, relay_e):
+        for part in relayed_h:
             task_ready(part)
         staged_h.wait()
 
@@ -1235,16 +1277,32 @@
         def seven():
             return s.dmg.at[0:1120]
 
-        def to_owners(src, dst_of, when):
-            got = {}
-            for o in offsets:
-                rr, yy, cc = peer(*o)
-                got[o] = ln.push(
-                    src.at[pl.ds(px_of(rr, yy, cc), 160)], dst_of().at[:, pl.ds(fhalf, 256)], dev(z, yy, cc, rr), when
-                )
+        def pieces(n):
+            return lambda: s.dmg.at[0 : 160 * n]
+
+        even = [o for o in offsets if (o[0] + o[1]) % 2 == 0]
+        uneven = [o for o in offsets if (o[0] + o[1]) % 2]
+
+        def to_owners(src, dst_of):
+            got = [ln.group(pieces(len(o)), special) for o in (even, uneven)]
+            for g, group in zip(got, (even, uneven)):
+                for o in group:
+                    rr, yy, cc = peer(*o)
+                    g.push(src.at[pl.ds(px_of(rr, yy, cc), 160)], dst_of().at[:, pl.ds(fhalf, 256)], dev(z, yy, cc, rr), special)
             return got
 
-        f_own = to_owners(s.fown, lambda: s.fg.at[r, 0], special)
+        def from_tasks(got):
+            wait([got[0]], special)
+            wait([got[1]], plain)
+
+        def to_tasks(src_of, dst):
+            got = [ln.group(pieces(len(o)), w) for o, w in ((even, special), (uneven, plain))]
+            for g, group, w in zip(got, (even, uneven), (special, plain)):
+                for o in group:
+                    rr, yy, cc = peer(*o)
+                    ll = pl.ds(pl.multiple_of(256 * cc, 128), 256)
+                    g.push(src_of(rr).at[:, ll], dst.at[pl.ds(own_px, 160)], dev(z, yy, cc, rr), w)
+            return got
 
         def keep(dst, src):
             def run():
@@ -1270,10 +1328,12 @@
 
             rows_loop(1280, 320, gate_step)
 
-        g_own = to_owners(s.gateb, lambda: s.fg.at[r, 1], special)
+        g_own = to_owners(s.gateb, lambda: s.fg.at[r, 1])
         pl.when(special)(keep(s.fg.at[r, 1], s.gateb))
+        f_own = to_owners(s.fown, lambda: s.fg.at[r, 0])
+
         relayed = [[task_relay(p, s.wq) for p in mess[0]]]
-        mess.append(mess_push(2))
+        mess[2].append(mess_push(2, True))
         spread(s.ffull, f3, 4, 512)
 
         wait([cls_got])
@@ -1282,8 +1342,7 @@
             s.ctf[0:40, 0:80] = s.cct[i].astype(F32)
             turned = s.ctf[...].T
             s.ccotv[80 * i : 80 * i + 80, :] = turned[0:80, :].astype(BF16)
-        for o in offsets:
-            wait([g_own[o]], (r != y) if (o[0] + o[1]) % 2 else special)
+        from_tasks(g_own)
 
         def early_step(base):
             rows = pl.ds(base, 32)
@@ -1308,11 +1367,7 @@
             rr, yy, cc = peer(*o)
             ll = pl.ds(pl.multiple_of(256 * cc, 128), 256)
             d_got.push(s.dm.at[2 * rr + yy, :, ll], s.dmg.at[pl.ds(own_px, 160)], dev(z, yy, cc, rr))
-        u_got = {}
-        for o in offsets:
-            rr, yy, cc = peer(*o)
-            ll = pl.ds(pl.multiple_of(256 * cc, 128), 256)
-            u_got[o] = ln.push(s.eu.at[rr, :, ll], s.exg.at[0, pl.ds(own_px, 160)], dev(z, yy, cc, rr), rr == yy)
+        u_got = to_tasks(lambda rr: s.eu.at[rr], s.exg.at[0])
         s.dmg[pl.ds(own_px, 160), :] = s.dm[task, :, pl.ds(fhalf, 256)]
 
         @pl.when(special)
@@ -1324,14 +1379,14 @@
             s.exg[0] = jnp.zeros(s.exg.shape[1:], BF16)
 
         relayed.append([task_relay(p, s.wq) for p in mess[1]])
+        relayed.append([task_relay(p, s.wq) for p in mess[2]])
         wait([d_got])
         spread(s.dmg, d3, 4, 256)
         conv_weight(f3, d3, s.gm, 4, 0, 9)
         staged_m.wait()
         gm_z = []
         for a in range(3):
-            if a == 2:
-                relayed.append([task_relay(p, s.wq) for p in mess[2]])
+            if a == 0:
                 for part in range(3):
                     gm_z.append(grad_push(0, s.gm, s.rm, 3 * part, 3 * part + 3))
             for p in relayed[a]:
@@ -1364,8 +1419,7 @@
 
         lax.fori_loop(0, 4, back_step, 0)
 
-        for o in offsets:
-            wait([f_own[o]], (r != y) if (o[0] + o[1]) % 2 else special)
+        from_tasks(f_own)
         wait([m_own])
 
         def stream_step(base):
@@ -1385,11 +1439,7 @@
             s.fg[1, 1, rows, :] = (dmer * sc * gc * (1.0 - gc)).astype(BF16)
 
         rows_loop(160, 32, stream_step)
-        e_got = {}
-        for o in offsets:
-            rr, yy, cc = peer(*o)
-            ll = pl.ds(pl.multiple_of(256 * cc, 128), 256)
-            e_got[o] = ln.push(s.fg.at[rr, 1, :, ll], s.exg.at[1, pl.ds(own_px, 160)], dev(z, yy, cc, rr), rr == yy)
+        e_got = to_tasks(lambda rr: s.fg.at[rr, 1], s.exg.at[1])
 
         @pl.when(special)
         def _():
@@ -1402,8 +1452,8 @@
             s.olt[i] = turned[0:40, 0:80].astype(BF16)
         out_near = [ln.near(s.ods, s.o_depth), ln.near(s.olt, s.o_logits)]
         s.gcls[...] = dot_first(s.mrg[...], s.ccotv[...]).astype(BF16).reshape(16, 32, 128)
-        wait([u_got[o] for o in offsets], special)
-        wait([e_got[o] for o in offsets], special)
+        grad_hop(gm_z[0])
+        wait(u_got + e_got, special)
 
         @pl.when(special)
         def _():
@@ -1460,6 +1510,7 @@
             src = pl.multiple_of(320 * (2 * yy) + 320 * (1 - c), 16)
             s.drs[pl.ds(320 * yy, 320), :] = dfull[pl.ds(src, 320), :].astype(BF16)
         dr_c = ln.push(s.drs, s.drr, core)
+        grad_hop(gm_z[1])
         wait([dr_c])
         for yy in range(2):
             src = pl.multiple_of(320 * (2 * yy) + 320 * c, 16)
@@ -1471,11 +1522,9 @@
             src = s.drr.at[pl.ds(pl.multiple_of(320 * yy + 160 * rr, 16), 160)]
             ro.append(ln.push(src, s.dro.at[len(ro)], dev(z, yy, c, rr)))
         gh_z = []
-        conv_weight(r3, d3, s.gh, 4, 0, 2)
-        grad_hop(gm_z[0])
-        gh_z.append(grad_push(1, s.gh, s.rh, 0, 2))
-        conv_weight(r3, d3, s.gh, 4, 2, 9)
-        grad_hop(gm_z[1])
+        conv_weight(r3, d3, s.gh, 4, 0, 3)
+        gh_z.append(grad_push(1, s.gh, s.rh, 0, 3))
+        conv_weight(r3, d3, s.gh, 4, 3, 9)
         wait(ro)
         keep_rows = pl.ds(pl.multiple_of(320 * y + 160 * r, 16), 160)
         total_red = s.drr[keep_rows, :].astype(F32)
@@ -1529,14 +1578,44 @@
                 mine_y = rc[t, :, y] if lead else rc[t, y]
                 ry[t] = (ry[t].astype(F32) + mine_y.astype(F32)).astype(BF16)
 
-        def to_z(ry, rz, lead):
-            return [
-                ln.push(ry.at[:, zk(k)] if lead else ry.at[zk(k)], rz.at[k - 1], dev(zk(k), y, c, r)) for k in (1, 2, 3)
-            ]
-
-        def add_z(ry, rz, fin, lead):
+        def to_z(ry, rz, lead, when=None, hop=None):
+            def part(zz):
+                return ry.at[:, zz] if lead else ry.at[zz]
+
+            got = {}
+            for q in (1, 2, 3):
+                direct = None if hop is None else {1: not_last, 2: ends, 3: not_first}[q]
+                got[q] = ln.push(part(zk(q)), rz.at[q - 1], dev(zk(q), y, c, r), both(when, direct))
+            if hop is not None:
+                got[0] = ln.push(part(3 - z), hop, near_end, both(when, ends))
+            return got, part, rz, hop, when
+
+        def hop_z(state):
+            got, part, rz, hop, when = state
+
+            def add():
+                got[0].wait_recv()
+                hop[...] = (hop[...].astype(F32) + part(jnp.where(z == 1, 3, 0))[...].astype(F32)).astype(BF16)
+
+            pl.when(both(when, inner))(add)
+            got[4] = ln.push(hop, rz.at[1], other_end, both(when, inner))
+
+        def wait_z(state):
+            got, _, _, hop, when = state
+            if hop is None:
+                wait([got[1], got[2], got[3]], when)
+            else:
+                wait([got[1]], both(when, not_first))
+                wait([got[3]], both(when, not_last))
+                wait([got[2]], both(when, inner))
+                wait([got[4]], both(when, ends))
+
+        def add_z(ry, rz, fin, lead, hop=True):
             mine_z = (ry[:, z] if lead else ry[z]).astype(F32)
-            fin[...] = ((mine_z + rz[0].astype(F32)) + (rz[1].astype(F32) + rz[2].astype(F32))).astype(BF16)
+            v0, v2 = rz[0].astype(F32), rz[2].astype(F32)
+            if hop:
+                v0, v2 = jnp.where(z == 0, 0.0, v0), jnp.where(z == 3, 0.0, v2)
+            fin[...] = ((mine_z + v0) + (rz[1].astype(F32) + v2)).astype(BF16)
 
         def task_out(states, rm, g, ps, out):
             for part in states:
@@ -1578,12 +1657,11 @@
         put_stats(3, su, sux, 1024, None)
         ar3 = plane_start(3)
         ds_x = ln.push(s.dsum.at[pl.ds(other_rows, 160)], s.dsr, xpeer)
+        grad_hop(gm_z[2])
         gr[...] = dot_first(s.blk[...], s.dred[...]).astype(BF16).reshape(gr.shape)
         gr_c = ln.push(gr, s.rcr, core, jnp.logical_not(odd))
         plane_end(3, ar3)
-        grad_hop(gm_z[2])
-        t = reduce_line(3)
-        gh_z.append(grad_push(1, s.gh, s.rh, 2, 5))
+        t = reduce_line(3, lambda: gh_z.append(grad_push(1, s.gh, s.rh, 3, 6)))
         gs3 = ln.push(s.at3, s.o_gs3.at[r], xpeer)
         gs3n = ln.near(s.at3, s.o_gs3.at[r])
         mu = jnp.concatenate([t[0:1], t[1:2]], axis=1) / count
@@ -1613,10 +1691,9 @@
             for q in range(4):
                 s.rcr[q] = (s.rcr[q].astype(F32) + gr[q].astype(F32)).astype(BF16)
 
-        later = {}
+        later = {"gr_y": ln.push(s.rcr.at[:, 1 - y], s.ryr, ypeer, odd)}
 
         def after_plane_two():
-            later["gr_y"] = ln.push(s.rcr.at[:, 1 - y], s.ryr, ypeer, odd)
             wait([gl_c])
             add_core(gl, s.rcl, False)
             later["gl_y"] = to_y(s.rcl, s.ryl, False)
@@ -1624,7 +1701,9 @@
         def after_plane_one():
             wait([gq_c])
             add_core(gq, s.rcm, True)
-            later["gq_y"] = to_y(s.rcm, s.rym, True)
+            later["gq_y"] = [
+                ln.push(s.rcm.at[3 * a : 3 * a + 3, :, 1 - y], s.rym.at[3 * a : 3 * a + 3], ypeer) for a in range(3)
+            ]
 
         wait([pa2])
 
@@ -1645,8 +1724,7 @@
             put_stats(n, su_, sux_, 256, None)
             reduce_plane(n)
             middle()
-            t_ = reduce_line(n)
-            after()
+            t_ = reduce_line(n, after)
             gsx = ln.push(getattr(s, "at%d" % n), out_gs.at[r], xpeer)
             gsn = ln.near(getattr(s, "at%d" % n), out_gs.at[r])
             mu_, mux_ = t_[0:1] / count, t_[1:2] / count
@@ -1662,12 +1740,22 @@
 
         def window_two():
             grad_hop(gh_z[0])
-            gh_z.append(grad_push(1, s.gh, s.rh, 5, 8))
+            gh_z.append(grad_push(1, s.gh, s.rh, 6, 9))
+            later["mess"] = task_out(gm_z, s.rm, s.gm, s.psm, s.o_mess)
+
+        def window_one():
             grad_hop(gh_z[1])
-
-        def window_one():
-            gh_z.append(grad_push(1, s.gh, s.rh, 8, 9))
-            grad_hop(gh_z[2])
+            wait([later["gr_y"]], odd)
+
+            @pl.when(odd)
+            def _():
+                for q in range(4):
+                    s.ryr[q] = (s.ryr[q].astype(F32) + s.rcr[q, y].astype(F32)).astype(BF16)
+
+            later["gr_z"] = to_z(s.ryr, s.rzr, False, odd, s.hpr)
+            wait([later["gl_y"]])
+            add_y(s.rcl, s.ryl, False)
+            later["gl_z"] = to_z(s.ryl, s.rzl, False, None, s.hpl)
 
         gs2, gs2n = norm_back(4, s.par2, s.pre2, s.bnp2, s.dp2, s.o_gs2, after_plane_two, window_two)
         spread(s.dp2, s.d3m, 1, 256)
@@ -1684,24 +1772,21 @@
         wait([gf_c])
         add_core(gf, s.rcf, False)
         gf_y = to_y(s.rcf, s.ryf, False)
-        gr_y, gl_y, gq_y = later["gr_y"], later["gl_y"], later["gq_y"]
-        ms, mn = task_out(gm_z, s.rm, s.gm, s.psm, s.o_mess)
-
-        wait([gr_y], odd)
-
-        @pl.when(odd)
-        def _():
-            for q in range(4):
-                s.ryr[q] = (s.ryr[q].astype(F32) + s.rcr[q, y].astype(F32)).astype(BF16)
-
-        grad_hop(gh_z[3])
-        gr_z = [ln.push(s.ryr.at[zk(q)], s.rzr.at[q - 1], dev(zk(q), y, c, r), odd) for q in (1, 2, 3)]
-        wait([gl_y])
-        add_y(s.rcl, s.ryl, False)
-        gl_z = to_z(s.ryl, s.rzl, False)
-        wait([gq_y])
-        add_y(s.rcm, s.rym, True)
-        gq_z = to_z(s.rym, s.rzm, True)
+        ms, mn = later["mess"]
+        gr_z, gl_z = later["gr_z"], later["gl_z"]
+        grad_hop(gh_z[2])
+        gq_z = []
+        for a in range(3):
+            wait([later["gq_y"][a]])
+            for t in range(3 * a, 3 * a + 3):
+                s.rym[t] = (s.rym[t].astype(F32) + s.rcm[t, :, y].astype(F32)).astype(BF16)
+            g = ln.group(lambda a=a: s.rzm.at[:, 3 * a : 3 * a + 3])
+            for q in (1, 2, 3):
+                g.push(s.rym.at[3 * a : 3 * a + 3, zk(q)], s.rzm.at[q - 1, 3 * a : 3 * a + 3], dev(zk(q), y, c, r))
+            gq_z.append(g)
+            if a == 0:
+                hop_z(gr_z)
+                hop_z(gl_z)
         wait([gf_y])
         add_y(s.rcf, s.ryf, False)
         gf_z = to_z(s.ryf, s.rzf, False)
@@ -1744,10 +1829,12 @@
             v = (s.gg[z].astype(F32) + s.rg[0].astype(F32)) + (s.rg[1].astype(F32) + s.rg[2].astype(F32))
             s.pg[...] = v.astype(BF16)
 
-        gx = {}
-        for o in offsets:
-            rr, yy, cc = peer(*o)
-            gx[o] = ln.push(s.pg.at[yy, cc], s.o_gates.at[r, :, pl.ds(fhalf, 256)], dev(z, yy, cc, rr), special)
+        gx = [ln.group(lambda n=n: s.wg.at[0:3, 0, 0] if n == 3 else s.wg.at[0:4, 0, 0], special) for n in (3, 4)]
+        for g, odd_one in zip(gx, (0, 1)):
+            for o in offsets:
+                if (o[0] + o[1]) % 2 == odd_one:
+                    rr, yy, cc = peer(*o)
+                    g.push(s.pg.at[yy, cc], s.o_gates.at[r, :, pl.ds(fhalf, 256)], dev(z, yy, cc, rr), special)
         gate_near = pltpu.make_async_copy(
             s.pg.at[y, c], s.o_gates.at[r, :, pl.ds(fhalf, 256)], s.near_sems.at[NEAR - 2]
         )
@@ -1760,26 +1847,21 @@
         s.clss[...] = v
         cls_x = ln.push(s.clss, s.clsr, xpeer)
 
-        wait(gr_z, odd)
-
-        @pl.when(odd)
-        def _():
-            v_ = s.ryr[z].astype(F32) + s.rzr[0].astype(F32)
-            s.fnr[...] = (v_ + (s.rzr[1].astype(F32) + s.rzr[2].astype(F32))).astype(BF16)
-
+        wait_z(gr_z)
+        pl.when(odd)(lambda: add_z(s.ryr, s.rzr, s.fnr, False))
         gr_x = ln.push(s.fnr, s.o_red, xpeer, odd)
         red_near = pltpu.make_async_copy(s.fnr, s.o_red, s.near_sems.at[NEAR - 3])
         pl.when(odd)(red_near.start)
-        wait(gl_z)
+        wait_z(gl_z)
         add_z(s.ryl, s.rzl, s.fnl, False)
         gl_x = ln.push(s.fnl, s.o_last.at[r], xpeer)
         n1 = ln.near(s.fnl, s.o_last.at[r])
         wait(gq_z)
-        add_z(s.rym, s.rzm, s.fnm, True)
+        add_z(s.rym, s.rzm, s.fnm, True, False)
         gq_x = ln.push(s.fnm, s.o_mid.at[:, :, pl.ds(half, 256)], xpeer)
         n2 = ln.near(s.fnm, s.o_mid.at[:, :, pl.ds(half, 256)])
-        wait(gf_z)
-        add_z(s.ryf, s.rzf, s.fnf, False)
+        wait_z(gf_z)
+        add_z(s.ryf, s.rzf, s.fnf, False, False)
         gf_x = ln.push(s.fnf, s.o_first.at[:, pl.ds(half, 256)], xpeer)
         n3 = ln.near(s.fnf, s.o_first.at[:, pl.ds(half, 256)])
         wait([cls_x])
@@ -1788,8 +1870,8 @@
         wait([gr_x], jnp.logical_not(odd))
         wait([gl_x, gq_x, gf_x, gs1, gs2, gs3])
         wait(ms + hs)
-        for o in offsets:
-            wait([gx[o]], (r != y) if (o[0] + o[1]) % 2 else special)
+        wait([gx[0]], special)
+        wait([gx[1]], plain)
         pl.when(special)(gate_near.wait)
         pl.when(odd)(red_near.wait)
         for cp in (gs1n, gs2n, gs3n, img_n, mn, hn, n1, n2, n3, n4):
@@ -1924,7 +2006,7 @@
         in_specs=[spec.get(n, hbm) for n in INS],
         out_specs=[hbm] * len(OUTS),
         scratch_shapes=[pltpu.VMEM(*v) for v in SHAPES.values()]
-        + [pltpu.SemaphoreType.DMA((n,)) for n in (SENDS, SENDS, NEAR)],
+        + [pltpu.SemaphoreType.DMA((n,)) for n in (SENDS, RECVS, NEAR)],
         compiler_params=pltpu.CompilerParams(has_side_effects=True, collective_id=0, vmem_limit_bytes=64 * 2**20),
         name="residual_distill",
     )(*ins)

time: 287 us -> 271 us (0.944)
  Pallas kernels: 283 us -> 267 us
    pallas_call x1, Pallas kernels: 276 us -> 260 us  [fast(): pl.pallas_call(functools.partial(body, names), out_shape=[jax.ShapeDtypeS...]
where the time goes in v4:
time: 271 us; the launch traced here: 270 us
  Pallas kernels  267 us (99%)
    pallas_call x1, Pallas kernels, fast(): pl.pallas_call(functools.partial(body, names), out_shape=[jax.ShapeDtypeS...  260 us
    pallas_call x1, Pallas kernels, fast(): pl.pallas_call(functools.partial(widen_out, taken + list(FINAL) + list(st...  7.11 us

profile of v4, /device:TPU:0, one launch (start us, length us, event | category | flops | bytes accessed | tf_op | source)
XLA Modules:
  0.0 269.6 jit_solution(18294074497077037121)
XLA Ops:
  0.7 0.8 maximum_bitcast_fusion
  1.4 1.3 maximum_convert_fusion.refs_11_
  2.7 259.6 %residual_distill.1 = (bf16[160,512]{1,0:T(8,128)(2,1)}, bf16[2,40,80]{2,1,0:T(8,128)(2,1)}, bf16[160,2048]{1,0:T(8,128)(2,1)}, bf16[128,512]{1,0:T(8,128)(2,1)}...) custom-call(s32[16]{0:T(128)} %refs_0_.1, ...), custom_call_target="tpu_custom_call" | custom-call | tf_op jit(solution)/shard_map/residual_distill/pallas_call | solution.py:2003
  262.3 7.1 %widen_out.1 = (bf16[160,512]{1,0:T(8,128)(2,1)}, bf16[2,40,80]{2,1,0:T(8,128)(2,1)}, f32[160,2048]{1,0:T(8,128)}, f32[128,512]{1,0:T(8,128)}, f32[1,32]{1,0:T(1...) custom-call(bf16[160,512]{1,0:T(8,128)(2,1)} %get-tuple-element.48.r, ...), custom_call_target="tpu_custom_call" | custom-call | tf_op jit(solution)/shard_map/widen_out/pallas_call | solution.py:2017

commit v5 on v4

--- a/solution.py
+++ b/solution.py
@@ -15,8 +15,8 @@
 BF16 = jnp.bfloat16
 ROOT = 0.7978845608028654
 CUBE = 0.044715
-SENDS = 118
-RECVS = 183
+SENDS = 121
+RECVS = 196
 NEAR = 21
 
 
@@ -606,6 +606,8 @@
     )
 
 
+BEHIND = (0, 1, 2, 3, 4, 5, )
+
 SHAPES = dict(
     wf=((4, 2, 2, 128, 256), BF16),
     wm=((9, 4, 2, 2, 32, 256), BF16),
@@ -613,6 +615,7 @@
     wr=((4, 2, 128, 512), BF16),
     wc=((16, 32, 128), BF16),
     wcs=((32, 128), BF16),
+    gains=((8, 128), F32),
     wcv=((32, 40), BF16),
     cct=((2, 40, 80), BF16),
     ctf=((128, 128), F32),
@@ -676,6 +679,7 @@
     ryr=((4, 128, 512), BF16),
     hpr=((128, 512), BF16),
     hpl=((32, 1024), BF16),
+    hpm=((9, 32, 256), BF16),
     ryl=((4, 32, 1024), BF16),
     rym=((9, 4, 32, 256), BF16),
     ryf=((4, 128, 256), BF16),
@@ -693,7 +697,7 @@
 
 INS = (
     "crop_h", "crop_w", "images", "first", "middle", "last", "reduce", "gates",
-    "classes", "heads", "messages", "gains", "dcot", "ccot",
+    "classes", "heads", "messages", "gain1", "shift1", "gain2", "shift2", "gain3", "shift3", "dcot", "ccot",
 )
 OUTS = dict(
     o_depth=((160, 512), BF16),
@@ -915,8 +919,6 @@
     line_y(go_wm, src_wm, at_wm, lambda: s.wm.at[:, :, 0, 0])
     for cp in near_last:
         cp.wait()
-    go_wl = line_start(at_wl(z), at_wl, lambda: s.wl.at[0, 0])
-    go_wr = line_start(s.reduce, at_wr, lambda: s.wr.at[0], odd)
 
     for i in range(4):
         high, wide = s.crop_h[4 * z + i], s.crop_w[4 * z + i]
@@ -933,6 +935,11 @@
     def mask_at(base, rows, width):
         return lanes(s.maskp[pl.ds(mine + base, rows), :], width)
 
+    s.gains[...] = jnp.zeros((8, 128), F32)
+    for i, ref in enumerate((s.gain1, s.shift1, s.gain2, s.shift2)):
+        s.gains[i : i + 1, 0:32] = ref[...].astype(F32)
+    s.gains[4:5, :] = s.gain3[...].astype(F32)
+    s.gains[5:6, :] = s.shift3[...].astype(F32)
     near_cls.wait()
     s.wcs[...] = jnp.zeros(s.wcs.shape, BF16)
     s.wcs[:, 0:40] = s.wcv[...]
@@ -944,6 +951,7 @@
     cores_wf = line_last(go_wf, at_wf, col_wf)
     near_wm.wait()
     line_relay(go_wm, at_wm)
+    go_wl = line_start(at_wl(z), at_wl, lambda: s.wl.at[0, 0])
     line_core(go_wf, col_wf, cores_wf)
     wait([img_x])
 
@@ -1012,9 +1020,11 @@
         two = ln.group(lambda: az)
         for q in (1, 2, 3):
             two.push(sm, az.at[q - 1], dev(zk(q), y, c, r))
-        if bulk is not None:
+        if bulk is not None and n in BEHIND:
             bulk()
         wait([two])
+        if bulk is not None and n not in BEHIND:
+            bulk()
         t[...] = (sm[...] + az[0]) + (az[1] + az[2])
         return t[...]
 
@@ -1043,12 +1053,12 @@
         out = []
         for p in range(2):
             if n < 2:
-                v = jnp.broadcast_to(s.gains[0:1, :], (8, 128))
-                v = pltpu.roll(v, lax.rem(spot + 128 - 32 * (2 * n + p), np.int32(128)), 1)
+                v = jnp.broadcast_to(s.gains[2 * n + p : 2 * n + p + 1, :], (8, 128))
+                v = pltpu.roll(v, spot, 1)
                 v = jnp.where((lane >= spot) & (lane < spot + 32), v, 0.0)
                 out.append(jnp.concatenate([jnp.where(quarter == 2 * r + i, v[0:1], 0.0) for i in range(2)], axis=1))
             else:
-                v = s.gains[1 + p : 2 + p, :]
+                v = s.gains[4 + p : 5 + p, :]
                 out.append(
                     [
                         jnp.concatenate(
@@ -1084,11 +1094,17 @@
     plane_end(0, plane_one)
     line_y(go_wl, at_wl(z), at_wl, lambda: s.wl.at[:, 0, 0])
     pl.when(odd)(red_local.wait)
-    line_relay(go_wl, at_wl)
-    line_relay(go_wr, at_wr, odd)
-    line_sides(go_wl, at_wl)
     heads = []
-    norm_terms(0, s.bnp1, 256, lambda: heads.append(task_push(s.heads.at[y], s.wh, 0, 9, False)))
+    late_wr = []
+
+    def bulk_one():
+        line_relay(go_wl, at_wl)
+        line_sides(go_wl, at_wl)
+        late_wr.append(line_start(s.reduce, at_wr, lambda: s.wr.at[0], odd))
+        heads.append(task_push(s.heads.at[y], s.wh, 0, 7, False))
+
+    norm_terms(0, s.bnp1, 256, bulk_one)
+    go_wr = late_wr[0]
 
     def act_from(prebuf, bnp, dst):
         def step(base):
@@ -1101,7 +1117,6 @@
     a1_x = ln.push(s.a1.at[:, pl.ds(half, 256)], s.a1.at[:, pl.ds(half, 256)], xpeer)
     line_core(go_wm, col_wm, cores_wm)
     cores_wl = line_last(go_wl, at_wl, col_wl)
-    over_h = ln.push(s.heads.at[1 - y], s.st_h, ypeer)
     wait(cores_wm)
     wait([a1_x])
     wfo_x.push(s.wf.at[2], s.wfo.at[2], xpeer)
@@ -1110,21 +1125,28 @@
     s.pre2[...] = pre
     first_sum, first_sq = stats_of(pre, 256, None)
     put_stats(1, first_sum, first_sq, 256, 1)
-    reduce_plane(1)
+    plane_two = plane_start(1)
+    over_h = ln.push(s.heads.at[1 - y], s.st_h, ypeer)
+    plane_end(1, plane_two)
+    relayed_h = []
+    mess = []
+
+    def mess_push(a, staged):
+        return task_push(s.st_m if staged else s.messages.at[y], s.wq, 3 * a, 3 * a + 3, staged)
+
+    def bulk_two():
+        line_relay(go_wr, at_wr, odd)
+        relayed_h.append(task_relay(heads[0], s.wh))
+        heads.append(task_push(s.heads.at[y], s.wh, 7, 9, False))
+        mess.append([mess_push(0, False)])
+
+    norm_terms(1, s.bnp2, 256, bulk_two)
     line_y(go_wr, s.reduce, at_wr, lambda: s.wr.at[:, 0], odd)
     line_sides(go_wr, at_wr, odd)
-    cores_wr = line_last(go_wr, at_wr, col_wr, odd)
-    relayed_h = []
-
-    def bulk_two():
-        relayed_h.append(task_relay(heads[0], s.wh))
-        wait([over_h])
-        heads.append(task_push(s.st_h, s.wh, 0, 5, True))
-
-    norm_terms(1, s.bnp2, 256, bulk_two)
     act_from(s.pre2, s.bnp2, s.a2)
     a2_x = ln.push(s.a2.at[:, pl.ds(half, 256)], s.a2.at[:, pl.ds(half, 256)], xpeer)
     line_core(go_wl, col_wl, cores_wl)
+    cores_wr = line_last(go_wr, at_wr, col_wr, odd)
     wait(cores_wl)
     wait([a2_x])
     wfo_x.push(s.wf.at[3], s.wfo.at[3], xpeer)
@@ -1132,17 +1154,15 @@
     s.pre3[...] = pre
     first_sum, first_sq = stats_of(pre, 1024, None)
     put_stats(2, first_sum, first_sq, 1024, 2)
-    reduce_plane(2)
+    plane_three = plane_start(2)
     over_m = ln.push(s.messages.at[1 - y], s.st_m, ypeer)
-    mess = []
-
-    def mess_push(a, staged):
-        return task_push(s.st_m if staged else s.messages.at[y], s.wq, 3 * a, 3 * a + 3, staged)
-
+    plane_end(2, plane_three)
     def bulk_three():
+        relayed_h.append(task_relay(heads[1], s.wh))
+        heads.append(task_push(s.st_h, s.wh, 0, 5, True))
         heads.append(task_push(s.st_h, s.wh, 5, 9, True))
-        mess.extend([[mess_push(a, False)] for a in range(2)])
-
+
+    wait([over_h])
     norm_terms(2, s.bnp3, 1024, bulk_three)
     staged_h = ln.near(s.st_h.at[:, :, pl.ds(fhalf, 256)], s.wh.at[:, z, 1 - y, c])
     gate_got = {}
@@ -1173,7 +1193,6 @@
         s.blk[pl.ds(base, 32), :] = (gelu_of(v) * mask_at(base, 32, 1024)).astype(BF16)
 
     rows_loop(320, 32, block_step)
-    relayed_h.append(task_relay(heads[1], s.wh))
     line_core(go_wr, col_wr, cores_wr, odd)
     wait(cores_wr, jnp.logical_not(odd))
     wred = s.wr[...].reshape(1024, 512)
@@ -1193,6 +1212,7 @@
     g_y = ln.push(own, own, ypeer)
     g_c = ln.push(own, own, core)
     wait([g_x])
+    relayed_h.append(task_relay(heads[2], s.wh))
     bx = block_of(1 - r, y, c, 0, 80)
     g_xy = ln.push(bx, bx, ypeer)
     wait([g_y])
@@ -1202,14 +1222,14 @@
     g_c1 = ln.push(bx, bx, core)
     by = block_of(r, 1 - y, c)
     g_c2 = ln.push(by, by, core)
+    relayed_h.append(task_relay(heads[3], s.wh))
     wait([g_xy, g_yx])
     bd = block_of(1 - r, 1 - y, c)
     g_c3 = ln.push(bd, bd, core)
-    relayed_h.append(task_relay(heads[2], s.wh))
     wait([over_m])
     staged_m = ln.near(s.st_m.at[:, :, pl.ds(fhalf, 256)], s.wq.at[:, z, 1 - y, c])
     mess[0].append(mess_push(0, True))
-    mess[1].append(mess_push(1, True))
+    mess.append([mess_push(1, False), mess_push(1, True)])
     mess.append([mess_push(2, False)])
     wait([g_c, g_c1, g_c2, g_c3])
 
@@ -1330,7 +1350,6 @@
 
         g_own = to_owners(s.gateb, lambda: s.fg.at[r, 1])
         pl.when(special)(keep(s.fg.at[r, 1], s.gateb))
-        f_own = to_owners(s.fown, lambda: s.fg.at[r, 0])
 
         relayed = [[task_relay(p, s.wq) for p in mess[0]]]
         mess[2].append(mess_push(2, True))
@@ -1367,7 +1386,6 @@
             rr, yy, cc = peer(*o)
             ll = pl.ds(pl.multiple_of(256 * cc, 128), 256)
             d_got.push(s.dm.at[2 * rr + yy, :, ll], s.dmg.at[pl.ds(own_px, 160)], dev(z, yy, cc, rr))
-        u_got = to_tasks(lambda rr: s.eu.at[rr], s.exg.at[0])
         s.dmg[pl.ds(own_px, 160), :] = s.dm[task, :, pl.ds(fhalf, 256)]
 
         @pl.when(special)
@@ -1379,20 +1397,12 @@
             s.exg[0] = jnp.zeros(s.exg.shape[1:], BF16)
 
         relayed.append([task_relay(p, s.wq) for p in mess[1]])
-        relayed.append([task_relay(p, s.wq) for p in mess[2]])
-        wait([d_got])
-        spread(s.dmg, d3, 4, 256)
-        conv_weight(f3, d3, s.gm, 4, 0, 9)
-        staged_m.wait()
-        gm_z = []
-        for a in range(3):
-            if a == 0:
-                for part in range(3):
-                    gm_z.append(grad_push(0, s.gm, s.rm, 3 * part, 3 * part + 3))
+
+        def mess_conv(a):
             for p in relayed[a]:
                 task_ready(p)
 
-            def mess_step(i, carry, a=a):
+            def mess_step(i, carry):
                 rows = pl.ds(pl.multiple_of(i * 320, 16), 320)
                 base = pl.multiple_of((5 * i + a) * 80, 16)
                 v = dot(f3[pl.ds(base, 320), :], s.wq[3 * a : 3 * a + 3].reshape(1536, 256))
@@ -1406,6 +1416,19 @@
 
             lax.fori_loop(0, 4, mess_step, 0)
 
+        staged_m.wait()
+        mess_conv(0)
+        wait([d_got])
+        f_own = to_owners(s.fown, lambda: s.fg.at[r, 0])
+        u_got = to_tasks(lambda rr: s.eu.at[rr], s.exg.at[0])
+        spread(s.dmg, d3, 4, 256)
+        conv_weight(f3, d3, s.gm, 4, 0, 6)
+        relayed.append([task_relay(p, s.wq) for p in mess[2]])
+        gm_z = [grad_push(0, s.gm, s.rm, 0, 3), grad_push(0, s.gm, s.rm, 3, 6)]
+        mess_conv(1)
+        conv_weight(f3, d3, s.gm, 4, 6, 9)
+        gm_z.append(grad_push(0, s.gm, s.rm, 6, 9))
+        mess_conv(2)
         m_own = ln.group(seven)
         for o in offsets:
             rr, yy, cc = peer(*o)
@@ -1723,8 +1746,12 @@
             su_, sux_ = lax.fori_loop(0, 4, u_step, (nil_, nil_))
             put_stats(n, su_, sux_, 256, None)
             reduce_plane(n)
-            middle()
-            t_ = reduce_line(n, after)
+
+            def bulk():
+                middle()
+                after()
+
+            t_ = reduce_line(n, bulk)
             gsx = ln.push(getattr(s, "at%d" % n), out_gs.at[r], xpeer)
             gsn = ln.near(getattr(s, "at%d" % n), out_gs.at[r])
             mu_, mux_ = t_[0:1] / count, t_[1:2] / count
@@ -1780,13 +1807,14 @@
             wait([later["gq_y"][a]])
             for t in range(3 * a, 3 * a + 3):
                 s.rym[t] = (s.rym[t].astype(F32) + s.rcm[t, :, y].astype(F32)).astype(BF16)
-            g = ln.group(lambda a=a: s.rzm.at[:, 3 * a : 3 * a + 3])
-            for q in (1, 2, 3):
-                g.push(s.rym.at[3 * a : 3 * a + 3, zk(q)], s.rzm.at[q - 1, 3 * a : 3 * a + 3], dev(zk(q), y, c, r))
-            gq_z.append(g)
+            lead = slice(3 * a, 3 * a + 3)
+            rz = SimpleNamespace(at=[s.rzm.at[q, lead] for q in range(3)])
+            gq_z.append(to_z(s.rym.at[lead], rz, True, None, s.hpm.at[lead] if a < 2 else None))
             if a == 0:
                 hop_z(gr_z)
                 hop_z(gl_z)
+            else:
+                hop_z(gq_z[a - 1])
         wait([gf_y])
         add_y(s.rcf, s.ryf, False)
         gf_z = to_z(s.ryf, s.rzf, False)
@@ -1856,8 +1884,10 @@
         add_z(s.ryl, s.rzl, s.fnl, False)
         gl_x = ln.push(s.fnl, s.o_last.at[r], xpeer)
         n1 = ln.near(s.fnl, s.o_last.at[r])
-        wait(gq_z)
-        add_z(s.rym, s.rzm, s.fnm, True, False)
+        for a in range(3):
+            wait_z(gq_z[a])
+            lead = slice(3 * a, 3 * a + 3)
+            add_z(s.rym.at[lead], s.rzm.at[:, lead], s.fnm.at[lead], True, a < 2)
         gq_x = ln.push(s.fnm, s.o_mid.at[:, :, pl.ds(half, 256)], xpeer)
         n2 = ln.near(s.fnm, s.o_mid.at[:, :, pl.ds(half, 256)])
         wait_z(gf_z)
@@ -1941,27 +1971,35 @@
         cp.start()
         return cp
 
-    done = [move(s.o_depth, s.depth), move(s.o_logits, s.logits)]
-    wide = ["mess", "heads", "mid", "img", "last", "red", "first", "gates"]
-    loads = {n: move(getattr(s, "o_" + n), getattr(s, "i_" + n)) for n in wide}
+    wide = [("img", slice(lo, lo + n)) for lo, n in ((0, 64), (64, 48), (112, 48))]
+    wide += [(n, slice(i, i + 1)) for n in ("mess", "heads") for i in range(2)]
+    wide += [("mid", slice(0, 9)), ("red", slice(0, 128)), ("first", slice(0, 128)), ("last", slice(0, 2)), ("gates", slice(0, 2))]
+    loads = [move(getattr(s, "o_" + n).at[at], getattr(s, "i_" + n).at[at]) for n, at in wide]
     small = [move(getattr(s, "o_" + n), getattr(s, "i_" + n)) for n in ("gs1", "gs2", "gs3", "cls")]
-    for n in wide:
-        loads[n].wait()
+    done = []
+    narrow = [move(s.o_depth, s.i_depth), move(s.o_logits, s.i_logits)]
+    for (n, at), cp in zip(wide, loads):
+        cp.wait()
         src, dst = getattr(s, "i_" + n), getattr(s, "v_" + n)
         if n == "last":
             for i in range(8):
                 for h in range(2):
                     lane = 128 * (2 * i + h)
                     dst[:, lane : lane + 128] = src[h, :, 128 * i : 128 * i + 128].astype(F32)
-        elif n == "img":
-            for i in range(0, 160, 32):
-                dst[i : i + 32, :] = src[i : i + 32, :].astype(F32)
+            done.append(move(dst, s.last))
+            continue
+        if n in ("mess", "heads"):
+            for t in range(9):
+                dst[at.start, t] = src[at.start, t].astype(F32)
         elif len(src.shape) > 2:
-            for i in range(src.shape[0]):
-                dst[i] = src[i].astype(F32)
+            for t in range(at.start, at.stop):
+                dst[t] = src[t].astype(F32)
         else:
-            dst[...] = src[...].astype(F32)
-        done.append(move(dst, getattr(s, n)))
+            dst[at] = src[at].astype(F32)
+        done.append(move(dst.at[at], getattr(s, n).at[at]))
+    for cp in narrow:
+        cp.wait()
+    done += [move(s.i_depth, s.depth), move(s.i_logits, s.logits)]
     for cp in small:
         cp.wait()
     quarter, spot = lax.div(b, np.int32(4)), lax.rem(b, np.int32(4))
@@ -1991,15 +2029,14 @@
         images, crop_height, crop_width, w_first, gain_first, shift_first, w_middle, gain_middle, shift_middle,
         w_last, gain_last, shift_last, w_reduce, w_heads, w_message, w_gates, w_classes, depth_cot, class_cot,
     ) = args
-    narrow = jnp.concatenate([gain_first, shift_first, gain_middle, shift_middle])
-    gains = jnp.stack([narrow, gain_last, shift_last]).astype(F32)
     ins = (
         crop_height, crop_width, images.reshape(160, 2048), w_first, w_middle, w_last, w_reduce, w_gates, w_classes,
-        w_heads, w_message, gains, depth_cot.reshape(160, 512), class_cot.transpose(0, 1, 3, 2).reshape(2, 40, 80),
+        w_heads, w_message, *(v.reshape(1, -1) for v in (gain_first, shift_first, gain_middle, shift_middle, gain_last, shift_last)), depth_cot.reshape(160, 512), class_cot.transpose(0, 1, 3, 2).reshape(2, 40, 80),
     )
     names = list(INS) + list(OUTS) + list(SHAPES) + ["send_sems", "recv_sems", "near_sems"]
     smem, hbm, vmem = (pl.BlockSpec(memory_space=m) for m in (pltpu.SMEM, pltpu.HBM, pltpu.VMEM))
-    spec = {"crop_h": smem, "crop_w": smem, "gains": vmem}
+    spec = {"crop_h": smem, "crop_w": smem}
+    spec.update({n: vmem for n in INS if n[:4] in ("gain", "shif")})
     outs = pl.pallas_call(
         functools.partial(body, names),
         out_shape=[jax.ShapeDtypeStruct(*v) for v in OUTS.values()],
@@ -2012,14 +2049,14 @@
     )(*ins)
     o = dict(zip(OUTS, outs))
     taken = [n for n in OUTS if n.startswith("o_")]
-    staged = {"i_" + n[2:]: OUTS[n] for n in taken if n not in ("o_depth", "o_logits")}
+    staged = {"i_" + n[2:]: OUTS[n] for n in taken}
     staged.update({"v_" + n: v for n, v in FINAL.items() if n not in ("depth", "logits")})
     final = pl.pallas_call(
         functools.partial(widen_out, taken + list(FINAL) + list(staged) + ["sems"]),
         out_shape=[jax.ShapeDtypeStruct(*v) for v in FINAL.values()],
         in_specs=[hbm] * len(taken),
         out_specs=[hbm] * len(FINAL),
-        scratch_shapes=[pltpu.VMEM(*v) for v in staged.values()] + [pltpu.SemaphoreType.DMA((40,))],
+        scratch_shapes=[pltpu.VMEM(*v) for v in staged.values()] + [pltpu.SemaphoreType.DMA((41,))],
         compiler_params=pltpu.CompilerParams(vmem_limit_bytes=64 * 2**20),
         name="widen_out",
     )(*[o[n] for n in taken])

time: 271 us -> 260 us (0.959)
  Pallas kernels: 267 us -> 259 us
    pallas_call x1, Pallas kernels: 260 us -> 255 us  [fast(): pl.pallas_call(functools.partial(body, names), out_shape=[jax.ShapeDtypeS...]
    pallas_call x1, Pallas kernels: 7.11 us -> 3.74 us  [fast(): pl.pallas_call(functools.partial(widen_out, taken + list(FINAL) + list(st...]
where the time goes in v5:
time: 260 us
  Pallas kernels  259 us (100%)
    pallas_call x1, Pallas kernels, fast(): pl.pallas_call(functools.partial(body, names), out_shape=[jax.ShapeDtypeS...  255 us

profile of v5, /device:TPU:0, one launch (start us, length us, event | category | flops | bytes accessed | tf_op | source)
XLA Modules:
  0.0 259.8 jit_solution(3431036099820321908)
XLA Ops:
  0.7 255.2 %residual_distill.1 = (bf16[160,512]{1,0:T(8,128)(2,1)}, bf16[2,40,80]{2,1,0:T(8,128)(2,1)}, bf16[160,2048]{1,0:T(8,128)(2,1)}, bf16[128,512]{1,0:T(8,128)(2,1)}...) custom-call(s32[16]{0:T(128)} %refs_0_.1, ...), custom_call_target="tpu_custom_call" | custom-call | tf_op jit(solution)/shard_map/residual_distill/pallas_call | solution.py:2040
  255.9 3.7 %widen_out.1 = (bf16[160,512]{1,0:T(8,128)(2,1)}, bf16[2,40,80]{2,1,0:T(8,128)(2,1)}, f32[160,2048]{1,0:T(8,128)}, f32[128,512]{1,0:T(8,128)}, f32[1,32]{1,0:T(1...) custom-call(bf16[160,512]{1,0:T(8,128)(2,1)} %get-tuple-element.48.r, ...), custom_call_target="tpu_custom_call" | custom-call | tf_op jit(solution)/shard_map/widen_out/pallas_call | solution.py:2054

commit v6 on v5

--- a/solution.py
+++ b/solution.py
@@ -16,7 +16,7 @@
 ROOT = 0.7978845608028654
 CUBE = 0.044715
 SENDS = 121
-RECVS = 196
+RECVS = 200
 NEAR = 21
 
 
@@ -679,6 +679,7 @@
     ryr=((4, 128, 512), BF16),
     hpr=((128, 512), BF16),
     hpl=((32, 1024), BF16),
+    hpf=((128, 256), BF16),
     hpm=((9, 32, 256), BF16),
     ryl=((4, 32, 1024), BF16),
     rym=((9, 4, 32, 256), BF16),
@@ -1090,7 +1091,6 @@
     put_stats(0, first_sum, first_sq, 256, 0)
     plane_one = plane_start(0)
     line_sides(go_wm, at_wm)
-    cores_wm = line_last(go_wm, at_wm, col_wm)
     plane_end(0, plane_one)
     line_y(go_wl, at_wl(z), at_wl, lambda: s.wl.at[:, 0, 0])
     pl.when(odd)(red_local.wait)
@@ -1101,10 +1101,12 @@
         line_relay(go_wl, at_wl)
         line_sides(go_wl, at_wl)
         late_wr.append(line_start(s.reduce, at_wr, lambda: s.wr.at[0], odd))
-        heads.append(task_push(s.heads.at[y], s.wh, 0, 7, False))
+        heads.append(task_push(s.heads.at[y], s.wh, 0, 6, False))
+        late_wr.append(line_last(go_wm, at_wm, col_wm))
 
     norm_terms(0, s.bnp1, 256, bulk_one)
     go_wr = late_wr[0]
+    cores_wm = late_wr[1]
 
     def act_from(prebuf, bnp, dst):
         def step(base):
@@ -1137,7 +1139,7 @@
     def bulk_two():
         line_relay(go_wr, at_wr, odd)
         relayed_h.append(task_relay(heads[0], s.wh))
-        heads.append(task_push(s.heads.at[y], s.wh, 7, 9, False))
+        heads.append(task_push(s.heads.at[y], s.wh, 6, 9, False))
         mess.append([mess_push(0, False)])
 
     norm_terms(1, s.bnp2, 256, bulk_two)
@@ -1809,7 +1811,7 @@
                 s.rym[t] = (s.rym[t].astype(F32) + s.rcm[t, :, y].astype(F32)).astype(BF16)
             lead = slice(3 * a, 3 * a + 3)
             rz = SimpleNamespace(at=[s.rzm.at[q, lead] for q in range(3)])
-            gq_z.append(to_z(s.rym.at[lead], rz, True, None, s.hpm.at[lead] if a < 2 else None))
+            gq_z.append(to_z(s.rym.at[lead], rz, True, None, s.hpm.at[lead]))
             if a == 0:
                 hop_z(gr_z)
                 hop_z(gl_z)
@@ -1817,8 +1819,9 @@
                 hop_z(gq_z[a - 1])
         wait([gf_y])
         add_y(s.rcf, s.ryf, False)
-        gf_z = to_z(s.ryf, s.rzf, False)
-
+        gf_z = to_z(s.ryf, s.rzf, False, None, s.hpf)
+
+        hs, hn = task_out(gh_z, s.rh, s.gh, s.psh, s.o_heads)
         wait([wfo_x])
         wfo_n = ln.near(s.wfo, s.wfov)
         wait([dp_x, ds_x])
@@ -1847,8 +1850,9 @@
 
             rows_loop(160, 32, img_step)
         img_n = ln.near(s.oimg, s.o_img)
-
-        hs, hn = task_out(gh_z, s.rh, s.gh, s.psh, s.o_heads)
+        hop_z(gq_z[2])
+
+        hop_z(gf_z)
 
         @pl.when(special)
         def _():
@@ -1887,11 +1891,11 @@
         for a in range(3):
             wait_z(gq_z[a])
             lead = slice(3 * a, 3 * a + 3)
-            add_z(s.rym.at[lead], s.rzm.at[:, lead], s.fnm.at[lead], True, a < 2)
+            add_z(s.rym.at[lead], s.rzm.at[:, lead], s.fnm.at[lead], True)
         gq_x = ln.push(s.fnm, s.o_mid.at[:, :, pl.ds(half, 256)], xpeer)
         n2 = ln.near(s.fnm, s.o_mid.at[:, :, pl.ds(half, 256)])
         wait_z(gf_z)
-        add_z(s.ryf, s.rzf, s.fnf, False, False)
+        add_z(s.ryf, s.rzf, s.fnf, False)
         gf_x = ln.push(s.fnf, s.o_first.at[:, pl.ds(half, 256)], xpeer)
         n3 = ln.near(s.fnf, s.o_first.at[:, pl.ds(half, 256)])
         wait([cls_x])

time: 260 us -> 256 us (0.985)
  Pallas kernels: 259 us -> 255 us
    pallas_call x1, Pallas kernels: 255 us -> 251 us  [fast(): pl.pallas_call(functools.partial(body, names), out_shape=[jax.ShapeDtypeS...]
where the time goes in v6:
time: 256 us
  Pallas kernels  255 us (100%)
    pallas_call x1, Pallas kernels, fast(): pl.pallas_call(functools.partial(body, names), out_shape=[jax.ShapeDtypeS...  251 us

profile of v6, /device:TPU:0, one launch (start us, length us, event | category | flops | bytes accessed | tf_op | source)
XLA Modules:
  0.0 255.6 jit_solution(11186932861339296366)
XLA Ops:
  0.7 251.1 %residual_distill.1 = (bf16[160,512]{1,0:T(8,128)(2,1)}, bf16[2,40,80]{2,1,0:T(8,128)(2,1)}, bf16[160,2048]{1,0:T(8,128)(2,1)}, bf16[128,512]{1,0:T(8,128)(2,1)}...) custom-call(s32[16]{0:T(128)} %refs_0_.1, ...), custom_call_target="tpu_custom_call" | custom-call | tf_op jit(solution)/shard_map/residual_distill/pallas_call | solution.py:2044
  251.8 3.7 %widen_out.1 = (bf16[160,512]{1,0:T(8,128)(2,1)}, bf16[2,40,80]{2,1,0:T(8,128)(2,1)}, f32[160,2048]{1,0:T(8,128)}, f32[128,512]{1,0:T(8,128)}, f32[1,32]{1,0:T(1...) custom-call(bf16[160,512]{1,0:T(8,128)(2,1)} %get-tuple-element.48.r, ...), custom_call_target="tpu_custom_call" | custom-call | tf_op jit(solution)/shard_map/widen_out/pallas_call | solution.py:2058

commit v7 on v6

--- a/solution.py
+++ b/solution.py
@@ -15,8 +15,8 @@
 BF16 = jnp.bfloat16
 ROOT = 0.7978845608028654
 CUBE = 0.044715
-SENDS = 121
-RECVS = 200
+SENDS = 122
+RECVS = 201
 NEAR = 21
 
 
@@ -913,7 +913,7 @@
     pl.semaphore_wait(barrier, len(friends))
 
     src_wf, src_wm = s.first.at[:, pl.ds(half, 256)], s.middle.at[:, :, pl.ds(half, 256)]
-    go_wf = line_start(src_wf, at_wf, lambda: s.wf.at[0, 0], relay=False)
+    go_wf = line_start(src_wf, at_wf, lambda: s.wf.at[0, 0])
     line_y(go_wf, src_wf, at_wf, lambda: s.wf.at[:, 0, 0])
     img_x = ln.push(s.images, s.xall.at[pl.ds(my_rows, 160)], xpeer)
     go_wm = line_start(src_wm, at_wm, lambda: s.wm.at[:, 0, 0])

time: 256 us -> 255 us (level)
  no operation moved by 1% of the time
where the time goes in v7:
time: 255 us; the launch traced here: 254 us
  Pallas kernels  254 us (100%)
    pallas_call x1, Pallas kernels, fast(): pl.pallas_call(functools.partial(body, names), out_shape=[jax.ShapeDtypeS...  250 us

profile of v7, /device:TPU:0, one launch (start us, length us, event | category | flops | bytes accessed | tf_op | source)
XLA Modules:
  0.0 254.5 jit_solution(4018847343753903632)
XLA Ops:
  0.7 249.9 %residual_distill.1 = (bf16[160,512]{1,0:T(8,128)(2,1)}, bf16[2,40,80]{2,1,0:T(8,128)(2,1)}, bf16[160,2048]{1,0:T(8,128)(2,1)}, bf16[128,512]{1,0:T(8,128)(2,1)}...) custom-call(s32[16]{0:T(128)} %refs_0_.1, ...), custom_call_target="tpu_custom_call" | custom-call | tf_op jit(solution)/shard_map/residual_distill/pallas_call | solution.py:2044
  250.6 3.7 %widen_out.1 = (bf16[160,512]{1,0:T(8,128)(2,1)}, bf16[2,40,80]{2,1,0:T(8,128)(2,1)}, f32[160,2048]{1,0:T(8,128)}, f32[128,512]{1,0:T(8,128)}, f32[1,32]{1,0:T(1...) custom-call(bf16[160,512]{1,0:T(8,128)(2,1)} %get-tuple-element.48.r, ...), custom_call_target="tpu_custom_call" | custom-call | tf_op jit(solution)/shard_map/widen_out/pallas_call | solution.py:2058
